TPU v7x, 128 devices: a whole 4x4x4 slice. The times are simulated.
128 devices in a mesh: section: 4 (over y), seq: 32 (over x, z, core).
Axes of the slice: x: 4, y: 4, z: 4, core: 2. Of those that a mesh axis runs over, the one named last changes fastest.
Arguments:
- tokens: bfloat16 [1, 4096, 2560], P(None, 'seq'), may hold values from -7 to 7
- w_qkv: bfloat16 [4, 2560, 3840], P('section', 'seq')
- w_out: bfloat16 [4, 1280, 2560], P('section', 'seq'), may hold values from -0.15625 to 0.15625
- offsets: int32 [4, 10], replicated, may hold values from 0 to 7, as said below
Outputs:
- layer_outputs: bfloat16 [4, 1, 4096, 2560], P('section', None, 'seq')
Inputs may be any that keep to these rules, and one draw needn't show every extreme that they name: offsets[b, h] lies below 2^b, and for each b every value below 2^b is taken by some head.
All inputs are finite; a program needn't handle non-finite values.
Results may differ from a plain program's by a relative error of at most 0.035.
Values may be sent and summed in bfloat16 or wider, within the bound.
No kernel may reach another device: no remote copies, remote signals or barrier semaphores. Data moves between devices by JAX's collectives and lax.ppermute only.
A program may use at most 128 MiB of HBM per device.

v0:
```python
import functools
import math

import jax
import jax.numpy as jnp
from jax import lax
from jax.experimental import pallas as pl
from jax.experimental.pallas import tpu as pltpu
from jax.sharding import PartitionSpec as P

NEG_FILL = -1e30
HD = 128
CHIP_ROWS = 256
GROUP_CHIPS = 4
BF16 = jnp.bfloat16
F32 = jnp.float32
VMEM_LIMIT = 32 * 1024 * 1024


def dot(a, b):
    return lax.dot_general(a, b, (((1,), (0,)), ((), ())), preferred_element_type=F32)


def dot_t(a, b):
    return lax.dot_general(a, b, (((1,), (1,)), ((), ())), preferred_element_type=F32)


def offset_of(scalars, branch, head_at, heads):
    return scalars[2 + branch * 2 * heads + scalars[0] * heads + head_at]


def kv_kernel(heads, scalars, x_own, x_other, w, kv_out, send_out, acc):
    half = pl.program_id(1)

    @pl.when(half == 0)
    def _():
        acc[...] = dot(x_own[...], w[...])

    @pl.when(half == 1)
    def _():
        rows = (acc[...] + dot(x_other[...], w[...])).astype(BF16)
        kv_out[...] = rows
        row = lax.broadcasted_iota(jnp.int32, (96, CHIP_ROWS), 0)
        col = lax.broadcasted_iota(jnp.int32, (96, CHIP_ROWS), 1)
        for i in range(heads):
            off2 = offset_of(scalars, 2, i, heads)
            off3 = offset_of(scalars, 3, i, heads)
            source = jnp.where(row < 64, 4 * row + off2, 8 * (row - 64) + off3)
            pick = jnp.where(col == source, 1.0, 0.0).astype(BF16)
            cols = slice(i * HD, (i + 1) * HD)
            send_out[:, cols] = dot(pick, rows[:, cols]).astype(BF16)


def local_kernel(heads, scalars, x_own, x_other, w, kv, q_out, acc_out, stat_out, acc):
    half = pl.program_id(0)

    @pl.when(half == 0)
    def _():
        acc[...] = dot(x_own[...], w[...])

    @pl.when(half == 1)
    def _():
        query = (acc[...] + dot(x_other[...], w[...])).astype(BF16)
        q_out[...] = query
        scaling = 1.0 / math.sqrt(HD)
        shape = (CHIP_ROWS, CHIP_ROWS)
        causal = lax.broadcasted_iota(jnp.int32, shape, 1) <= lax.broadcasted_iota(
            jnp.int32, shape, 0
        )
        row = lax.broadcasted_iota(jnp.int32, (CHIP_ROWS, HD), 0)
        lane = lax.broadcasted_iota(jnp.int32, (CHIP_ROWS, HD), 1)
        first = ((lane == 0) & (row < 128)) | ((lane == 1) & (row >= 128))
        period = jnp.where(lane == 2, 1, jnp.where(lane == 3, 3, 7))
        in_branch = (lane >= 2) & (lane <= 4)
        stats = jnp.zeros((CHIP_ROWS, HD), F32)
        width = heads * HD
        for i in range(heads):
            cols = slice(i * HD, (i + 1) * HD)
            offset = jnp.where(
                lane == 2,
                offset_of(scalars, 1, i, heads),
                jnp.where(
                    lane == 3, offset_of(scalars, 2, i, heads), offset_of(scalars, 3, i, heads)
                ),
            )
            member = first | (in_branch & ((row & period) == offset))
            member = jnp.where(member, 1.0, 0.0).astype(BF16)
            times = jnp.where(causal, dot_t(member, member), 0.0)
            scores = dot_t(query[:, cols], kv[:, cols]) * scaling
            scores = jnp.where(times > 0.0, scores, NEG_FILL)
            peak = jnp.max(scores, axis=1, keepdims=True)
            expos = times * jnp.exp(scores - peak)
            total = jnp.sum(expos, axis=1, keepdims=True)
            acc_out[:, cols] = dot(
                expos.astype(BF16), kv[:, width + i * HD : width + (i + 1) * HD]
            )
            stats = jnp.where(lane == i, peak, jnp.where(lane == heads + i, total, stats))
        stat_out[...] = stats


def remote_kernel(heads, scalars, query, acc, stats, near, mid, far, out):
    scaling = 1.0 / math.sqrt(HD)
    chip = scalars[1]
    width = heads * HD
    keys = 160
    row = lax.broadcasted_iota(jnp.int32, (CHIP_ROWS, keys), 0)
    col = lax.broadcasted_iota(jnp.int32, (CHIP_ROWS, keys), 1)
    second = (col < 64) & ((chip & 1) == 1)
    third = (col >= 64) & (chip >= 1 + (col - 64) // 32)
    stat = stats[...]
    for i in range(heads):
        cols = slice(i * HD, (i + 1) * HD)
        vals = slice(width + i * HD, width + (i + 1) * HD)
        off2 = offset_of(scalars, 2, i, heads)
        off3 = offset_of(scalars, 3, i, heads)
        allowed = (second & ((row & 3) == off2)) | (third & ((row & 7) == off3))
        key_rows = jnp.concatenate([near[:, cols], mid[:, cols], far[:, cols]], axis=0)
        value_rows = jnp.concatenate([near[:, vals], mid[:, vals], far[:, vals]], axis=0)
        scores = dot_t(query[:, cols], key_rows) * scaling
        scores = jnp.where(allowed, scores, NEG_FILL)
        peak = stat[:, i : i + 1]
        total = stat[:, heads + i : heads + i + 1]
        new_peak = jnp.maximum(peak, jnp.max(scores, axis=1, keepdims=True))
        expos = jnp.exp(scores - new_peak)
        shrink = jnp.exp(peak - new_peak)
        total = total * shrink + jnp.sum(expos, axis=1, keepdims=True)
        mixed = acc[:, cols] * shrink + dot(expos.astype(BF16), value_rows)
        out[:, cols] = (mixed / total).astype(BF16)


def back_kernel(scalars, x_own, att_own, att_other, w, out, acc):
    half = pl.program_id(0)

    @pl.when(half == 0)
    def _():
        acc[...] = x_own[...].astype(F32) + dot(att_own[...], w[...])

    @pl.when(half == 1)
    def _():
        out[...] = (acc[...] + dot(att_other[...], w[...])).astype(BF16)


def call(body, grid, in_specs, out_specs, out_shape, scratch, flops, moved):
    return pl.pallas_call(
        body,
        grid_spec=pltpu.PrefetchScalarGridSpec(
            num_scalar_prefetch=1,
            grid=grid,
            in_specs=in_specs,
            out_specs=out_specs,
            scratch_shapes=scratch,
        ),
        out_shape=out_shape,
        compiler_params=pltpu.CompilerParams(vmem_limit_bytes=VMEM_LIMIT),
        cost_estimate=pl.CostEstimate(flops=flops, bytes_accessed=moved, transcendentals=0),
    )


def whole(shape):
    return pl.BlockSpec(shape, lambda *_: (0,) * len(shape))


def project_kv(scalars, x_own, x_other, w):
    rows, half = x_own.shape
    width = w.shape[1] // 3
    heads = width // HD
    return call(
        functools.partial(kv_kernel, heads),
        (2, 2),
        [
            whole((rows, half)),
            whole((rows, half)),
            pl.BlockSpec((half, width), lambda n, k, s: ((k + s[0]) % 2, n)),
        ],
        [
            pl.BlockSpec((rows, width), lambda n, k, s: (0, n)),
            pl.BlockSpec((96, width), lambda n, k, s: (0, n)),
        ],
        [
            jax.ShapeDtypeStruct((rows, 2 * width), BF16),
            jax.ShapeDtypeStruct((96, 2 * width), BF16),
        ],
        [pltpu.VMEM((rows, width), F32)],
        8 * rows * half * width,
        8 * half * width,
    )(scalars, x_own, x_other, w)


def attend_local(scalars, x_own, x_other, w, kv):
    rows, half = x_own.shape
    width = w.shape[1] // 3
    heads = width // HD
    return call(
        functools.partial(local_kernel, heads),
        (2,),
        [
            whole((rows, half)),
            whole((rows, half)),
            pl.BlockSpec((half, width), lambda k, s: ((k + s[0]) % 2, 2)),
            whole((rows, 2 * width)),
        ],
        [whole((rows, width)), whole((rows, width)), whole((rows, HD))],
        [
            jax.ShapeDtypeStruct((rows, width), BF16),
            jax.ShapeDtypeStruct((rows, width), F32),
            jax.ShapeDtypeStruct((rows, HD), F32),
        ],
        [pltpu.VMEM((rows, width), F32)],
        4 * rows * half * width,
        4 * half * width,
    )(scalars, x_own, x_other, w, kv)


def attend_remote(scalars, query, acc, stats, near, mid, far):
    rows, width = query.shape
    heads = width // HD
    return call(
        functools.partial(remote_kernel, heads),
        (1,),
        [
            whole(query.shape),
            whole(acc.shape),
            whole(stats.shape),
            whole(near.shape),
            whole(mid.shape),
            whole(far.shape),
        ],
        whole((rows, width)),
        jax.ShapeDtypeStruct((rows, width), BF16),
        [],
        4 * rows * 160 * width,
        rows * width * 8,
    )(scalars, query, acc, stats, near, mid, far)


def project_back(scalars, x_own, att_own, att_other, w):
    rows, half = x_own.shape
    width = att_own.shape[1]
    return call(
        back_kernel,
        (2,),
        [
            whole((rows, half)),
            whole((rows, width)),
            whole((rows, width)),
            pl.BlockSpec((width, half), lambda k, s: ((k + s[0]) % 2, 0)),
        ],
        whole((rows, half)),
        jax.ShapeDtypeStruct((rows, half), BF16),
        [pltpu.VMEM((rows, half), F32)],
        4 * rows * half * width,
        4 * half * width,
    )(scalars, x_own, att_own, att_other, w)


def swap(value):
    count = lax.axis_size("seq")
    return lax.ppermute(value, "seq", [(i, i ^ 1) for i in range(count)])


def to_later_chip(value, steps):
    count = lax.axis_size("seq")
    pairs = []
    for source in range(count):
        if (source // 2) % GROUP_CHIPS + steps < GROUP_CHIPS:
            pairs.append((source, source + 2 * steps))
    return lax.ppermute(value, "seq", pairs)


def in_order(core, own, other, axis):
    return jnp.where(
        core == 0,
        jnp.concatenate([own, other], axis=axis),
        jnp.concatenate([other, own], axis=axis),
    )


def gather_chips(block):
    count = lax.axis_size("seq")
    groups = [list(range(core, count, 2)) for core in range(2)]
    return lax.all_gather(block, "seq", axis=0, tiled=True, axis_index_groups=groups)


def local(tokens, w_qkv, w_out, offsets):
    section = lax.axis_index("section")
    section_count = lax.axis_size("section")
    seq = lax.axis_index("seq")
    core = seq % 2
    scalars = jnp.concatenate(
        [
            jnp.stack([core, (seq // 2) % GROUP_CHIPS]).astype(jnp.int32),
            offsets.reshape(-1).astype(jnp.int32),
        ]
    )
    with jax.named_scope("weights"):
        rows = w_qkv.shape[1]
        width = w_qkv.shape[2] // 6
        parts = w_qkv[0].reshape(rows, 3, 2, width)
        halves = [
            jnp.concatenate([parts[:, 1, h], parts[:, 2, h], parts[:, 0, h]], axis=1)
            for h in range(2)
        ]
        own = jnp.where(core == 0, halves[0], halves[1])
        other = swap(jnp.where(core == 0, halves[1], halves[0]))
        w_in = gather_chips(in_order(core, own, other, 0))
        cut = w_out.shape[2] // 2
        left, right = w_out[0][:, :cut], w_out[0][:, cut:]
        own = jnp.where(core == 0, left, right)
        other = swap(jnp.where(core == 0, right, left))
        w_back = gather_chips(in_order(core, own, other, 0))
    with jax.named_scope("tokens"):
        both = in_order(core, tokens[0], swap(tokens[0]), 0)
        left, right = both[:, :cut], both[:, cut:]
        x_own = jnp.where(core == 0, left, right)
        x_other = jnp.where(core == 0, right, left)
    result = jnp.zeros_like(x_own)
    for tick in range(section_count):
        kv, send = project_kv(scalars, x_own, x_other, w_in)
        near = to_later_chip(send, 1)
        mid = to_later_chip(send[64:], 2)
        far = to_later_chip(send[64:], 3)
        query, acc, stats = attend_local(scalars, x_own, x_other, w_in, kv)
        att = attend_remote(scalars, query, acc, stats, near, mid, far)
        produced = project_back(scalars, x_own, att, swap(att), w_back)
        result = jnp.where(section == tick, produced, result)
        if tick + 1 < section_count:
            x_own = lax.ppermute(produced, "section", [(tick, tick + 1)])
            x_other = swap(x_own)
    with jax.named_scope("result"):
        top, bottom = result[:128], result[128:]
        mine = jnp.where(core == 0, top, bottom)
        theirs = swap(jnp.where(core == 0, bottom, top))
        return in_order(core, mine, theirs, 1)[None, None]


def solution(mesh):
    return jax.shard_map(
        local,
        mesh=mesh,
        in_specs=(P(None, "seq", None), P("section", "seq", None), P("section", "seq", None), P()),
        out_specs=P("section", None, "seq", None),
        check_vma=False,
    )
```

profile of v0, /device:TPU:25, one launch (start us, length us, event | category | flops | bytes accessed | tf_op | source)
XLA Modules:
  0.0 294.1 jit_solution(14630164932257254443)
XLA Ops:
  17.2 74.7 %all-gather.3.cloned.1.call-done.w = bf16[2560,1920]{1,0:T(8,128)(2,1)} async-done(((bf16[160,1920]{1,0:T(8,128)(2,1)}), bf16[2560,1920]{1,0:T(8,128)(2,1)}) %all-gather.3.cloned.1.call-update) | async-done | bytes 9830416 | tf_op jit(solution)/shard_map/weights/all_gather | solution.py:281
  92.0 3.8 %copy-done = bf16[2560,1920]{1,0:T(8,128)(2,1)S(1)} copy-done((bf16[2560,1920]{1,0:T(8,128)(2,1)S(1)}, bf16[2560,1920]{1,0:T(8,128)(2,1)}, u32[]{:S(2)}) %copy-start) | copy-done | bytes 9830424
  95.7 4.5 %shard_map.46 = (bf16[256,1280]{1,0:T(8,128)(2,1)S(1)}, bf16[96,1280]{1,0:T(8,128)(2,1)S(1)}) custom-call(s32[42]{0:T(128)S(1)} %pad_add_fusion.scalars, bf16[256,1280]{1,0:T(8,128)(2,1)S(1)} %get-tuple-element.46.x_own, bf16[256,1280]{1,0:T(8,128)(2,1)S(1)} %get-tuple-element.45.x_other, bf16[2560,1920]{1,0:T(8,128)(2,1)S(1)} %copy-done), custom_call_target="tpu_custom_call" | custom-call | flops 1677721600 | bytes 6553600 | tf_op jit(solution)/shard_map/pallas_call | solution.py:167
  100.2 2.9 collective-permute-start.2
  103.2 4.5 %collective-permute-start.3 = (bf16[32,1280]{1,0:T(8,128)(2,1)S(1)}, bf16[32,1280]{1,0:T(8,128)(2,1)S(1)}, u32[]{:S(2)}, u32[]{:S(2)}) collective-permute-start(bf16[32,1280]{1,0:T(8,128)(2,1)S(1)} %slice.60), channel_id=1, source_target_pairs={{0,4},{1,5},{2,6},{3,7},{8,12},{9,13},{10,14},{11,15},{16,20},{17,... | collective-permute-start | bytes 245768 | tf_op jit(solution)/shard_map/ppermute | solution.py:267
  109.0 3.8 %shard_map.47 = (bf16[256,640]{1,0:T(8,128)(2,1)S(1)}, f32[256,640]{1,0:T(8,128)S(1)}, f32[256,128]{1,0:T(8,128)S(1)}) custom-call(s32[42]{0:T(128)S(1)} %pad_add_fusion.scalars, bf16[256,1280]{1,0:T(8,128)(2,1)S(1)} %get-tuple-element.46.x_own, bf16[256,1280]{1,0:T(8,128)(2,1)S(1)} %get-tuple-element.45.x_other, bf16[2560,1920]{1,0:T(8,128)(2,1)S(1)} %copy-done, ...), custom_call_target="tpu_custom_call" | custom-call | flops 838860800 | bytes 3276800 | tf_op jit(solution)/shard_map/pallas_call | solution.py:193
  112.8 3.4 %shard_map.48.att_own = bf16[256,640]{1,0:T(8,128)(2,1)S(1)} custom-call(s32[42]{0:T(128)S(1)} %pad_add_fusion.scalars, bf16[256,640]{1,0:T(8,128)(2,1)S(1)} %get-tuple-element.26.query, f32[256,640]{1,0:T(8,128)S(1)} %get-tuple-element.27.acc, f32[256,128]{1,0:T(8,128)S(1)} %get-tuple-element.28.stats, bf16[96,1280]{1,0:T(8,128)(2,1)S(1)} %collective-permute-done.2.near, ...), custom_call_target="tpu_custom_call" | custom-call | flops 104857600 | bytes 1310720 | tf_op jit(solution)/shard_map/pallas_call | solution.py:217
  117.6 25.0 %all-gather.5.cloned.1.call-done.w = bf16[1280,1280]{1,0:T(8,128)(2,1)} async-done(((bf16[80,1280]{1,0:T(8,128)(2,1)}), bf16[1280,1280]{1,0:T(8,128)(2,1)}) %all-gather.5.cloned.1.call-update) | async-done | bytes 3276816 | tf_op jit(solution)/shard_map/weights/all_gather | solution.py:281
  150.2 3.8 %copy-done.1 = bf16[2560,1920]{1,0:T(8,128)(2,1)S(1)} copy-done((bf16[2560,1920]{1,0:T(8,128)(2,1)S(1)}, bf16[2560,1920]{1,0:T(8,128)(2,1)}, u32[]{:S(2)}) %copy-start.1) | copy-done | bytes 9830424
  154.0 4.5 %shard_map.50 = (bf16[256,1280]{1,0:T(8,128)(2,1)S(1)}, bf16[96,1280]{1,0:T(8,128)(2,1)S(1)}) custom-call(s32[42]{0:T(128)S(1)} %pad_add_fusion.scalars, bf16[256,1280]{1,0:T(8,128)(2,1)S(1)} %collective-permute-done.7.x_own, bf16[256,1280]{1,0:T(8,128)(2,1)S(1)} %collective-permute-done.8.x_other, bf16[2560,1920]{1,0:T(8,128)(2,1)S(1)} %copy-done.1), custom_call_target="tpu_custom_call" | custom-call | flops 1677721600 | bytes 6553600 | tf_op jit(solution)/shard_map/pallas_call | solution.py:167
  158.5 2.2 collective-permute-start.9
  160.8 4.3 %collective-permute-start.10 = (bf16[32,1280]{1,0:T(8,128)(2,1)S(1)}, bf16[32,1280]{1,0:T(8,128)(2,1)S(1)}, u32[]{:S(2)}, u32[]{:S(2)}) collective-permute-start(bf16[32,1280]{1,0:T(8,128)(2,1)S(1)} %slice.63), channel_id=1, source_target_pairs={{0,4},{1,5},{2,6},{3,7},{8,12},{9,13},{10,14},{11,15},{16,20},{17,... | collective-permute-start | bytes 245768 | tf_op jit(solution)/shard_map/ppermute | solution.py:267
  166.4 3.8 %shard_map.51 = (bf16[256,640]{1,0:T(8,128)(2,1)S(1)}, f32[256,640]{1,0:T(8,128)S(1)}, f32[256,128]{1,0:T(8,128)S(1)}) custom-call(s32[42]{0:T(128)S(1)} %pad_add_fusion.scalars, bf16[256,1280]{1,0:T(8,128)(2,1)S(1)} %collective-permute-done.7.x_own, bf16[256,1280]{1,0:T(8,128)(2,1)S(1)} %collective-permute-done.8.x_other, bf16[2560,1920]{1,0:T(8,128)(2,1)S(1)} %copy-done.1, ...), custom_call_target="tpu_custom_call" | custom-call | flops 838860800 | bytes 3276800 | tf_op jit(solution)/shard_map/pallas_call | solution.py:193
  170.2 3.4 %shard_map.52.att_own = bf16[256,640]{1,0:T(8,128)(2,1)S(1)} custom-call(s32[42]{0:T(128)S(1)} %pad_add_fusion.scalars, bf16[256,640]{1,0:T(8,128)(2,1)S(1)} %get-tuple-element.31.query, f32[256,640]{1,0:T(8,128)S(1)} %get-tuple-element.32.acc, f32[256,128]{1,0:T(8,128)S(1)} %get-tuple-element.33.stats, bf16[96,1280]{1,0:T(8,128)(2,1)S(1)} %collective-permute-done.9.near, ...), custom_call_target="tpu_custom_call" | custom-call | flops 104857600 | bytes 1310720 | tf_op jit(solution)/shard_map/pallas_call | solution.py:217
  180.9 4.5 %shard_map.54 = (bf16[256,1280]{1,0:T(8,128)(2,1)S(1)}, bf16[96,1280]{1,0:T(8,128)(2,1)S(1)}) custom-call(s32[42]{0:T(128)S(1)} %pad_add_fusion.scalars, bf16[256,1280]{1,0:T(8,128)(2,1)S(1)} %collective-permute-done.13.x_own, bf16[256,1280]{1,0:T(8,128)(2,1)S(1)} %collective-permute-done.14.x_other, bf16[2560,1920]{1,0:T(8,128)(2,1)S(1)} %bitcast.20), custom_call_target="tpu_custom_call" | custom-call | flops 1677721600 | bytes 6553600 | tf_op jit(solution)/shard_map/pallas_call | solution.py:167
  186.7 5.2 %collective-permute-start.16 = (bf16[32,1280]{1,0:T(8,128)(2,1)S(1)}, bf16[32,1280]{1,0:T(8,128)(2,1)S(1)}, u32[]{:S(2)}, u32[]{:S(2)}) collective-permute-start(bf16[32,1280]{1,0:T(8,128)(2,1)S(1)} %slice.64), channel_id=1, source_target_pairs={{0,4},{1,5},{2,6},{3,7},{8,12},{9,13},{10,14},{11,15},{16,20},{17,... | collective-permute-start | bytes 245768 | tf_op jit(solution)/shard_map/ppermute | solution.py:267
  193.4 3.8 %shard_map.55 = (bf16[256,640]{1,0:T(8,128)(2,1)S(1)}, f32[256,640]{1,0:T(8,128)S(1)}, f32[256,128]{1,0:T(8,128)S(1)}) custom-call(s32[42]{0:T(128)S(1)} %pad_add_fusion.scalars, bf16[256,1280]{1,0:T(8,128)(2,1)S(1)} %collective-permute-done.13.x_own, bf16[256,1280]{1,0:T(8,128)(2,1)S(1)} %collective-permute-done.14.x_other, ...), custom_call_target="tpu_custom_call" | custom-call | flops 838860800 | bytes 3276800 | tf_op jit(solution)/shard_map/pallas_call | solution.py:193
  197.3 3.4 %shard_map.56.att_own = bf16[256,640]{1,0:T(8,128)(2,1)S(1)} custom-call(s32[42]{0:T(128)S(1)} %pad_add_fusion.scalars, bf16[256,640]{1,0:T(8,128)(2,1)S(1)} %get-tuple-element.36.query, f32[256,640]{1,0:T(8,128)S(1)} %get-tuple-element.37.acc, f32[256,128]{1,0:T(8,128)S(1)} %get-tuple-element.38.stats, bf16[96,1280]{1,0:T(8,128)(2,1)S(1)} %collective-permute-done.15.near, ...), custom_call_target="tpu_custom_call" | custom-call | flops 104857600 | bytes 1310720 | tf_op jit(solution)/shard_map/pallas_call | solution.py:217
  206.3 48.3 %collective-permute-done.19.x_own = bf16[256,1280]{1,0:T(8,128)(2,1)S(1)} collective-permute-done((bf16[256,1280]{1,0:T(8,128)(2,1)S(1)}, bf16[256,1280]{1,0:T(8,128)(2,1)S(1)}, u32[]{:S(2)}, u32[]{:S(2)}) %collective-permute-start.19) | collective-permute-done | bytes 655392 | tf_op jit(solution)/shard_map/ppermute | solution.py:327
  257.2 4.5 %shard_map.58 = (bf16[256,1280]{1,0:T(8,128)(2,1)S(1)}, bf16[96,1280]{1,0:T(8,128)(2,1)S(1)}) custom-call(s32[42]{0:T(128)S(1)} %pad_add_fusion.scalars, bf16[256,1280]{1,0:T(8,128)(2,1)S(1)} %collective-permute-done.19.x_own, bf16[256,1280]{1,0:T(8,128)(2,1)S(1)} %collective-permute-done.20.x_other, bf16[2560,1920]{1,0:T(8,128)(2,1)S(1)} %bitcast.20), custom_call_target="tpu_custom_call" | custom-call | flops 1677721600 | bytes 6553600 | tf_op jit(solution)/shard_map/pallas_call | solution.py:167
  263.1 4.9 %collective-permute-start.22 = (bf16[32,1280]{1,0:T(8,128)(2,1)S(1)}, bf16[32,1280]{1,0:T(8,128)(2,1)S(1)}, u32[]{:S(2)}, u32[]{:S(2)}) collective-permute-start(bf16[32,1280]{1,0:T(8,128)(2,1)S(1)} %slice.65), channel_id=1, source_target_pairs={{0,4},{1,5},{2,6},{3,7},{8,12},{9,13},{10,14},{11,15},{16,20},{17,... | collective-permute-start | bytes 245768 | tf_op jit(solution)/shard_map/ppermute | solution.py:267
  269.6 3.8 %shard_map.59 = (bf16[256,640]{1,0:T(8,128)(2,1)S(1)}, f32[256,640]{1,0:T(8,128)S(1)}, f32[256,128]{1,0:T(8,128)S(1)}) custom-call(s32[42]{0:T(128)S(1)} %pad_add_fusion.scalars, bf16[256,1280]{1,0:T(8,128)(2,1)S(1)} %collective-permute-done.19.x_own, bf16[256,1280]{1,0:T(8,128)(2,1)S(1)} %collective-permute-done.20.x_other, ...), custom_call_target="tpu_custom_call" | custom-call | flops 838860800 | bytes 3276800 | tf_op jit(solution)/shard_map/pallas_call | solution.py:193
  273.5 4.2 %shard_map.60.att_own = bf16[256,640]{1,0:T(8,128)(2,1)} custom-call(s32[42]{0:T(128)S(1)} %pad_add_fusion.scalars, bf16[256,640]{1,0:T(8,128)(2,1)S(1)} %get-tuple-element.41.query, f32[256,640]{1,0:T(8,128)S(1)} %get-tuple-element.42.acc, f32[256,128]{1,0:T(8,128)S(1)} %get-tuple-element.43.stats, bf16[96,1280]{1,0:T(8,128)(2,1)S(1)} %collective-permute-done.21.near, ...), custom_call_target="tpu_custom_call" | custom-call | flops 104857600 | bytes 1310720 | tf_op jit(solution)/shard_map/pallas_call | solution.py:217
  281.3 3.1 %shard_map.61 = bf16[256,1280]{1,0:T(8,128)(2,1)S(1)} custom-call(s32[42]{0:T(128)S(1)} %pad_add_fusion.scalars, bf16[256,1280]{1,0:T(8,128)(2,1)S(1)} %copy-done.5, bf16[256,640]{1,0:T(8,128)(2,1)} %shard_map.60.att_own, bf16[256,640]{1,0:T(8,128)(2,1)} %collective-permute-done.24.att_other, bf16[1280,1280]{1,0:T(8,128)(2,1)S(1)} %copy-done.3), custom_call_target="tpu_custom_call" | custom-call | flops 838860800 | bytes 3276800 | tf_op jit(solution)/shard_map/pallas_call | solution.py:239
  (107 shorter events, 49.6 us)
Async XLA Ops:
  6.5 85.4 %all-gather.3.cloned.1.call-start = ((), (), s32[]{:S(2)}) async-start(), calls=%async_computation | async-start | bytes 10444800 | tf_op jit(solution)/shard_map/weights/all_gather | solution.py:281
  9.5 2.0 collective-permute-start.1
  12.4 130.1 %all-gather.5.cloned.1.call-start = ((), (), s32[]{:S(2)}) async-start(), calls=%async_computation.1 | async-start | bytes 3481600 | tf_op jit(solution)/shard_map/weights/all_gather | solution.py:281
  14.7 2.2 collective-permute-start
  100.2 12.6 %collective-permute-start.2 = (bf16[96,1280]{1,0:T(8,128)(2,1)S(1)}, bf16[96,1280]{1,0:T(8,128)(2,1)S(1)}, u32[]{:S(2)}, u32[]{:S(2)}) collective-permute-start(bf16[96,1280]{1,0:T(8,128)(2,1)S(1)} %get-tuple-element.29), channel_id=1, source_target_pairs={{0,2},{1,3},{2,4},{3,5},{4,6},{5,7},{8,10},{9,11},{10,12},{11,13},... | collective-permute-start | bytes 737288 | tf_op jit(solution)/shard_map/ppermute | solution.py:267
  103.2 9.6 %collective-permute-start.3 = (bf16[32,1280]{1,0:T(8,128)(2,1)S(1)}, bf16[32,1280]{1,0:T(8,128)(2,1)S(1)}, u32[]{:S(2)}, u32[]{:S(2)}) collective-permute-start(bf16[32,1280]{1,0:T(8,128)(2,1)S(1)} %slice.60), channel_id=1, source_target_pairs={{0,4},{1,5},{2,6},{3,7},{8,12},{9,13},{10,14},{11,15},{16,20},{17,... | collective-permute-start | bytes 245768 | tf_op jit(solution)/shard_map/ppermute | solution.py:267
  107.7 5.1 %collective-permute-start.4 = (bf16[32,1280]{1,0:T(8,128)(2,1)S(1)}, bf16[32,1280]{1,0:T(8,128)(2,1)S(1)}, u32[]{:S(2)}, u32[]{:S(2)}) collective-permute-start(bf16[32,1280]{1,0:T(8,128)(2,1)S(1)} %slice.60), channel_id=1, source_target_pairs={{0,6},{1,7},{8,14},{9,15},{16,22},{17,23},{24,30},{25,31},{32,38},... | collective-permute-start | bytes 245768 | tf_op jit(solution)/shard_map/ppermute | solution.py:267
  116.2 26.3 %collective-permute-start.5 = (bf16[256,640]{1,0:T(8,128)(2,1)S(1)}, bf16[256,640]{1,0:T(8,128)(2,1)S(1)}, u32[]{:S(2)}, u32[]{:S(2)}) collective-permute-start(bf16[256,640]{1,0:T(8,128)(2,1)S(1)} %shard_map.48.att_own), channel_id=1, source_target_pairs={{0,1},{1,0},{2,3},{3,2},{4,5},{5,4},{6,7},{7,6},{8,9},{9,8},{10,11... | collective-permute-start | bytes 983048 | tf_op jit(solution)/shard_map/ppermute | solution.py:258
  147.2 3.0 %collective-permute-start.8 = (bf16[256,1280]{1,0:T(8,128)(2,1)S(1)}, bf16[256,1280]{1,0:T(8,128)(2,1)S(1)}, u32[]{:S(2)}, u32[]{:S(2)}) collective-permute-start(bf16[256,1280]{1,0:T(8,128)(2,1)S(1)} %collective-permute-done.7.x_own), channel_id=1, source_target_pairs={{0,1},{1,0},{2,3},{3,2},{4,5},{5,4},{6,7},{7,6},{8,9},{9,8},{10,11... | collective-permute-start | bytes 1966088 | tf_op jit(solution)/shard_map/ppermute | solution.py:258
  158.5 11.7 %collective-permute-start.9 = (bf16[96,1280]{1,0:T(8,128)(2,1)S(1)}, bf16[96,1280]{1,0:T(8,128)(2,1)S(1)}, u32[]{:S(2)}, u32[]{:S(2)}) collective-permute-start(bf16[96,1280]{1,0:T(8,128)(2,1)S(1)} %get-tuple-element.34), channel_id=1, source_target_pairs={{0,2},{1,3},{2,4},{3,5},{4,6},{5,7},{8,10},{9,11},{10,12},{11,13},... | collective-permute-start | bytes 737288 | tf_op jit(solution)/shard_map/ppermute | solution.py:267
  160.8 9.5 %collective-permute-start.10 = (bf16[32,1280]{1,0:T(8,128)(2,1)S(1)}, bf16[32,1280]{1,0:T(8,128)(2,1)S(1)}, u32[]{:S(2)}, u32[]{:S(2)}) collective-permute-start(bf16[32,1280]{1,0:T(8,128)(2,1)S(1)} %slice.63), channel_id=1, source_target_pairs={{0,4},{1,5},{2,6},{3,7},{8,12},{9,13},{10,14},{11,15},{16,20},{17,... | collective-permute-start | bytes 245768 | tf_op jit(solution)/shard_map/ppermute | solution.py:267
  165.1 5.2 %collective-permute-start.11 = (bf16[32,1280]{1,0:T(8,128)(2,1)S(1)}, bf16[32,1280]{1,0:T(8,128)(2,1)S(1)}, u32[]{:S(2)}, u32[]{:S(2)}) collective-permute-start(bf16[32,1280]{1,0:T(8,128)(2,1)S(1)} %slice.63), channel_id=1, source_target_pairs={{0,6},{1,7},{8,14},{9,15},{16,22},{17,23},{24,30},{25,31},{32,38},... | collective-permute-start | bytes 245768 | tf_op jit(solution)/shard_map/ppermute | solution.py:267
  173.7 2.3 collective-permute-start.12
  178.7 2.2 collective-permute-start.14
  185.4 11.9 %collective-permute-start.15 = (bf16[96,1280]{1,0:T(8,128)(2,1)S(1)}, bf16[96,1280]{1,0:T(8,128)(2,1)S(1)}, u32[]{:S(2)}, u32[]{:S(2)}) collective-permute-start(bf16[96,1280]{1,0:T(8,128)(2,1)S(1)} %get-tuple-element.39), channel_id=1, source_target_pairs={{0,2},{1,3},{2,4},{3,5},{4,6},{5,7},{8,10},{9,11},{10,12},{11,13},... | collective-permute-start | bytes 737288 | tf_op jit(solution)/shard_map/ppermute | solution.py:267
  186.7 10.5 %collective-permute-start.16 = (bf16[32,1280]{1,0:T(8,128)(2,1)S(1)}, bf16[32,1280]{1,0:T(8,128)(2,1)S(1)}, u32[]{:S(2)}, u32[]{:S(2)}) collective-permute-start(bf16[32,1280]{1,0:T(8,128)(2,1)S(1)} %slice.64), channel_id=1, source_target_pairs={{0,4},{1,5},{2,6},{3,7},{8,12},{9,13},{10,14},{11,15},{16,20},{17,... | collective-permute-start | bytes 245768 | tf_op jit(solution)/shard_map/ppermute | solution.py:267
  191.9 5.4 %collective-permute-start.17 = (bf16[32,1280]{1,0:T(8,128)(2,1)S(1)}, bf16[32,1280]{1,0:T(8,128)(2,1)S(1)}, u32[]{:S(2)}, u32[]{:S(2)}) collective-permute-start(bf16[32,1280]{1,0:T(8,128)(2,1)S(1)} %slice.64), channel_id=1, source_target_pairs={{0,6},{1,7},{8,14},{9,15},{16,22},{17,23},{24,30},{25,31},{32,38},... | collective-permute-start | bytes 245768 | tf_op jit(solution)/shard_map/ppermute | solution.py:267
  200.7 2.3 collective-permute-start.18
  205.0 49.6 %collective-permute-start.19 = (bf16[256,1280]{1,0:T(8,128)(2,1)S(1)}, bf16[256,1280]{1,0:T(8,128)(2,1)S(1)}, u32[]{:S(2)}, u32[]{:S(2)}) collective-permute-start(bf16[256,1280]{1,0:T(8,128)(2,1)S(1)} %shard_map.57), channel_id=1, source_target_pairs={{64,96},{65,97},{66,98},{67,99},{68,100},{69,101},{70,102},{71,103... | collective-permute-start | bytes 1966088 | tf_op jit(solution)/shard_map/ppermute | solution.py:327
  254.6 2.6 collective-permute-start.20
  261.8 11.7 %collective-permute-start.21 = (bf16[96,1280]{1,0:T(8,128)(2,1)S(1)}, bf16[96,1280]{1,0:T(8,128)(2,1)S(1)}, u32[]{:S(2)}, u32[]{:S(2)}) collective-permute-start(bf16[96,1280]{1,0:T(8,128)(2,1)S(1)} %get-tuple-element.44), channel_id=1, source_target_pairs={{0,2},{1,3},{2,4},{3,5},{4,6},{5,7},{8,10},{9,11},{10,12},{11,13},... | collective-permute-start | bytes 737288 | tf_op jit(solution)/shard_map/ppermute | solution.py:267
  263.1 10.4 %collective-permute-start.22 = (bf16[32,1280]{1,0:T(8,128)(2,1)S(1)}, bf16[32,1280]{1,0:T(8,128)(2,1)S(1)}, u32[]{:S(2)}, u32[]{:S(2)}) collective-permute-start(bf16[32,1280]{1,0:T(8,128)(2,1)S(1)} %slice.65), channel_id=1, source_target_pairs={{0,4},{1,5},{2,6},{3,7},{8,12},{9,13},{10,14},{11,15},{16,20},{17,... | collective-permute-start | bytes 245768 | tf_op jit(solution)/shard_map/ppermute | solution.py:267
  268.0 5.4 %collective-permute-start.23 = (bf16[32,1280]{1,0:T(8,128)(2,1)S(1)}, bf16[32,1280]{1,0:T(8,128)(2,1)S(1)}, u32[]{:S(2)}, u32[]{:S(2)}) collective-permute-start(bf16[32,1280]{1,0:T(8,128)(2,1)S(1)} %slice.65), channel_id=1, source_target_pairs={{0,6},{1,7},{8,14},{9,15},{16,22},{17,23},{24,30},{25,31},{32,38},... | collective-permute-start | bytes 245768 | tf_op jit(solution)/shard_map/ppermute | solution.py:267
  277.7 2.5 collective-permute-start.24
  (22 other events, 193.5 us)
Sparse Core Ops, SparseCore 0:
  12.5 79.3 all-gather.2
  94.1 48.3 all-gather.4
where the time goes:
time: 295 us; the launch traced here: 294 us
  waiting for transfers between devices  162 us (55%)
  Pallas kernels  56.8 us (19%)
  starting transfers between devices  44 us (15%)
  between operations  14 us (5%)
  local copies, waits for them, and re-layouts  13.6 us (5%)
  other arithmetic  3.36 us (1%)
    all_gather x2, waiting for transfers between devices, gather_chips(): lax.all_gather(block, 'seq', axis=0, tiled=True, axis_index_groups=groups)  99.7 us
    ppermute x3, waiting for transfers between devices, local(): x_own = lax.ppermute(produced, 'section', [(tick, tick + 1)])  48.3 us
    ppermute x12, starting transfers between devices, to_later_chip(): return lax.ppermute(value, 'seq', pairs)  32.3 us
    pallas_call x4, Pallas kernels, project_kv(): call(functools.partial(kv_kernel, heads), (2, 2), [whole((rows, half)), w...  18.1 us
    pallas_call x4, Pallas kernels, attend_local(): call(functools.partial(local_kernel, heads), (2,), [whole((rows, half)),...  15.3 us
    pallas_call x4, Pallas kernels, attend_remote(): call(functools.partial(remote_kernel, heads), (1,), [whole(query.shape),...  14.4 us
    ppermute x11, waiting for transfers between devices, swap(): return lax.ppermute(value, 'seq', [(i, i ^ 1) for i in range(count)])  14.3 us
    unnamed x36, local copies, waits for them, and re-layouts  10.7 us
  transfers between devices with their start and end apart: 28, of which 13 were waited for; matrix products, arithmetic and copies ran while one was open for 0% of the time, Pallas kernels for 8%

commit v1 on v0

v1 whole, which is shorter than its diff:
```python
import math

import jax
import jax.numpy as jnp
from jax import lax
from jax.experimental import pallas as pl
from jax.experimental.pallas import tpu as pltpu
from jax.sharding import PartitionSpec as P

NEG_FILL = -1e30
HD = 128
CHIP_ROWS = 256
GROUP_CHIPS = 4
BF16 = jnp.bfloat16
F32 = jnp.float32
VMEM_LIMIT = 24 * 1024 * 1024


def dot(a, b):
    return lax.dot_general(a, b, (((1,), (0,)), ((), ())), preferred_element_type=F32)


def dot_t(a, b):
    return lax.dot_general(a, b, (((1,), (1,)), ((), ())), preferred_element_type=F32)


def offset_of(scalars, branch, head_at, heads):
    return scalars[2 + branch * 2 * heads + scalars[0] * heads + head_at]


def spread(target, scalars, own, other):
    half = own.shape[1]
    core = scalars[0]
    target[:, pl.ds(pl.multiple_of(core * half, 128), half)] = own[...]
    target[:, pl.ds(pl.multiple_of((1 - core) * half, 128), half)] = other[...]


def kv_kernel(scalars, x_own, x_other, w, x_out, kv_out, send_out):
    width = kv_out.shape[1]
    heads = width // (2 * HD)
    spread(x_out, scalars, x_own, x_other)
    kv_out[...] = dot(x_out[...], w[...]).astype(BF16)
    row = lax.broadcasted_iota(jnp.int32, (96, CHIP_ROWS), 0)
    col = lax.broadcasted_iota(jnp.int32, (96, CHIP_ROWS), 1)
    for i in range(heads):
        off2 = offset_of(scalars, 2, i, heads)
        off3 = offset_of(scalars, 3, i, heads)
        source = jnp.where(row < 64, 4 * row + off2, 8 * (row - 64) + off3)
        pick = jnp.where(col == source, 1.0, 0.0).astype(BF16)
        cols = slice(2 * i * HD, 2 * (i + 1) * HD)
        send_out[:, cols] = dot(pick, kv_out[:, cols]).astype(BF16)


def local_kernel(scalars, x, w, kv, q_out, acc_out, stat_out):
    width = q_out.shape[1]
    heads = width // HD
    q_out[...] = dot(x[...], w[...]).astype(BF16)
    scaling = 1.0 / math.sqrt(HD)
    row = lax.broadcasted_iota(jnp.int32, (CHIP_ROWS, HD), 0)
    lane = lax.broadcasted_iota(jnp.int32, (CHIP_ROWS, HD), 1)
    first = ((lane == 0) & (row < 128)) | ((lane == 1) & (row >= 128))
    period = jnp.where(lane == 2, 1, jnp.where(lane == 3, 3, 7))
    in_branch = (lane >= 2) & (lane <= 4)
    phase = row & period
    causal = []
    for r in range(2):
        shape = (128, 128 * (r + 1))
        causal.append(
            lax.broadcasted_iota(jnp.int32, shape, 1)
            <= lax.broadcasted_iota(jnp.int32, shape, 0) + 128 * r
        )
    lane_half = lax.broadcasted_iota(jnp.int32, (128, HD), 1)
    stats = [jnp.zeros((128, HD), F32) for _ in range(2)]
    for i in range(heads):
        cols = slice(i * HD, (i + 1) * HD)
        keys = slice(2 * i * HD, (2 * i + 1) * HD)
        vals = slice((2 * i + 1) * HD, (2 * i + 2) * HD)
        offset = jnp.where(
            lane == 2,
            offset_of(scalars, 1, i, heads),
            jnp.where(
                lane == 3, offset_of(scalars, 2, i, heads), offset_of(scalars, 3, i, heads)
            ),
        )
        member = first | (in_branch & (phase == offset))
        member = jnp.where(member, 1.0, 0.0).astype(BF16)
        for r in range(2):
            rows = slice(128 * r, 128 * (r + 1))
            seen = slice(0, 128 * (r + 1))
            times = jnp.where(causal[r], dot_t(member[rows], member[seen]), 0.0)
            scores = dot_t(q_out[rows, cols], kv[seen, keys]) * scaling
            scores = jnp.where(times > 0.0, scores, NEG_FILL)
            peak = jnp.max(scores, axis=1, keepdims=True)
            expos = times * jnp.exp(scores - peak)
            total = jnp.sum(expos, axis=1, keepdims=True)
            acc_out[rows, cols] = dot(expos.astype(BF16), kv[seen, vals])
            stats[r] = jnp.where(
                lane_half == i, peak, jnp.where(lane_half == heads + i, total, stats[r])
            )
    stat_out[:128] = stats[0]
    stat_out[128:] = stats[1]


def remote_kernel(scalars, query, acc, stat, near, mid, far, out):
    heads = out.shape[1] // HD
    scaling = 1.0 / math.sqrt(HD)
    chip = scalars[1]
    shape = (CHIP_ROWS, 160)
    row = lax.broadcasted_iota(jnp.int32, shape, 0)
    col = lax.broadcasted_iota(jnp.int32, shape, 1)
    second = (col < 64) & ((chip & 1) == 1)
    third = (col >= 64) & (chip >= 1 + (col - 64) // 32)
    row2 = jnp.where(second, row & 3, -1)
    row3 = jnp.where(third, row & 7, -1)
    for i in range(heads):
        cols = slice(i * HD, (i + 1) * HD)
        keys = slice(2 * i * HD, (2 * i + 1) * HD)
        vals = slice((2 * i + 1) * HD, (2 * i + 2) * HD)
        off2 = offset_of(scalars, 2, i, heads)
        off3 = offset_of(scalars, 3, i, heads)
        allowed = (row2 == off2) | (row3 == off3)
        key_rows = jnp.concatenate([near[:, keys], mid[:, keys], far[:, keys]], axis=0)
        value_rows = jnp.concatenate([near[:, vals], mid[:, vals], far[:, vals]], axis=0)
        scores = dot_t(query[:, cols], key_rows) * scaling
        scores = jnp.where(allowed, scores, NEG_FILL)
        peak = stat[:, i : i + 1]
        total = stat[:, heads + i : heads + i + 1]
        new_peak = jnp.maximum(peak, jnp.max(scores, axis=1, keepdims=True))
        expos = jnp.exp(scores - new_peak)
        shrink = jnp.exp(peak - new_peak)
        total = total * shrink + jnp.sum(expos, axis=1, keepdims=True)
        mixed = acc[:, cols] * shrink + dot(expos.astype(BF16), value_rows)
        out[:, cols] = (mixed / total).astype(BF16)


def back_kernel(scalars, x_own, att_own, att_other, w, out, att):
    spread(att, scalars, att_own, att_other)
    out[...] = (x_own[...].astype(F32) + dot(att[...], w[...])).astype(BF16)


def unpack_kv_kernel(w, out, sems):
    parts = sems.shape[0]
    rows = out.shape[0] // parts
    copies = []
    for i in range(parts):
        at = pl.ds(i * rows, rows)
        copies.append(
            pltpu.make_async_copy(
                w.at[at, pl.ds(0, out.shape[1])], out.at[at, :], sems.at[i]
            )
        )
    for copy in copies:
        copy.start()
    for copy in copies:
        copy.wait()


def unpack_rest_kernel(w, query, back, query_sems, back_sems):
    width = query.shape[1]
    copies = []
    parts = query_sems.shape[0]
    rows = query.shape[0] // parts
    for i in range(parts):
        at = pl.ds(i * rows, rows)
        copies.append(
            pltpu.make_async_copy(
                w.at[at, pl.ds(2 * width, width)], query.at[at, :], query_sems.at[i]
            )
        )
    chips = back_sems.shape[0] // 2
    rows = back.shape[0] // chips
    for i in range(chips):
        for h in range(2):
            copies.append(
                pltpu.make_async_copy(
                    w.at[pl.ds((2 * i + h) * rows, rows), pl.ds(3 * width, width)],
                    back.at[pl.ds(i * rows, rows), pl.ds(h * width, width)],
                    back_sems.at[2 * i + h],
                )
            )
    for copy in copies:
        copy.start()
    for copy in copies:
        copy.wait()


def unpack(body, w, out_shape, sems):
    return pl.pallas_call(
        body,
        in_specs=[pl.BlockSpec(memory_space=pl.ANY)],
        out_specs=jax.tree.map(lambda _: pl.BlockSpec(memory_space=pltpu.VMEM), out_shape),
        out_shape=out_shape,
        scratch_shapes=[pltpu.SemaphoreType.DMA((count,)) for count in sems],
        compiler_params=pltpu.CompilerParams(vmem_limit_bytes=VMEM_LIMIT),
    )(w)


def call(body, out_shape, scratch, flops, scalars, *operands):
    in_specs = [pl.BlockSpec(memory_space=pltpu.SMEM)]
    in_specs += [pl.BlockSpec(memory_space=pltpu.VMEM) for _ in operands]
    out_specs = jax.tree.map(lambda _: pl.BlockSpec(memory_space=pltpu.VMEM), out_shape)
    return pl.pallas_call(
        body,
        in_specs=in_specs,
        out_specs=out_specs,
        out_shape=out_shape,
        scratch_shapes=scratch,
        compiler_params=pltpu.CompilerParams(vmem_limit_bytes=VMEM_LIMIT),
        cost_estimate=pl.CostEstimate(flops=flops, bytes_accessed=2**20, transcendentals=0),
    )(scalars, *operands)


def project_kv(scalars, x_own, x_other, w):
    rows, half = x_own.shape
    width = w.shape[1] // 2
    return call(
        kv_kernel,
        [
            jax.ShapeDtypeStruct((rows, 2 * half), BF16),
            jax.ShapeDtypeStruct((rows, 2 * width), BF16),
            jax.ShapeDtypeStruct((96, 2 * width), BF16),
        ],
        [],
        8 * rows * half * width,
        scalars,
        x_own,
        x_other,
        w,
    )


def attend_local(scalars, x, w, kv):
    rows = x.shape[0]
    width = w.shape[1]
    return call(
        local_kernel,
        [
            jax.ShapeDtypeStruct((rows, width), BF16),
            jax.ShapeDtypeStruct((rows, width), F32),
            jax.ShapeDtypeStruct((rows, HD), F32),
        ],
        [],
        4 * rows * x.shape[1] * width,
        scalars,
        x,
        w,
        kv,
    )


def attend_remote(scalars, query, acc, stats, near, mid, far):
    rows, width = query.shape
    return call(
        remote_kernel,
        jax.ShapeDtypeStruct((rows, width), BF16),
        [],
        4 * rows * 160 * width,
        scalars,
        query,
        acc,
        stats,
        near,
        mid,
        far,
    )


def project_back(scalars, x_own, att_own, att_other, w):
    rows, half = x_own.shape
    width = att_own.shape[1]
    return call(
        back_kernel,
        jax.ShapeDtypeStruct((rows, half), BF16),
        [pltpu.VMEM((rows, 2 * width), BF16)],
        4 * rows * half * width,
        scalars,
        x_own,
        att_own,
        att_other,
        w,
    )


def swap(value):
    count = lax.axis_size("seq")
    return lax.ppermute(value, "seq", [(i, i ^ 1) for i in range(count)])


def to_later_chip(value, steps):
    count = lax.axis_size("seq")
    pairs = []
    for source in range(count):
        if (source // 2) % GROUP_CHIPS + steps < GROUP_CHIPS:
            pairs.append((source, source + 2 * steps))
    return lax.ppermute(value, "seq", pairs)


def in_order(core, own, other, axis):
    return jnp.where(
        core == 0,
        jnp.concatenate([own, other], axis=axis),
        jnp.concatenate([other, own], axis=axis),
    )


def gather_chips(block):
    count = lax.axis_size("seq")
    groups = [list(range(core, count, 2)) for core in range(2)]
    return lax.all_gather(block, "seq", axis=0, tiled=True, axis_index_groups=groups)


def local(tokens, w_qkv, w_out, offsets):
    section = lax.axis_index("section")
    section_count = lax.axis_size("section")
    seq = lax.axis_index("seq")
    core = seq % 2
    scalars = jnp.concatenate(
        [
            jnp.stack([core, (seq // 2) % GROUP_CHIPS]).astype(jnp.int32),
            offsets.reshape(-1).astype(jnp.int32),
        ]
    )
    with jax.named_scope("weights"):
        rows = w_qkv.shape[1]
        width = w_qkv.shape[2] // 6
        heads = width // HD
        cut = w_out.shape[2] // 2
        parts = w_qkv[0].reshape(rows, 3, 2, heads, HD)

        def half_of(h):
            kv = jnp.stack([parts[:, 1, h], parts[:, 2, h]], axis=2).reshape(rows, 2 * width)
            query = parts[:, 0, h].reshape(rows, width)
            back = w_out[0][:, h * cut : (h + 1) * cut]
            back = jnp.concatenate([back[:, :width], back[:, width:]], axis=0)
            return jnp.concatenate([kv, query, back], axis=1)

        halves = [half_of(0), half_of(1)]
        own = jnp.where(core == 0, halves[0], halves[1])
        other = swap(jnp.where(core == 0, halves[1], halves[0]))
        block = in_order(core, own[:, : 3 * width], other[:, : 3 * width], 0)
        back = [
            in_order(core, own[at, 3 * width :], other[at, 3 * width :], 0)
            for at in (slice(0, rows // 2), slice(rows // 2, rows))
        ]
        block = jnp.concatenate([block, jnp.concatenate(back, axis=0)], axis=1)
        w_all = gather_chips(block)
        depth = w_all.shape[0]
        w_kv = unpack(
            unpack_kv_kernel, w_all, jax.ShapeDtypeStruct((depth, 2 * width), BF16), [8]
        )
        w_q, w_back = unpack(
            unpack_rest_kernel,
            w_all,
            [
                jax.ShapeDtypeStruct((depth, width), BF16),
                jax.ShapeDtypeStruct((depth // 2, cut), BF16),
            ],
            [8, depth // rows],
        )
    with jax.named_scope("tokens"):
        both = in_order(core, tokens[0], swap(tokens[0]), 0)
        left, right = both[:, :cut], both[:, cut:]
        x_own = jnp.where(core == 0, left, right)
        x_other = jnp.where(core == 0, right, left)
    result = jnp.zeros_like(x_own)
    for tick in range(section_count):
        x, kv, send = project_kv(scalars, x_own, x_other, w_kv)
        near = to_later_chip(send, 1)
        mid = to_later_chip(send[64:], 2)
        far = to_later_chip(send[64:], 3)
        query, acc, stats = attend_local(scalars, x, w_q, kv)
        att = attend_remote(scalars, query, acc, stats, near, mid, far)
        produced = project_back(scalars, x_own, att, swap(att), w_back)
        result = jnp.where(section == tick, produced, result)
        if tick + 1 < section_count:
            x_own = lax.ppermute(produced, "section", [(tick, tick + 1)])
            x_other = swap(x_own)
    with jax.named_scope("result"):
        top, bottom = result[:128], result[128:]
        mine = jnp.where(core == 0, top, bottom)
        theirs = swap(jnp.where(core == 0, bottom, top))
        return in_order(core, mine, theirs, 1)[None, None]


def solution(mesh):
    return jax.shard_map(
        local,
        mesh=mesh,
        in_specs=(P(None, "seq", None), P("section", "seq", None), P("section", "seq", None), P()),
        out_specs=P("section", None, "seq", None),
        check_vma=False,
    )
```

time: 295 us -> 271 us (0.919)
  starting transfers between devices: 44 us -> 37.6 us
  Pallas kernels: 56.8 us -> 50.5 us
  waiting for transfers between devices: 162 us -> 156 us
  local copies, waits for them, and re-layouts: 13.6 us -> 9.89 us
    all_gather x2 -> x1, waiting for transfers between devices: 99.7 us -> 91.9 us  [gather_chips(): lax.all_gather(block, 'seq', axis=0, tiled=True, axis_index_groups=groups)]
    pallas_call x16 -> x18, Pallas kernels: 56.8 us -> 50.5 us  [the longest x16 48.8 us: call(): pl.pallas_call(body, in_specs=in_specs, out_specs=out_specs, out_shape=ou...]
    ppermute x12, starting transfers between devices: 32.3 us -> 27.7 us  [to_later_chip(): return lax.ppermute(value, 'seq', pairs)]
    unnamed x36, local copies, waits for them, and re-layouts: 10.7 us -> 6.26 us
    ppermute x11 -> x10, starting transfers between devices: 8.98 us -> 7.14 us  [swap(): return lax.ppermute(value, 'seq', [(i, i ^ 1) for i in range(count)])]
    ppermute x11 -> x10, waiting for transfers between devices: 14.3 us -> 14.7 us  [swap(): return lax.ppermute(value, 'seq', [(i, i ^ 1) for i in range(count)])]
  transfers between devices with their start and end apart: 28 -> 26, of which waited for: 13 -> 12; matrix products, arithmetic and copies ran while one was open for 0% -> 0% of each run, Pallas kernels for 8% -> 7%
where the time goes in v1:
time: 271 us
  waiting for transfers between devices  156 us (58%)
  Pallas kernels  50.5 us (19%)
  starting transfers between devices  37.6 us (14%)
  between operations  14.1 us (5%)
  local copies, waits for them, and re-layouts  9.89 us (4%)
  other arithmetic  2.88 us (1%)
    all_gather x1, waiting for transfers between devices, gather_chips(): lax.all_gather(block, 'seq', axis=0, tiled=True, axis_index_groups=groups)  91.9 us
    ppermute x3, waiting for transfers between devices, local(): x_own = lax.ppermute(produced, 'section', [(tick, tick + 1)])  49.1 us
    pallas_call x16, Pallas kernels, call(): pl.pallas_call(body, in_specs=in_specs, out_specs=out_specs, out_shape=ou...  48.8 us
    ppermute x12, starting transfers between devices, to_later_chip(): return lax.ppermute(value, 'seq', pairs)  27.7 us
    ppermute x10, waiting for transfers between devices, swap(): return lax.ppermute(value, 'seq', [(i, i ^ 1) for i in range(count)])  14.7 us
    ppermute x10, starting transfers between devices, swap(): return lax.ppermute(value, 'seq', [(i, i ^ 1) for i in range(count)])  7.14 us
    unnamed x36, local copies, waits for them, and re-layouts  6.26 us
  transfers between devices with their start and end apart: 26, of which 12 were waited for; matrix products, arithmetic and copies ran while one was open for 0% of the time, Pallas kernels for 7%

profile of v1, /device:TPU:25, one launch (start us, length us, event | category | flops | bytes accessed | tf_op | source)
XLA Modules:
  0.0 270.6 jit_solution(6673422085278967194)
XLA Ops:
  16.5 91.9 %all-gather.2.cloned.1.call-done.w = bf16[2560,2560]{1,0:T(8,128)(2,1)} async-done(((bf16[160,2560]{1,0:T(8,128)(2,1)}), bf16[2560,2560]{1,0:T(8,128)(2,1)}) %all-gather.2.cloned.1.call-update) | async-done | bytes 13107216 | tf_op jit(solution)/shard_map/weights/all_gather | solution.py:309
  108.3 4.7 %copy-done = bf16[2560,2560]{1,0:T(8,128)(2,1)S(1)} copy-done((bf16[2560,2560]{1,0:T(8,128)(2,1)S(1)}, bf16[2560,2560]{1,0:T(8,128)(2,1)}, u32[]{:S(2)}) %copy-start) | copy-done | bytes 13107224
  113.6 2.7 %shard_map.46 = (bf16[256,2560]{1,0:T(8,128)(2,1)S(1)}, bf16[256,1280]{1,0:T(8,128)(2,1)S(1)}, bf16[96,1280]{1,0:T(8,128)(2,1)S(1)}) custom-call(s32[42]{0:T(128)S(1)} %pad_add_fusion.scalars, bf16[256,1280]{1,0:T(8,128)(2,1)S(1)} %get-tuple-element.58.x_own, bf16[256,1280]{1,0:T(8,128)(2,1)S(1)} %get-tuple-element.57.x_other, bf16[2560,1280]{1,0:T(8,128)(2,1)S(1)} %weights.2.w), custom_call_target="tpu_custom_call" | custom-call | flops 1677721600 | bytes 1048576 | tf_op jit(solution)/shard_map/pallas_call | solution.py:202
  116.3 3.1 %collective-permute-start.2 = (bf16[96,1280]{1,0:T(8,128)(2,1)S(1)}, bf16[96,1280]{1,0:T(8,128)(2,1)S(1)}, u32[]{:S(2)}, u32[]{:S(2)}) collective-permute-start(bf16[96,1280]{1,0:T(8,128)(2,1)S(1)} %get-tuple-element.37), channel_id=1, source_target_pairs={{0,2},{1,3},{2,4},{3,5},{4,6},{5,7},{8,10},{9,11},{10,12},{11,13},... | collective-permute-start | bytes 737288 | tf_op jit(solution)/shard_map/ppermute | solution.py:295
  119.4 2.7 collective-permute-start.4
  122.1 2.5 collective-permute-start.3
  125.8 4.2 %shard_map.47 = (bf16[256,640]{1,0:T(8,128)(2,1)S(1)}, f32[256,640]{1,0:T(8,128)S(1)}, f32[256,128]{1,0:T(8,128)S(1)}) custom-call(s32[42]{0:T(128)S(1)} %pad_add_fusion.scalars, bf16[256,2560]{1,0:T(8,128)(2,1)S(1)} %get-tuple-element.31.x, bf16[2560,640]{1,0:T(8,128)(2,1)S(1)} %get-tuple-element.32.w, bf16[256,1280]{1,0:T(8,128)(2,1)S(1)} %get-tuple-element.33.kv), custom_call_target="tpu_custom_call" | custom-call | flops 1677721600 | bytes 1048576 | tf_op jit(solution)/shard_map/pallas_call | solution.py:202
  130.0 3.4 %shard_map.48.att_own = bf16[256,640]{1,0:T(8,128)(2,1)S(1)} custom-call(s32[42]{0:T(128)S(1)} %pad_add_fusion.scalars, bf16[256,640]{1,0:T(8,128)(2,1)S(1)} %get-tuple-element.34.query, f32[256,640]{1,0:T(8,128)S(1)} %get-tuple-element.35.acc, f32[256,128]{1,0:T(8,128)S(1)} %get-tuple-element.36.stat, bf16[96,1280]{1,0:T(8,128)(2,1)S(1)} %collective-permute-done.2.near, ...), custom_call_target="tpu_custom_call" | custom-call | flops 104857600 | bytes 1048576 | tf_op jit(solution)/shard_map/pallas_call | solution.py:202
  140.7 2.7 %shard_map.50 = (bf16[256,2560]{1,0:T(8,128)(2,1)S(1)}, bf16[256,1280]{1,0:T(8,128)(2,1)S(1)}, bf16[96,1280]{1,0:T(8,128)(2,1)S(1)}) custom-call(s32[42]{0:T(128)S(1)} %pad_add_fusion.scalars, bf16[256,1280]{1,0:T(8,128)(2,1)S(1)} %collective-permute-done.6.x_own, bf16[256,1280]{1,0:T(8,128)(2,1)S(1)} %collective-permute-done.7.x_other, ...), custom_call_target="tpu_custom_call" | custom-call | flops 1677721600 | bytes 1048576 | tf_op jit(solution)/shard_map/pallas_call | solution.py:202
  146.0 2.1 collective-permute-start.9
  148.2 4.2 %shard_map.51 = (bf16[256,640]{1,0:T(8,128)(2,1)S(1)}, f32[256,640]{1,0:T(8,128)S(1)}, f32[256,128]{1,0:T(8,128)S(1)}) custom-call(s32[42]{0:T(128)S(1)} %pad_add_fusion.scalars, bf16[256,2560]{1,0:T(8,128)(2,1)S(1)} %get-tuple-element.39.x, bf16[2560,640]{1,0:T(8,128)(2,1)S(1)} %get-tuple-element.32.w, bf16[256,1280]{1,0:T(8,128)(2,1)S(1)} %get-tuple-element.40.kv), custom_call_target="tpu_custom_call" | custom-call | flops 1677721600 | bytes 1048576 | tf_op jit(solution)/shard_map/pallas_call | solution.py:202
  152.4 3.4 %shard_map.52.att_own = bf16[256,640]{1,0:T(8,128)(2,1)S(1)} custom-call(s32[42]{0:T(128)S(1)} %pad_add_fusion.scalars, bf16[256,640]{1,0:T(8,128)(2,1)S(1)} %get-tuple-element.41.query, f32[256,640]{1,0:T(8,128)S(1)} %get-tuple-element.42.acc, f32[256,128]{1,0:T(8,128)S(1)} %get-tuple-element.43.stat, bf16[96,1280]{1,0:T(8,128)(2,1)S(1)} %collective-permute-done.8.near, ...), custom_call_target="tpu_custom_call" | custom-call | flops 104857600 | bytes 1048576 | tf_op jit(solution)/shard_map/pallas_call | solution.py:202
  162.4 2.7 %shard_map.54 = (bf16[256,2560]{1,0:T(8,128)(2,1)S(1)}, bf16[256,1280]{1,0:T(8,128)(2,1)S(1)}, bf16[96,1280]{1,0:T(8,128)(2,1)S(1)}) custom-call(s32[42]{0:T(128)S(1)} %pad_add_fusion.scalars, bf16[256,1280]{1,0:T(8,128)(2,1)S(1)} %collective-permute-done.12.x_own, bf16[256,1280]{1,0:T(8,128)(2,1)S(1)} %collective-permute-done.13.x_other, ...), custom_call_target="tpu_custom_call" | custom-call | flops 1677721600 | bytes 1048576 | tf_op jit(solution)/shard_map/pallas_call | solution.py:202
  165.2 2.3 collective-permute-start.14
  169.1 4.0 %collective-permute-start.15 = (bf16[32,1280]{1,0:T(8,128)(2,1)S(1)}, bf16[32,1280]{1,0:T(8,128)(2,1)S(1)}, u32[]{:S(2)}, u32[]{:S(2)}) collective-permute-start(bf16[32,1280]{1,0:T(8,128)(2,1)S(1)} %slice.102), channel_id=1, source_target_pairs={{0,4},{1,5},{2,6},{3,7},{8,12},{9,13},{10,14},{11,15},{16,20},{17,... | collective-permute-start | bytes 245768 | tf_op jit(solution)/shard_map/ppermute | solution.py:295
  173.1 4.1 %shard_map.55 = (bf16[256,640]{1,0:T(8,128)(2,1)S(1)}, f32[256,640]{1,0:T(8,128)S(1)}, f32[256,128]{1,0:T(8,128)S(1)}) custom-call(s32[42]{0:T(128)S(1)} %pad_add_fusion.scalars, bf16[256,2560]{1,0:T(8,128)(2,1)S(1)} %get-tuple-element.45.x, bf16[2560,640]{1,0:T(8,128)(2,1)S(1)} %get-tuple-element.32.w, bf16[256,1280]{1,0:T(8,128)(2,1)S(1)} %get-tuple-element.46.kv), custom_call_target="tpu_custom_call" | custom-call | flops 1677721600 | bytes 1048576 | tf_op jit(solution)/shard_map/pallas_call | solution.py:202
  177.3 3.4 %shard_map.56.att_own = bf16[256,640]{1,0:T(8,128)(2,1)S(1)} custom-call(s32[42]{0:T(128)S(1)} %pad_add_fusion.scalars, bf16[256,640]{1,0:T(8,128)(2,1)S(1)} %get-tuple-element.47.query, f32[256,640]{1,0:T(8,128)S(1)} %get-tuple-element.48.acc, f32[256,128]{1,0:T(8,128)S(1)} %get-tuple-element.49.stat, bf16[96,1280]{1,0:T(8,128)(2,1)S(1)} %collective-permute-done.14.near, ...), custom_call_target="tpu_custom_call" | custom-call | flops 104857600 | bytes 1048576 | tf_op jit(solution)/shard_map/pallas_call | solution.py:202
  185.6 49.1 %collective-permute-done.18.x_own = bf16[256,1280]{1,0:T(8,128)(2,1)S(1)} collective-permute-done((bf16[256,1280]{1,0:T(8,128)(2,1)S(1)}, bf16[256,1280]{1,0:T(8,128)(2,1)S(1)}, u32[]{:S(2)}, u32[]{:S(2)}) %collective-permute-start.18) | collective-permute-done | bytes 655392 | tf_op jit(solution)/shard_map/ppermute | solution.py:376
  237.3 2.7 %shard_map.58 = (bf16[256,2560]{1,0:T(8,128)(2,1)S(1)}, bf16[256,1280]{1,0:T(8,128)(2,1)S(1)}, bf16[96,1280]{1,0:T(8,128)(2,1)S(1)}) custom-call(s32[42]{0:T(128)S(1)} %pad_add_fusion.scalars, bf16[256,1280]{1,0:T(8,128)(2,1)S(1)} %collective-permute-done.18.x_own, bf16[256,1280]{1,0:T(8,128)(2,1)S(1)} %collective-permute-done.19.x_other, ...), custom_call_target="tpu_custom_call" | custom-call | flops 1677721600 | bytes 1048576 | tf_op jit(solution)/shard_map/pallas_call | solution.py:202
  240.0 1.8 collective-permute-start.20
  243.2 3.8 %collective-permute-start.21 = (bf16[32,1280]{1,0:T(8,128)(2,1)S(1)}, bf16[32,1280]{1,0:T(8,128)(2,1)S(1)}, u32[]{:S(2)}, u32[]{:S(2)}) collective-permute-start(bf16[32,1280]{1,0:T(8,128)(2,1)S(1)} %slice.103), channel_id=1, source_target_pairs={{0,4},{1,5},{2,6},{3,7},{8,12},{9,13},{10,14},{11,15},{16,20},{17,... | collective-permute-start | bytes 245768 | tf_op jit(solution)/shard_map/ppermute | solution.py:295
  247.0 4.2 %shard_map.59 = (bf16[256,640]{1,0:T(8,128)(2,1)S(1)}, f32[256,640]{1,0:T(8,128)S(1)}, f32[256,128]{1,0:T(8,128)S(1)}) custom-call(s32[42]{0:T(128)S(1)} %pad_add_fusion.scalars, bf16[256,2560]{1,0:T(8,128)(2,1)S(1)} %get-tuple-element.51.x, bf16[2560,640]{1,0:T(8,128)(2,1)S(1)} %get-tuple-element.32.w, bf16[256,1280]{1,0:T(8,128)(2,1)S(1)} %get-tuple-element.52.kv), custom_call_target="tpu_custom_call" | custom-call | flops 1677721600 | bytes 1048576 | tf_op jit(solution)/shard_map/pallas_call | solution.py:202
  251.2 4.2 %shard_map.60.att_own = bf16[256,640]{1,0:T(8,128)(2,1)} custom-call(s32[42]{0:T(128)S(1)} %pad_add_fusion.scalars, bf16[256,640]{1,0:T(8,128)(2,1)S(1)} %get-tuple-element.53.query, f32[256,640]{1,0:T(8,128)S(1)} %get-tuple-element.54.acc, f32[256,128]{1,0:T(8,128)S(1)} %get-tuple-element.55.stat, bf16[96,1280]{1,0:T(8,128)(2,1)S(1)} %collective-permute-done.20.near, ...), custom_call_target="tpu_custom_call" | custom-call | flops 104857600 | bytes 1048576 | tf_op jit(solution)/shard_map/pallas_call | solution.py:202
  258.7 2.1 shard_map.61
  (116 shorter events, 44.6 us)
Async XLA Ops:
  6.5 101.8 %all-gather.2.cloned.1.call-start = ((), (), s32[]{:S(2)}) async-start(), calls=%async_computation | async-start | bytes 13926400 | tf_op jit(solution)/shard_map/weights/all_gather | solution.py:309
  10.3 2.1 collective-permute-start.1
  14.0 2.1 collective-permute-start
  116.3 13.6 %collective-permute-start.2 = (bf16[96,1280]{1,0:T(8,128)(2,1)S(1)}, bf16[96,1280]{1,0:T(8,128)(2,1)S(1)}, u32[]{:S(2)}, u32[]{:S(2)}) collective-permute-start(bf16[96,1280]{1,0:T(8,128)(2,1)S(1)} %get-tuple-element.37), channel_id=1, source_target_pairs={{0,2},{1,3},{2,4},{3,5},{4,6},{5,7},{8,10},{9,11},{10,12},{11,13},... | collective-permute-start | bytes 737288 | tf_op jit(solution)/shard_map/ppermute | solution.py:295
  119.4 10.5 %collective-permute-start.4 = (bf16[32,1280]{1,0:T(8,128)(2,1)S(1)}, bf16[32,1280]{1,0:T(8,128)(2,1)S(1)}, u32[]{:S(2)}, u32[]{:S(2)}) collective-permute-start(bf16[32,1280]{1,0:T(8,128)(2,1)S(1)} %slice.100), channel_id=1, source_target_pairs={{0,6},{1,7},{8,14},{9,15},{16,22},{17,23},{24,30},{25,31},{32,38},... | collective-permute-start | bytes 245768 | tf_op jit(solution)/shard_map/ppermute | solution.py:295
  122.1 7.9 %collective-permute-start.3 = (bf16[32,1280]{1,0:T(8,128)(2,1)S(1)}, bf16[32,1280]{1,0:T(8,128)(2,1)S(1)}, u32[]{:S(2)}, u32[]{:S(2)}) collective-permute-start(bf16[32,1280]{1,0:T(8,128)(2,1)S(1)} %slice.100), channel_id=1, source_target_pairs={{0,4},{1,5},{2,6},{3,7},{8,12},{9,13},{10,14},{11,15},{16,20},{17,... | collective-permute-start | bytes 245768 | tf_op jit(solution)/shard_map/ppermute | solution.py:295
  133.4 2.6 collective-permute-start.5
  138.3 2.4 collective-permute-start.7
  143.4 9.0 %collective-permute-start.8 = (bf16[96,1280]{1,0:T(8,128)(2,1)S(1)}, bf16[96,1280]{1,0:T(8,128)(2,1)S(1)}, u32[]{:S(2)}, u32[]{:S(2)}) collective-permute-start(bf16[96,1280]{1,0:T(8,128)(2,1)S(1)} %get-tuple-element.44), channel_id=1, source_target_pairs={{0,2},{1,3},{2,4},{3,5},{4,6},{5,7},{8,10},{9,11},{10,12},{11,13},... | collective-permute-start | bytes 737288 | tf_op jit(solution)/shard_map/ppermute | solution.py:295
  144.7 7.6 %collective-permute-start.10 = (bf16[32,1280]{1,0:T(8,128)(2,1)S(1)}, bf16[32,1280]{1,0:T(8,128)(2,1)S(1)}, u32[]{:S(2)}, u32[]{:S(2)}) collective-permute-start(bf16[32,1280]{1,0:T(8,128)(2,1)S(1)} %slice.101), channel_id=1, source_target_pairs={{0,6},{1,7},{8,14},{9,15},{16,22},{17,23},{24,30},{25,31},{32,38},... | collective-permute-start | bytes 245768 | tf_op jit(solution)/shard_map/ppermute | solution.py:295
  146.0 6.3 %collective-permute-start.9 = (bf16[32,1280]{1,0:T(8,128)(2,1)S(1)}, bf16[32,1280]{1,0:T(8,128)(2,1)S(1)}, u32[]{:S(2)}, u32[]{:S(2)}) collective-permute-start(bf16[32,1280]{1,0:T(8,128)(2,1)S(1)} %slice.101), channel_id=1, source_target_pairs={{0,4},{1,5},{2,6},{3,7},{8,12},{9,13},{10,14},{11,15},{16,20},{17,... | collective-permute-start | bytes 245768 | tf_op jit(solution)/shard_map/ppermute | solution.py:295
  155.8 2.1 collective-permute-start.11
  160.3 2.2 collective-permute-start.13
  165.2 12.1 %collective-permute-start.14 = (bf16[96,1280]{1,0:T(8,128)(2,1)S(1)}, bf16[96,1280]{1,0:T(8,128)(2,1)S(1)}, u32[]{:S(2)}, u32[]{:S(2)}) collective-permute-start(bf16[96,1280]{1,0:T(8,128)(2,1)S(1)} %get-tuple-element.50), channel_id=1, source_target_pairs={{0,2},{1,3},{2,4},{3,5},{4,6},{5,7},{8,10},{9,11},{10,12},{11,13},... | collective-permute-start | bytes 737288 | tf_op jit(solution)/shard_map/ppermute | solution.py:295
  167.5 9.7 %collective-permute-start.16 = (bf16[32,1280]{1,0:T(8,128)(2,1)S(1)}, bf16[32,1280]{1,0:T(8,128)(2,1)S(1)}, u32[]{:S(2)}, u32[]{:S(2)}) collective-permute-start(bf16[32,1280]{1,0:T(8,128)(2,1)S(1)} %slice.102), channel_id=1, source_target_pairs={{0,6},{1,7},{8,14},{9,15},{16,22},{17,23},{24,30},{25,31},{32,38},... | collective-permute-start | bytes 245768 | tf_op jit(solution)/shard_map/ppermute | solution.py:295
  169.1 8.2 %collective-permute-start.15 = (bf16[32,1280]{1,0:T(8,128)(2,1)S(1)}, bf16[32,1280]{1,0:T(8,128)(2,1)S(1)}, u32[]{:S(2)}, u32[]{:S(2)}) collective-permute-start(bf16[32,1280]{1,0:T(8,128)(2,1)S(1)} %slice.102), channel_id=1, source_target_pairs={{0,4},{1,5},{2,6},{3,7},{8,12},{9,13},{10,14},{11,15},{16,20},{17,... | collective-permute-start | bytes 245768 | tf_op jit(solution)/shard_map/ppermute | solution.py:295
  180.7 2.0 collective-permute-start.17
  184.3 50.4 %collective-permute-start.18 = (bf16[256,1280]{1,0:T(8,128)(2,1)S(1)}, bf16[256,1280]{1,0:T(8,128)(2,1)S(1)}, u32[]{:S(2)}, u32[]{:S(2)}) collective-permute-start(bf16[256,1280]{1,0:T(8,128)(2,1)S(1)} %shard_map.57), channel_id=1, source_target_pairs={{64,96},{65,97},{66,98},{67,99},{68,100},{69,101},{70,102},{71,103... | collective-permute-start | bytes 1966088 | tf_op jit(solution)/shard_map/ppermute | solution.py:376
  234.6 2.6 collective-permute-start.19
  240.0 11.2 %collective-permute-start.20 = (bf16[96,1280]{1,0:T(8,128)(2,1)S(1)}, bf16[96,1280]{1,0:T(8,128)(2,1)S(1)}, u32[]{:S(2)}, u32[]{:S(2)}) collective-permute-start(bf16[96,1280]{1,0:T(8,128)(2,1)S(1)} %get-tuple-element.56), channel_id=1, source_target_pairs={{0,2},{1,3},{2,4},{3,5},{4,6},{5,7},{8,10},{9,11},{10,12},{11,13},... | collective-permute-start | bytes 737288 | tf_op jit(solution)/shard_map/ppermute | solution.py:295
  241.9 9.3 %collective-permute-start.22 = (bf16[32,1280]{1,0:T(8,128)(2,1)S(1)}, bf16[32,1280]{1,0:T(8,128)(2,1)S(1)}, u32[]{:S(2)}, u32[]{:S(2)}) collective-permute-start(bf16[32,1280]{1,0:T(8,128)(2,1)S(1)} %slice.103), channel_id=1, source_target_pairs={{0,6},{1,7},{8,14},{9,15},{16,22},{17,23},{24,30},{25,31},{32,38},... | collective-permute-start | bytes 245768 | tf_op jit(solution)/shard_map/ppermute | solution.py:295
  243.2 8.0 %collective-permute-start.21 = (bf16[32,1280]{1,0:T(8,128)(2,1)S(1)}, bf16[32,1280]{1,0:T(8,128)(2,1)S(1)}, u32[]{:S(2)}, u32[]{:S(2)}) collective-permute-start(bf16[32,1280]{1,0:T(8,128)(2,1)S(1)} %slice.103), channel_id=1, source_target_pairs={{0,4},{1,5},{2,6},{3,7},{8,12},{9,13},{10,14},{11,15},{16,20},{17,... | collective-permute-start | bytes 245768 | tf_op jit(solution)/shard_map/ppermute | solution.py:295
  255.3 2.2 collective-permute-start.23
  261.0 1.7 collective-permute-start.24
  (19 other events, 210.5 us)
Sparse Core Ops, SparseCore 0:
  13.8 94.5 all-gather.1

commit v2 on v1

--- a/solution.py
+++ b/solution.py
@@ -13,7 +13,8 @@
 GROUP_CHIPS = 4
 BF16 = jnp.bfloat16
 F32 = jnp.float32
-VMEM_LIMIT = 24 * 1024 * 1024
+VMEM_LIMIT = 20 * 1024 * 1024
+UNPACK_LIMIT = 46 * 1024 * 1024
 
 
 def dot(a, b):
@@ -28,18 +29,19 @@
     return scalars[2 + branch * 2 * heads + scalars[0] * heads + head_at]
 
 
-def spread(target, scalars, own, other):
-    half = own.shape[1]
-    core = scalars[0]
-    target[:, pl.ds(pl.multiple_of(core * half, 128), half)] = own[...]
-    target[:, pl.ds(pl.multiple_of((1 - core) * half, 128), half)] = other[...]
-
-
-def kv_kernel(scalars, x_own, x_other, w, x_out, kv_out, send_out):
+def rows_of(core, w):
+    half = w.shape[0] // 2
+    return w[pl.ds(pl.multiple_of(core * half, 128), half), :]
+
+
+def early_kernel(scalars, own, w, acc):
+    acc[...] = dot(own[...], rows_of(scalars[0], w))
+
+
+def kv_kernel(scalars, acc, other, w, kv_out, send_out):
     width = kv_out.shape[1]
     heads = width // (2 * HD)
-    spread(x_out, scalars, x_own, x_other)
-    kv_out[...] = dot(x_out[...], w[...]).astype(BF16)
+    kv_out[...] = (acc[...] + dot(other[...], rows_of(1 - scalars[0], w))).astype(BF16)
     row = lax.broadcasted_iota(jnp.int32, (96, CHIP_ROWS), 0)
     col = lax.broadcasted_iota(jnp.int32, (96, CHIP_ROWS), 1)
     for i in range(heads):
@@ -51,17 +53,19 @@
         send_out[:, cols] = dot(pick, kv_out[:, cols]).astype(BF16)
 
 
-def local_kernel(scalars, x, w, kv, q_out, acc_out, stat_out):
+def local_kernel(scalars, own, other, w, kv, q_out, acc_out, stat_out):
     width = q_out.shape[1]
     heads = width // HD
-    q_out[...] = dot(x[...], w[...]).astype(BF16)
+    core = scalars[0]
+    query = dot(own[...], rows_of(core, w)) + dot(other[...], rows_of(1 - core, w))
+    q_out[...] = query.astype(BF16)
     scaling = 1.0 / math.sqrt(HD)
     row = lax.broadcasted_iota(jnp.int32, (CHIP_ROWS, HD), 0)
     lane = lax.broadcasted_iota(jnp.int32, (CHIP_ROWS, HD), 1)
     first = ((lane == 0) & (row < 128)) | ((lane == 1) & (row >= 128))
     period = jnp.where(lane == 2, 1, jnp.where(lane == 3, 3, 7))
-    in_branch = (lane >= 2) & (lane <= 4)
-    phase = row & period
+    phase = jnp.where((lane >= 2) & (lane <= 4), row & period, -1)
+    phase = jnp.where(first, -2, phase)
     causal = []
     for r in range(2):
         shape = (128, 128 * (r + 1))
@@ -71,10 +75,9 @@
         )
     lane_half = lax.broadcasted_iota(jnp.int32, (128, HD), 1)
     stats = [jnp.zeros((128, HD), F32) for _ in range(2)]
-    for i in range(heads):
-        cols = slice(i * HD, (i + 1) * HD)
-        keys = slice(2 * i * HD, (2 * i + 1) * HD)
-        vals = slice((2 * i + 1) * HD, (2 * i + 2) * HD)
+    work = [(i, r) for i in range(heads) for r in range(2)]
+    members = []
+    for i in range(heads):
         offset = jnp.where(
             lane == 2,
             offset_of(scalars, 1, i, heads),
@@ -82,21 +85,30 @@
                 lane == 3, offset_of(scalars, 2, i, heads), offset_of(scalars, 3, i, heads)
             ),
         )
-        member = first | (in_branch & (phase == offset))
-        member = jnp.where(member, 1.0, 0.0).astype(BF16)
-        for r in range(2):
-            rows = slice(128 * r, 128 * (r + 1))
-            seen = slice(0, 128 * (r + 1))
-            times = jnp.where(causal[r], dot_t(member[rows], member[seen]), 0.0)
-            scores = dot_t(q_out[rows, cols], kv[seen, keys]) * scaling
-            scores = jnp.where(times > 0.0, scores, NEG_FILL)
-            peak = jnp.max(scores, axis=1, keepdims=True)
-            expos = times * jnp.exp(scores - peak)
-            total = jnp.sum(expos, axis=1, keepdims=True)
-            acc_out[rows, cols] = dot(expos.astype(BF16), kv[seen, vals])
-            stats[r] = jnp.where(
-                lane_half == i, peak, jnp.where(lane_half == heads + i, total, stats[r])
-            )
+        member = (phase == offset) | (phase == -2)
+        members.append(jnp.where(member, 1.0, 0.0).astype(BF16))
+    times, scores, peaks, expos = {}, {}, {}, {}
+    for i, r in work:
+        rows = slice(128 * r, 128 * (r + 1))
+        seen = slice(0, 128 * (r + 1))
+        times[i, r] = jnp.where(causal[r], dot_t(members[i][rows], members[i][seen]), 0.0)
+        keys = slice(2 * i * HD, (2 * i + 1) * HD)
+        raw = dot_t(q_out[rows, i * HD : (i + 1) * HD], kv[seen, keys]) * scaling
+        scores[i, r] = jnp.where(times[i, r] > 0.0, raw, NEG_FILL)
+    for at in work:
+        peaks[at] = jnp.max(scores[at], axis=1, keepdims=True)
+    for at in work:
+        expos[at] = times[at] * jnp.exp(scores[at] - peaks[at])
+    for i, r in work:
+        rows = slice(128 * r, 128 * (r + 1))
+        seen = slice(0, 128 * (r + 1))
+        vals = slice((2 * i + 1) * HD, (2 * i + 2) * HD)
+        acc_out[rows, i * HD : (i + 1) * HD] = dot(expos[i, r].astype(BF16), kv[seen, vals])
+    for i, r in work:
+        total = jnp.sum(expos[i, r], axis=1, keepdims=True)
+        stats[r] = jnp.where(
+            lane_half == i, peaks[i, r], jnp.where(lane_half == heads + i, total, stats[r])
+        )
     stat_out[:128] = stats[0]
     stat_out[128:] = stats[1]
 
@@ -112,30 +124,38 @@
     third = (col >= 64) & (chip >= 1 + (col - 64) // 32)
     row2 = jnp.where(second, row & 3, -1)
     row3 = jnp.where(third, row & 7, -1)
-    for i in range(heads):
-        cols = slice(i * HD, (i + 1) * HD)
+    scores, peaks, expos, mixed = [], [], [], []
+    for i in range(heads):
         keys = slice(2 * i * HD, (2 * i + 1) * HD)
-        vals = slice((2 * i + 1) * HD, (2 * i + 2) * HD)
         off2 = offset_of(scalars, 2, i, heads)
         off3 = offset_of(scalars, 3, i, heads)
         allowed = (row2 == off2) | (row3 == off3)
         key_rows = jnp.concatenate([near[:, keys], mid[:, keys], far[:, keys]], axis=0)
+        raw = dot_t(query[:, i * HD : (i + 1) * HD], key_rows) * scaling
+        scores.append(jnp.where(allowed, raw, NEG_FILL))
+    for i in range(heads):
+        peaks.append(jnp.maximum(stat[:, i : i + 1], jnp.max(scores[i], axis=1, keepdims=True)))
+    for i in range(heads):
+        expos.append(jnp.exp(scores[i] - peaks[i]))
+    for i in range(heads):
+        vals = slice((2 * i + 1) * HD, (2 * i + 2) * HD)
         value_rows = jnp.concatenate([near[:, vals], mid[:, vals], far[:, vals]], axis=0)
-        scores = dot_t(query[:, cols], key_rows) * scaling
-        scores = jnp.where(allowed, scores, NEG_FILL)
-        peak = stat[:, i : i + 1]
-        total = stat[:, heads + i : heads + i + 1]
-        new_peak = jnp.maximum(peak, jnp.max(scores, axis=1, keepdims=True))
-        expos = jnp.exp(scores - new_peak)
-        shrink = jnp.exp(peak - new_peak)
-        total = total * shrink + jnp.sum(expos, axis=1, keepdims=True)
-        mixed = acc[:, cols] * shrink + dot(expos.astype(BF16), value_rows)
-        out[:, cols] = (mixed / total).astype(BF16)
-
-
-def back_kernel(scalars, x_own, att_own, att_other, w, out, att):
-    spread(att, scalars, att_own, att_other)
-    out[...] = (x_own[...].astype(F32) + dot(att[...], w[...])).astype(BF16)
+        mixed.append(dot(expos[i].astype(BF16), value_rows))
+    for i in range(heads):
+        cols = slice(i * HD, (i + 1) * HD)
+        shrink = jnp.exp(stat[:, i : i + 1] - peaks[i])
+        total = stat[:, heads + i : heads + i + 1] * shrink
+        total = total + jnp.sum(expos[i], axis=1, keepdims=True)
+        inverse = 1.0 / total
+        out[:, cols] = (acc[:, cols] * (shrink * inverse) + mixed[i] * inverse).astype(BF16)
+
+
+def back_early_kernel(scalars, x_own, att_own, w, acc):
+    acc[...] = x_own[...].astype(F32) + dot(att_own[...], rows_of(scalars[0], w))
+
+
+def back_kernel(scalars, acc, att_other, w, out):
+    out[...] = (acc[...] + dot(att_other[...], rows_of(1 - scalars[0], w))).astype(BF16)
 
 
 def unpack_kv_kernel(w, out, sems):
@@ -191,11 +211,11 @@
         out_specs=jax.tree.map(lambda _: pl.BlockSpec(memory_space=pltpu.VMEM), out_shape),
         out_shape=out_shape,
         scratch_shapes=[pltpu.SemaphoreType.DMA((count,)) for count in sems],
-        compiler_params=pltpu.CompilerParams(vmem_limit_bytes=VMEM_LIMIT),
+        compiler_params=pltpu.CompilerParams(vmem_limit_bytes=UNPACK_LIMIT),
     )(w)
 
 
-def call(body, out_shape, scratch, flops, scalars, *operands):
+def call(body, out_shape, flops, scalars, *operands):
     in_specs = [pl.BlockSpec(memory_space=pltpu.SMEM)]
     in_specs += [pl.BlockSpec(memory_space=pltpu.VMEM) for _ in operands]
     out_specs = jax.tree.map(lambda _: pl.BlockSpec(memory_space=pltpu.VMEM), out_shape)
@@ -204,33 +224,41 @@
         in_specs=in_specs,
         out_specs=out_specs,
         out_shape=out_shape,
-        scratch_shapes=scratch,
         compiler_params=pltpu.CompilerParams(vmem_limit_bytes=VMEM_LIMIT),
-        cost_estimate=pl.CostEstimate(flops=flops, bytes_accessed=2**20, transcendentals=0),
+        cost_estimate=pl.CostEstimate(flops=flops, bytes_accessed=1, transcendentals=0),
     )(scalars, *operands)
 
 
-def project_kv(scalars, x_own, x_other, w):
-    rows, half = x_own.shape
-    width = w.shape[1] // 2
+def project_early(scalars, own, w):
+    rows, size = own.shape
+    return call(
+        early_kernel,
+        jax.ShapeDtypeStruct((rows, w.shape[1]), F32),
+        2 * rows * size * w.shape[1],
+        scalars,
+        own,
+        w,
+    )
+
+
+def project_kv(scalars, acc, other, w):
+    rows, width = acc.shape
     return call(
         kv_kernel,
         [
-            jax.ShapeDtypeStruct((rows, 2 * half), BF16),
-            jax.ShapeDtypeStruct((rows, 2 * width), BF16),
-            jax.ShapeDtypeStruct((96, 2 * width), BF16),
+            jax.ShapeDtypeStruct((rows, width), BF16),
+            jax.ShapeDtypeStruct((96, width), BF16),
         ],
-        [],
-        8 * rows * half * width,
-        scalars,
-        x_own,
-        x_other,
+        2 * rows * other.shape[1] * width,
+        scalars,
+        acc,
+        other,
         w,
     )
 
 
-def attend_local(scalars, x, w, kv):
-    rows = x.shape[0]
+def attend_local(scalars, own, other, w, kv):
+    rows = own.shape[0]
     width = w.shape[1]
     return call(
         local_kernel,
@@ -239,10 +267,10 @@
             jax.ShapeDtypeStruct((rows, width), F32),
             jax.ShapeDtypeStruct((rows, HD), F32),
         ],
-        [],
-        4 * rows * x.shape[1] * width,
-        scalars,
-        x,
+        4 * rows * (own.shape[1] + 2 * HD) * width,
+        scalars,
+        own,
+        other,
         w,
         kv,
     )
@@ -253,7 +281,6 @@
     return call(
         remote_kernel,
         jax.ShapeDtypeStruct((rows, width), BF16),
-        [],
         4 * rows * 160 * width,
         scalars,
         query,
@@ -265,17 +292,27 @@
     )
 
 
-def project_back(scalars, x_own, att_own, att_other, w):
-    rows, half = x_own.shape
-    width = att_own.shape[1]
-    return call(
-        back_kernel,
-        jax.ShapeDtypeStruct((rows, half), BF16),
-        [pltpu.VMEM((rows, 2 * width), BF16)],
-        4 * rows * half * width,
+def project_back_early(scalars, x_own, att_own, w):
+    rows, size = x_own.shape
+    return call(
+        back_early_kernel,
+        jax.ShapeDtypeStruct((rows, size), F32),
+        2 * rows * size * att_own.shape[1],
         scalars,
         x_own,
         att_own,
+        w,
+    )
+
+
+def project_back(scalars, acc, att_other, w):
+    rows, size = acc.shape
+    return call(
+        back_kernel,
+        jax.ShapeDtypeStruct((rows, size), BF16),
+        2 * rows * size * att_other.shape[1],
+        scalars,
+        acc,
         att_other,
         w,
     )
@@ -364,13 +401,15 @@
         x_other = jnp.where(core == 0, right, left)
     result = jnp.zeros_like(x_own)
     for tick in range(section_count):
-        x, kv, send = project_kv(scalars, x_own, x_other, w_kv)
+        acc = project_early(scalars, x_own, w_kv)
+        kv, send = project_kv(scalars, acc, x_other, w_kv)
         near = to_later_chip(send, 1)
         mid = to_later_chip(send[64:], 2)
         far = to_later_chip(send[64:], 3)
-        query, acc, stats = attend_local(scalars, x, w_q, kv)
+        query, acc, stats = attend_local(scalars, x_own, x_other, w_q, kv)
         att = attend_remote(scalars, query, acc, stats, near, mid, far)
-        produced = project_back(scalars, x_own, att, swap(att), w_back)
+        acc = project_back_early(scalars, x_own, att, w_back)
+        produced = project_back(scalars, acc, swap(att), w_back)
         result = jnp.where(section == tick, produced, result)
         if tick + 1 < section_count:
             x_own = lax.ppermute(produced, "section", [(tick, tick + 1)])

time: 271 us -> 267 us (0.985)
  waiting for transfers between devices: 156 us -> 146 us
  starting transfers between devices: 37.6 us -> 43 us
  Pallas kernels: 50.5 us -> 55.3 us
  local copies, waits for them, and re-layouts: 9.89 us -> 5.16 us
    ppermute x10, waiting for transfers between devices: 14.7 us -> 5 us  [swap(): return lax.ppermute(value, 'seq', [(i, i ^ 1) for i in range(count)])]
    ppermute x12, starting transfers between devices: 27.7 us -> 32.9 us  [to_later_chip(): return lax.ppermute(value, 'seq', pairs)]
    unnamed x36 -> x30, local copies, waits for them, and re-layouts: 6.26 us -> 1.54 us
    pallas_call x2, Pallas kernels: 1.66 us -> 6.33 us  [unpack(): pl.pallas_call(body, in_specs=[pl.BlockSpec(memory_space=pl.ANY)], out_sp...]
    pallas_call x16 -> x24, Pallas kernels: 48.8 us -> 49 us  [call(): pl.pallas_call(body, in_specs=in_specs, out_specs=out_specs, out_shape=ou...]
  transfers between devices with their start and end apart: 26 -> 26, of which waited for: 12 -> 9; matrix products, arithmetic and copies ran while one was open for 0% -> 0% of each run, Pallas kernels for 7% -> 9%
where the time goes in v2:
time: 267 us
  waiting for transfers between devices  146 us (55%)
  Pallas kernels  55.3 us (21%)
  starting transfers between devices  43 us (16%)
  between operations  14.2 us (5%)
  local copies, waits for them, and re-layouts  5.16 us (2%)
  other arithmetic  2.88 us (1%)
    all_gather x1, waiting for transfers between devices, gather_chips(): lax.all_gather(block, 'seq', axis=0, tiled=True, axis_index_groups=groups)  91.8 us
    ppermute x3, waiting for transfers between devices, local(): x_own = lax.ppermute(produced, 'section', [(tick, tick + 1)])  49.1 us
    pallas_call x24, Pallas kernels, call(): pl.pallas_call(body, in_specs=in_specs, out_specs=out_specs, out_shape=ou...  49 us
    ppermute x12, starting transfers between devices, to_later_chip(): return lax.ppermute(value, 'seq', pairs)  32.9 us
    ppermute x10, starting transfers between devices, swap(): return lax.ppermute(value, 'seq', [(i, i ^ 1) for i in range(count)])  7.41 us
    pallas_call x2, Pallas kernels, unpack(): pl.pallas_call(body, in_specs=[pl.BlockSpec(memory_space=pl.ANY)], out_sp...  6.33 us
  transfers between devices with their start and end apart: 26, of which 9 were waited for; matrix products, arithmetic and copies ran while one was open for 0% of the time, Pallas kernels for 9%

profile of v2, /device:TPU:25, one launch (start us, length us, event | category | flops | bytes accessed | tf_op | source)
XLA Modules:
  0.0 266.6 jit_solution(423381187001200379)
XLA Ops:
  7.4 1.8 squeeze.30
  16.5 91.8 %all-gather.2.cloned.1.call-done.w = bf16[2560,2560]{1,0:T(8,128)(2,1)} async-done(((bf16[160,2560]{1,0:T(8,128)(2,1)}), bf16[2560,2560]{1,0:T(8,128)(2,1)}) %all-gather.2.cloned.1.call-update) | async-done | bytes 13107216 | tf_op jit(solution)/shard_map/weights/all_gather | solution.py:346
  108.3 2.9 %weights.3.w = bf16[2560,1280]{1,0:T(8,128)(2,1)S(1)} custom-call(bf16[2560,2560]{1,0:T(8,128)(2,1)} %all-gather.2.cloned.1.call-done.w), custom_call_target="tpu_custom_call" | custom-call | tf_op jit(solution)/shard_map/weights/pallas_call | solution.py:208
  114.6 2.9 %collective-permute-start.2 = (bf16[96,1280]{1,0:T(8,128)(2,1)S(1)}, bf16[96,1280]{1,0:T(8,128)(2,1)S(1)}, u32[]{:S(2)}, u32[]{:S(2)}) collective-permute-start(bf16[96,1280]{1,0:T(8,128)(2,1)S(1)} %get-tuple-element.32), channel_id=1, source_target_pairs={{0,2},{1,3},{2,4},{3,5},{4,6},{5,7},{8,10},{9,11},{10,12},{11,13},... | collective-permute-start | bytes 737288 | tf_op jit(solution)/shard_map/ppermute | solution.py:332
  117.6 4.6 %collective-permute-start.3 = (bf16[32,1280]{1,0:T(8,128)(2,1)S(1)}, bf16[32,1280]{1,0:T(8,128)(2,1)S(1)}, u32[]{:S(2)}, u32[]{:S(2)}) collective-permute-start(bf16[32,1280]{1,0:T(8,128)(2,1)S(1)} %slice.100), channel_id=1, source_target_pairs={{0,4},{1,5},{2,6},{3,7},{8,12},{9,13},{10,14},{11,15},{16,20},{17,... | collective-permute-start | bytes 245768 | tf_op jit(solution)/shard_map/ppermute | solution.py:332
  123.5 3.4 %weights.2 = (bf16[2560,640]{1,0:T(8,128)(2,1)S(1)}, bf16[1280,1280]{1,0:T(8,128)(2,1)S(1)}) custom-call(bf16[2560,2560]{1,0:T(8,128)(2,1)} %all-gather.2.cloned.1.call-done.w), custom_call_target="tpu_custom_call" | custom-call | tf_op jit(solution)/shard_map/weights/pallas_call | solution.py:208
  127.0 2.4 shard_map.48
  129.4 3.5 %shard_map.49.att_own = bf16[256,640]{1,0:T(8,128)(2,1)S(1)} custom-call(s32[42]{0:T(128)S(1)} %pad_add_fusion.scalars, bf16[256,640]{1,0:T(8,128)(2,1)S(1)} %get-tuple-element.29.query, f32[256,640]{1,0:T(8,128)S(1)} %get-tuple-element.30.acc, f32[256,128]{1,0:T(8,128)S(1)} %get-tuple-element.31.stat, bf16[96,1280]{1,0:T(8,128)(2,1)S(1)} %collective-permute-done.2.near, ...), custom_call_target="tpu_custom_call" | custom-call | flops 104857600 | bytes 1 | tf_op jit(solution)/shard_map/pallas_call | solution.py:222
  139.9 1.8 shard_map.53
  143.0 3.2 %collective-permute-start.9 = (bf16[32,1280]{1,0:T(8,128)(2,1)S(1)}, bf16[32,1280]{1,0:T(8,128)(2,1)S(1)}, u32[]{:S(2)}, u32[]{:S(2)}) collective-permute-start(bf16[32,1280]{1,0:T(8,128)(2,1)S(1)} %slice.101), channel_id=1, source_target_pairs={{0,4},{1,5},{2,6},{3,7},{8,12},{9,13},{10,14},{11,15},{16,20},{17,... | collective-permute-start | bytes 245768 | tf_op jit(solution)/shard_map/ppermute | solution.py:332
  147.5 2.4 shard_map.54
  150.0 3.5 %shard_map.55.att_own = bf16[256,640]{1,0:T(8,128)(2,1)S(1)} custom-call(s32[42]{0:T(128)S(1)} %pad_add_fusion.scalars, bf16[256,640]{1,0:T(8,128)(2,1)S(1)} %get-tuple-element.35.query, f32[256,640]{1,0:T(8,128)S(1)} %get-tuple-element.36.acc, f32[256,128]{1,0:T(8,128)S(1)} %get-tuple-element.37.stat, bf16[96,1280]{1,0:T(8,128)(2,1)S(1)} %collective-permute-done.8.near, ...), custom_call_target="tpu_custom_call" | custom-call | flops 104857600 | bytes 1 | tf_op jit(solution)/shard_map/pallas_call | solution.py:222
  160.0 1.8 shard_map.59
  161.8 2.8 %collective-permute-start.14 = (bf16[96,1280]{1,0:T(8,128)(2,1)S(1)}, bf16[96,1280]{1,0:T(8,128)(2,1)S(1)}, u32[]{:S(2)}, u32[]{:S(2)}) collective-permute-start(bf16[96,1280]{1,0:T(8,128)(2,1)S(1)} %get-tuple-element.43), channel_id=1, source_target_pairs={{0,2},{1,3},{2,4},{3,5},{4,6},{5,7},{8,10},{9,11},{10,12},{11,13},... | collective-permute-start | bytes 737288 | tf_op jit(solution)/shard_map/ppermute | solution.py:332
  164.6 5.0 %collective-permute-start.15 = (bf16[32,1280]{1,0:T(8,128)(2,1)S(1)}, bf16[32,1280]{1,0:T(8,128)(2,1)S(1)}, u32[]{:S(2)}, u32[]{:S(2)}) collective-permute-start(bf16[32,1280]{1,0:T(8,128)(2,1)S(1)} %slice.102), channel_id=1, source_target_pairs={{0,4},{1,5},{2,6},{3,7},{8,12},{9,13},{10,14},{11,15},{16,20},{17,... | collective-permute-start | bytes 245768 | tf_op jit(solution)/shard_map/ppermute | solution.py:332
  171.2 2.5 shard_map.60
  173.7 3.5 %shard_map.61.att_own = bf16[256,640]{1,0:T(8,128)(2,1)S(1)} custom-call(s32[42]{0:T(128)S(1)} %pad_add_fusion.scalars, bf16[256,640]{1,0:T(8,128)(2,1)S(1)} %get-tuple-element.40.query, f32[256,640]{1,0:T(8,128)S(1)} %get-tuple-element.41.acc, f32[256,128]{1,0:T(8,128)S(1)} %get-tuple-element.42.stat, bf16[96,1280]{1,0:T(8,128)(2,1)S(1)} %collective-permute-done.14.near, ...), custom_call_target="tpu_custom_call" | custom-call | flops 104857600 | bytes 1 | tf_op jit(solution)/shard_map/pallas_call | solution.py:222
  182.0 49.1 %collective-permute-done.18.own.x_own = bf16[256,1280]{1,0:T(8,128)(2,1)S(1)} collective-permute-done((bf16[256,1280]{1,0:T(8,128)(2,1)S(1)}, bf16[256,1280]{1,0:T(8,128)(2,1)S(1)}, u32[]{:S(2)}, u32[]{:S(2)}) %collective-permute-start.18) | collective-permute-done | bytes 655392 | tf_op jit(solution)/shard_map/ppermute | solution.py:415
  233.7 1.8 shard_map.65
  235.5 2.3 collective-permute-start.20
  237.8 5.4 %collective-permute-start.21 = (bf16[32,1280]{1,0:T(8,128)(2,1)S(1)}, bf16[32,1280]{1,0:T(8,128)(2,1)S(1)}, u32[]{:S(2)}, u32[]{:S(2)}) collective-permute-start(bf16[32,1280]{1,0:T(8,128)(2,1)S(1)} %slice.103), channel_id=1, source_target_pairs={{0,4},{1,5},{2,6},{3,7},{8,12},{9,13},{10,14},{11,15},{16,20},{17,... | collective-permute-start | bytes 245768 | tf_op jit(solution)/shard_map/ppermute | solution.py:332
  244.5 2.4 shard_map.66
  247.0 4.3 %shard_map.67.att_own = bf16[256,640]{1,0:T(8,128)(2,1)} custom-call(s32[42]{0:T(128)S(1)} %pad_add_fusion.scalars, bf16[256,640]{1,0:T(8,128)(2,1)S(1)} %get-tuple-element.45.query, f32[256,640]{1,0:T(8,128)S(1)} %get-tuple-element.46.acc, f32[256,128]{1,0:T(8,128)S(1)} %get-tuple-element.47.stat, bf16[96,1280]{1,0:T(8,128)(2,1)S(1)} %collective-permute-done.20.near, ...), custom_call_target="tpu_custom_call" | custom-call | flops 104857600 | bytes 1 | tf_op jit(solution)/shard_map/pallas_call | solution.py:222
  255.0 1.8 shard_map.69
  (117 shorter events, 45.3 us)
Async XLA Ops:
  6.5 101.8 %all-gather.2.cloned.1.call-start = ((), (), s32[]{:S(2)}) async-start(), calls=%async_computation | async-start | bytes 13926400 | tf_op jit(solution)/shard_map/weights/all_gather | solution.py:346
  10.3 2.1 collective-permute-start.1
  14.0 2.1 collective-permute-start
  114.6 14.8 %collective-permute-start.2 = (bf16[96,1280]{1,0:T(8,128)(2,1)S(1)}, bf16[96,1280]{1,0:T(8,128)(2,1)S(1)}, u32[]{:S(2)}, u32[]{:S(2)}) collective-permute-start(bf16[96,1280]{1,0:T(8,128)(2,1)S(1)} %get-tuple-element.32), channel_id=1, source_target_pairs={{0,2},{1,3},{2,4},{3,5},{4,6},{5,7},{8,10},{9,11},{10,12},{11,13},... | collective-permute-start | bytes 737288 | tf_op jit(solution)/shard_map/ppermute | solution.py:332
  117.6 11.8 %collective-permute-start.3 = (bf16[32,1280]{1,0:T(8,128)(2,1)S(1)}, bf16[32,1280]{1,0:T(8,128)(2,1)S(1)}, u32[]{:S(2)}, u32[]{:S(2)}) collective-permute-start(bf16[32,1280]{1,0:T(8,128)(2,1)S(1)} %slice.100), channel_id=1, source_target_pairs={{0,4},{1,5},{2,6},{3,7},{8,12},{9,13},{10,14},{11,15},{16,20},{17,... | collective-permute-start | bytes 245768 | tf_op jit(solution)/shard_map/ppermute | solution.py:332
  122.2 7.2 %collective-permute-start.4 = (bf16[32,1280]{1,0:T(8,128)(2,1)S(1)}, bf16[32,1280]{1,0:T(8,128)(2,1)S(1)}, u32[]{:S(2)}, u32[]{:S(2)}) collective-permute-start(bf16[32,1280]{1,0:T(8,128)(2,1)S(1)} %slice.100), channel_id=1, source_target_pairs={{0,6},{1,7},{8,14},{9,15},{16,22},{17,23},{24,30},{25,31},{32,38},... | collective-permute-start | bytes 245768 | tf_op jit(solution)/shard_map/ppermute | solution.py:332
  133.0 2.6 collective-permute-start.5
  137.5 2.4 collective-permute-start.7
  141.7 8.3 %collective-permute-start.8 = (bf16[96,1280]{1,0:T(8,128)(2,1)S(1)}, bf16[96,1280]{1,0:T(8,128)(2,1)S(1)}, u32[]{:S(2)}, u32[]{:S(2)}) collective-permute-start(bf16[96,1280]{1,0:T(8,128)(2,1)S(1)} %get-tuple-element.38), channel_id=1, source_target_pairs={{0,2},{1,3},{2,4},{3,5},{4,6},{5,7},{8,10},{9,11},{10,12},{11,13},... | collective-permute-start | bytes 737288 | tf_op jit(solution)/shard_map/ppermute | solution.py:332
  143.0 7.0 %collective-permute-start.9 = (bf16[32,1280]{1,0:T(8,128)(2,1)S(1)}, bf16[32,1280]{1,0:T(8,128)(2,1)S(1)}, u32[]{:S(2)}, u32[]{:S(2)}) collective-permute-start(bf16[32,1280]{1,0:T(8,128)(2,1)S(1)} %slice.101), channel_id=1, source_target_pairs={{0,4},{1,5},{2,6},{3,7},{8,12},{9,13},{10,14},{11,15},{16,20},{17,... | collective-permute-start | bytes 245768 | tf_op jit(solution)/shard_map/ppermute | solution.py:332
  146.2 3.8 %collective-permute-start.10 = (bf16[32,1280]{1,0:T(8,128)(2,1)S(1)}, bf16[32,1280]{1,0:T(8,128)(2,1)S(1)}, u32[]{:S(2)}, u32[]{:S(2)}) collective-permute-start(bf16[32,1280]{1,0:T(8,128)(2,1)S(1)} %slice.101), channel_id=1, source_target_pairs={{0,6},{1,7},{8,14},{9,15},{16,22},{17,23},{24,30},{25,31},{32,38},... | collective-permute-start | bytes 245768 | tf_op jit(solution)/shard_map/ppermute | solution.py:332
  153.6 2.2 collective-permute-start.11
  157.8 2.2 collective-permute-start.13
  161.8 11.9 %collective-permute-start.14 = (bf16[96,1280]{1,0:T(8,128)(2,1)S(1)}, bf16[96,1280]{1,0:T(8,128)(2,1)S(1)}, u32[]{:S(2)}, u32[]{:S(2)}) collective-permute-start(bf16[96,1280]{1,0:T(8,128)(2,1)S(1)} %get-tuple-element.43), channel_id=1, source_target_pairs={{0,2},{1,3},{2,4},{3,5},{4,6},{5,7},{8,10},{9,11},{10,12},{11,13},... | collective-permute-start | bytes 737288 | tf_op jit(solution)/shard_map/ppermute | solution.py:332
  164.6 9.0 %collective-permute-start.15 = (bf16[32,1280]{1,0:T(8,128)(2,1)S(1)}, bf16[32,1280]{1,0:T(8,128)(2,1)S(1)}, u32[]{:S(2)}, u32[]{:S(2)}) collective-permute-start(bf16[32,1280]{1,0:T(8,128)(2,1)S(1)} %slice.102), channel_id=1, source_target_pairs={{0,4},{1,5},{2,6},{3,7},{8,12},{9,13},{10,14},{11,15},{16,20},{17,... | collective-permute-start | bytes 245768 | tf_op jit(solution)/shard_map/ppermute | solution.py:332
  169.6 4.0 %collective-permute-start.16 = (bf16[32,1280]{1,0:T(8,128)(2,1)S(1)}, bf16[32,1280]{1,0:T(8,128)(2,1)S(1)}, u32[]{:S(2)}, u32[]{:S(2)}) collective-permute-start(bf16[32,1280]{1,0:T(8,128)(2,1)S(1)} %slice.102), channel_id=1, source_target_pairs={{0,6},{1,7},{8,14},{9,15},{16,22},{17,23},{24,30},{25,31},{32,38},... | collective-permute-start | bytes 245768 | tf_op jit(solution)/shard_map/ppermute | solution.py:332
  177.2 2.3 collective-permute-start.17
  180.7 50.4 %collective-permute-start.18 = (bf16[256,1280]{1,0:T(8,128)(2,1)S(1)}, bf16[256,1280]{1,0:T(8,128)(2,1)S(1)}, u32[]{:S(2)}, u32[]{:S(2)}) collective-permute-start(bf16[256,1280]{1,0:T(8,128)(2,1)S(1)} %shard_map.63), channel_id=1, source_target_pairs={{64,96},{65,97},{66,98},{67,99},{68,100},{69,101},{70,102},{71,103... | collective-permute-start | bytes 1966088 | tf_op jit(solution)/shard_map/ppermute | solution.py:415
  231.1 2.6 collective-permute-start.19
  235.5 11.5 %collective-permute-start.20 = (bf16[96,1280]{1,0:T(8,128)(2,1)S(1)}, bf16[96,1280]{1,0:T(8,128)(2,1)S(1)}, u32[]{:S(2)}, u32[]{:S(2)}) collective-permute-start(bf16[96,1280]{1,0:T(8,128)(2,1)S(1)} %get-tuple-element.48), channel_id=1, source_target_pairs={{0,2},{1,3},{2,4},{3,5},{4,6},{5,7},{8,10},{9,11},{10,12},{11,13},... | collective-permute-start | bytes 737288 | tf_op jit(solution)/shard_map/ppermute | solution.py:332
  237.8 9.1 %collective-permute-start.21 = (bf16[32,1280]{1,0:T(8,128)(2,1)S(1)}, bf16[32,1280]{1,0:T(8,128)(2,1)S(1)}, u32[]{:S(2)}, u32[]{:S(2)}) collective-permute-start(bf16[32,1280]{1,0:T(8,128)(2,1)S(1)} %slice.103), channel_id=1, source_target_pairs={{0,4},{1,5},{2,6},{3,7},{8,12},{9,13},{10,14},{11,15},{16,20},{17,... | collective-permute-start | bytes 245768 | tf_op jit(solution)/shard_map/ppermute | solution.py:332
  243.2 3.8 %collective-permute-start.22 = (bf16[32,1280]{1,0:T(8,128)(2,1)S(1)}, bf16[32,1280]{1,0:T(8,128)(2,1)S(1)}, u32[]{:S(2)}, u32[]{:S(2)}) collective-permute-start(bf16[32,1280]{1,0:T(8,128)(2,1)S(1)} %slice.103), channel_id=1, source_target_pairs={{0,6},{1,7},{8,14},{9,15},{16,22},{17,23},{24,30},{25,31},{32,38},... | collective-permute-start | bytes 245768 | tf_op jit(solution)/shard_map/ppermute | solution.py:332
  251.3 3.7 %collective-permute-start.23 = (bf16[256,640]{1,0:T(8,128)(2,1)}, bf16[256,640]{1,0:T(8,128)(2,1)}, u32[]{:S(2)}, u32[]{:S(2)}) collective-permute-start(bf16[256,640]{1,0:T(8,128)(2,1)} %shard_map.67.att_own), channel_id=1, source_target_pairs={{0,1},{1,0},{2,3},{3,2},{4,5},{5,4},{6,7},{7,6},{8,9},{9,8},{10,11... | collective-permute-start | bytes 983048 | tf_op jit(solution)/shard_map/ppermute | solution.py:323
  257.0 1.7 collective-permute-start.24
  (16 other events, 241.4 us)
Sparse Core Ops, SparseCore 0:
  13.8 94.5 all-gather.1

commit v3 on v2

--- a/solution.py
+++ b/solution.py
@@ -15,6 +15,7 @@
 F32 = jnp.float32
 VMEM_LIMIT = 20 * 1024 * 1024
 UNPACK_LIMIT = 46 * 1024 * 1024
+PACK_LIMIT = 60 * 1024 * 1024
 
 
 def dot(a, b):
@@ -51,6 +52,10 @@
         pick = jnp.where(col == source, 1.0, 0.0).astype(BF16)
         cols = slice(2 * i * HD, 2 * (i + 1) * HD)
         send_out[:, cols] = dot(pick, kv_out[:, cols]).astype(BF16)
+
+
+def with_ones(values):
+    return jnp.concatenate([values, jnp.ones_like(values)], axis=1)
 
 
 def local_kernel(scalars, own, other, w, kv, q_out, acc_out, stat_out):
@@ -103,12 +108,10 @@
         rows = slice(128 * r, 128 * (r + 1))
         seen = slice(0, 128 * (r + 1))
         vals = slice((2 * i + 1) * HD, (2 * i + 2) * HD)
-        acc_out[rows, i * HD : (i + 1) * HD] = dot(expos[i, r].astype(BF16), kv[seen, vals])
-    for i, r in work:
-        total = jnp.sum(expos[i, r], axis=1, keepdims=True)
-        stats[r] = jnp.where(
-            lane_half == i, peaks[i, r], jnp.where(lane_half == heads + i, total, stats[r])
-        )
+        acc_out[rows, 2 * i * HD : 2 * (i + 1) * HD] = dot(
+            expos[i, r].astype(BF16), with_ones(kv[seen, vals])
+        )
+        stats[r] = jnp.where(lane_half == i, peaks[i, r], stats[r])
     stat_out[:128] = stats[0]
     stat_out[128:] = stats[1]
 
@@ -140,14 +143,11 @@
     for i in range(heads):
         vals = slice((2 * i + 1) * HD, (2 * i + 2) * HD)
         value_rows = jnp.concatenate([near[:, vals], mid[:, vals], far[:, vals]], axis=0)
-        mixed.append(dot(expos[i].astype(BF16), value_rows))
-    for i in range(heads):
-        cols = slice(i * HD, (i + 1) * HD)
+        mixed.append(dot(expos[i].astype(BF16), with_ones(value_rows)))
+    for i in range(heads):
         shrink = jnp.exp(stat[:, i : i + 1] - peaks[i])
-        total = stat[:, heads + i : heads + i + 1] * shrink
-        total = total + jnp.sum(expos[i], axis=1, keepdims=True)
-        inverse = 1.0 / total
-        out[:, cols] = (acc[:, cols] * (shrink * inverse) + mixed[i] * inverse).astype(BF16)
+        both = acc[:, 2 * i * HD : 2 * (i + 1) * HD] * shrink + mixed[i]
+        out[:, i * HD : (i + 1) * HD] = (both[:, :HD] / both[:, HD:]).astype(BF16)
 
 
 def back_early_kernel(scalars, x_own, att_own, w, acc):
@@ -156,6 +156,49 @@
 
 def back_kernel(scalars, acc, att_other, w, out):
     out[...] = (acc[...] + dot(att_other[...], rows_of(1 - scalars[0], w))).astype(BF16)
+
+
+def pack_kernel(core_ref, w_qkv_hbm, w_out_hbm, own, other, w_qkv, w_out, sems):
+    copies = [
+        pltpu.make_async_copy(w_qkv_hbm, w_qkv, sems.at[0]),
+        pltpu.make_async_copy(w_out_hbm, w_out, sems.at[1]),
+    ]
+    for copy in copies:
+        copy.start()
+    third = w_qkv.shape[2] // 3
+    width = third // 2
+    cut = w_out.shape[2] // 2
+
+    def columns(ref, start, size):
+        return ref[0, :, pl.ds(pl.multiple_of(start, 128), size)]
+
+    targets = ((own, core_ref[0]), (other, 1 - core_ref[0]))
+    copies[0].wait()
+    for target, core in targets:
+        for i in range(width // HD):
+            start = third + core * width + i * HD
+            target[:, 2 * i * HD : (2 * i + 1) * HD] = columns(w_qkv, start, HD)
+            target[:, (2 * i + 1) * HD : (2 * i + 2) * HD] = columns(w_qkv, start + third, HD)
+        target[:, 2 * width : 3 * width] = columns(w_qkv, core * width, width)
+    copies[1].wait()
+    for target, core in targets:
+        left = columns(w_out, core * cut, width).astype(F32)
+        right = columns(w_out, core * cut + width, width).astype(F32)
+        target[:, 3 * width :] = jnp.concatenate([left, right], axis=0).astype(BF16)
+
+
+def join_kernel(core_ref, own, other, block):
+    rows = own.shape[0]
+    wide = block.shape[1] * 3 // 4
+    core = core_ref[0]
+    block[pl.ds(pl.multiple_of(core * rows, 16), rows), :wide] = own[:, :wide]
+    block[pl.ds(pl.multiple_of((1 - core) * rows, 16), rows), :wide] = other[:, :wide]
+    mine, theirs = own[:, wide:].astype(F32), other[:, wide:].astype(F32)
+    first = jnp.where(core == 0, mine, theirs)
+    second = jnp.where(core == 0, theirs, mine)
+    half = rows // 2
+    parts = [first[:half], second[:half], first[half:], second[half:]]
+    block[:, wide:] = jnp.concatenate(parts, axis=0).astype(BF16)
 
 
 def unpack_kv_kernel(w, out, sems):
@@ -229,6 +272,28 @@
     )(scalars, *operands)
 
 
+def pack_weights(core, w_qkv, w_out):
+    shape = (w_qkv.shape[1], w_qkv.shape[2] * 2 // 3)
+    return pl.pallas_call(
+        pack_kernel,
+        in_specs=[pl.BlockSpec(memory_space=pltpu.SMEM)]
+        + [pl.BlockSpec(memory_space=pl.ANY)] * 2,
+        out_specs=[pl.BlockSpec(memory_space=pltpu.VMEM)] * 2,
+        out_shape=[jax.ShapeDtypeStruct(shape, BF16)] * 2,
+        scratch_shapes=[
+            pltpu.VMEM(w_qkv.shape, BF16),
+            pltpu.VMEM(w_out.shape, BF16),
+            pltpu.SemaphoreType.DMA((2,)),
+        ],
+        compiler_params=pltpu.CompilerParams(vmem_limit_bytes=PACK_LIMIT),
+    )(core, w_qkv, w_out)
+
+
+def join_weights(core, own, other):
+    shape = (2 * own.shape[0], own.shape[1])
+    return call(join_kernel, jax.ShapeDtypeStruct(shape, BF16), 1, core, own, other)
+
+
 def project_early(scalars, own, w):
     rows, size = own.shape
     return call(
@@ -264,7 +329,7 @@
         local_kernel,
         [
             jax.ShapeDtypeStruct((rows, width), BF16),
-            jax.ShapeDtypeStruct((rows, width), F32),
+            jax.ShapeDtypeStruct((rows, 2 * width), F32),
             jax.ShapeDtypeStruct((rows, HD), F32),
         ],
         4 * rows * (own.shape[1] + 2 * HD) * width,
@@ -360,27 +425,10 @@
     with jax.named_scope("weights"):
         rows = w_qkv.shape[1]
         width = w_qkv.shape[2] // 6
-        heads = width // HD
         cut = w_out.shape[2] // 2
-        parts = w_qkv[0].reshape(rows, 3, 2, heads, HD)
-
-        def half_of(h):
-            kv = jnp.stack([parts[:, 1, h], parts[:, 2, h]], axis=2).reshape(rows, 2 * width)
-            query = parts[:, 0, h].reshape(rows, width)
-            back = w_out[0][:, h * cut : (h + 1) * cut]
-            back = jnp.concatenate([back[:, :width], back[:, width:]], axis=0)
-            return jnp.concatenate([kv, query, back], axis=1)
-
-        halves = [half_of(0), half_of(1)]
-        own = jnp.where(core == 0, halves[0], halves[1])
-        other = swap(jnp.where(core == 0, halves[1], halves[0]))
-        block = in_order(core, own[:, : 3 * width], other[:, : 3 * width], 0)
-        back = [
-            in_order(core, own[at, 3 * width :], other[at, 3 * width :], 0)
-            for at in (slice(0, rows // 2), slice(rows // 2, rows))
-        ]
-        block = jnp.concatenate([block, jnp.concatenate(back, axis=0)], axis=1)
-        w_all = gather_chips(block)
+        core_array = jnp.full((1,), core, jnp.int32)
+        own, other = pack_weights(core_array, w_qkv, w_out)
+        w_all = gather_chips(join_weights(core_array, own, swap(other)))
         depth = w_all.shape[0]
         w_kv = unpack(
             unpack_kv_kernel, w_all, jax.ShapeDtypeStruct((depth, 2 * width), BF16), [8]

time: 267 us -> 261 us (0.978)
  local copies, waits for them, and re-layouts: 5.16 us -> 2.26 us
    pallas_call x24 -> x25, Pallas kernels: 49 us -> 45 us  [call(): pl.pallas_call(body, in_specs=in_specs, out_specs=out_specs, out_shape=ou...]
  transfers between devices with their start and end apart: 26 -> 26, of which waited for: 9 -> 8; matrix products, arithmetic and copies ran while one was open for 0% -> 0% of each run, Pallas kernels for 9% -> 9%
where the time goes in v3:
time: 261 us
  waiting for transfers between devices  147 us (56%)
  Pallas kernels  53.5 us (20%)
  starting transfers between devices  42.8 us (16%)
  between operations  14.1 us (5%)
    all_gather x1, waiting for transfers between devices, gather_chips(): lax.all_gather(block, 'seq', axis=0, tiled=True, axis_index_groups=groups)  92.1 us
    ppermute x3, waiting for transfers between devices, local(): x_own = lax.ppermute(produced, 'section', [(tick, tick + 1)])  49.3 us
    pallas_call x25, Pallas kernels, call(): pl.pallas_call(body, in_specs=in_specs, out_specs=out_specs, out_shape=ou...  45 us
    ppermute x12, starting transfers between devices, to_later_chip(): return lax.ppermute(value, 'seq', pairs)  32.7 us
    ppermute x10, starting transfers between devices, swap(): return lax.ppermute(value, 'seq', [(i, i ^ 1) for i in range(count)])  7.37 us
    pallas_call x2, Pallas kernels, unpack(): pl.pallas_call(body, in_specs=[pl.BlockSpec(memory_space=pl.ANY)], out_sp...  6.37 us
    ppermute x10, waiting for transfers between devices, swap(): return lax.ppermute(value, 'seq', [(i, i ^ 1) for i in range(count)])  5.25 us
  transfers between devices with their start and end apart: 26, of which 8 were waited for; matrix products, arithmetic and copies ran while one was open for 0% of the time, Pallas kernels for 9%

profile of v3, /device:TPU:25, one launch (start us, length us, event | category | flops | bytes accessed | tf_op | source)
XLA Modules:
  0.0 260.9 jit_solution(1398749992707674409)
XLA Ops:
  6.5 2.2 weights.4
  15.6 92.1 %all-gather.2.cloned.1.call-done.w = bf16[2560,2560]{1,0:T(8,128)(2,1)} async-done(((bf16[160,2560]{1,0:T(8,128)(2,1)}), bf16[2560,2560]{1,0:T(8,128)(2,1)}) %all-gather.2.cloned.1.call-update) | async-done | bytes 13107216 | tf_op jit(solution)/shard_map/weights/all_gather | solution.py:411
  107.7 3.0 %weights.7.w = bf16[2560,1280]{1,0:T(8,128)(2,1)S(1)} custom-call(bf16[2560,2560]{1,0:T(8,128)(2,1)} %all-gather.2.cloned.1.call-done.w), custom_call_target="tpu_custom_call" | custom-call | tf_op jit(solution)/shard_map/weights/pallas_call | solution.py:251
  114.1 2.9 %collective-permute-start.2 = (bf16[96,1280]{1,0:T(8,128)(2,1)S(1)}, bf16[96,1280]{1,0:T(8,128)(2,1)S(1)}, u32[]{:S(2)}, u32[]{:S(2)}) collective-permute-start(bf16[96,1280]{1,0:T(8,128)(2,1)S(1)} %get-tuple-element.36), channel_id=1, source_target_pairs={{0,2},{1,3},{2,4},{3,5},{4,6},{5,7},{8,10},{9,11},{10,12},{11,13},... | collective-permute-start | bytes 737288 | tf_op jit(solution)/shard_map/ppermute | solution.py:397
  117.1 4.6 %collective-permute-start.3 = (bf16[32,1280]{1,0:T(8,128)(2,1)S(1)}, bf16[32,1280]{1,0:T(8,128)(2,1)S(1)}, u32[]{:S(2)}, u32[]{:S(2)}) collective-permute-start(bf16[32,1280]{1,0:T(8,128)(2,1)S(1)} %slice.30), channel_id=1, source_target_pairs={{0,4},{1,5},{2,6},{3,7},{8,12},{9,13},{10,14},{11,15},{16,20},{17,... | collective-permute-start | bytes 245768 | tf_op jit(solution)/shard_map/ppermute | solution.py:397
  123.0 3.4 %weights.6 = (bf16[2560,640]{1,0:T(8,128)(2,1)S(1)}, bf16[1280,1280]{1,0:T(8,128)(2,1)S(1)}) custom-call(bf16[2560,2560]{1,0:T(8,128)(2,1)} %all-gather.2.cloned.1.call-done.w), custom_call_target="tpu_custom_call" | custom-call | tf_op jit(solution)/shard_map/weights/pallas_call | solution.py:251
  126.4 2.5 shard_map.48
  128.9 2.2 shard_map.49.att_own
  137.9 1.8 shard_map.53
  141.0 3.1 %collective-permute-start.9 = (bf16[32,1280]{1,0:T(8,128)(2,1)S(1)}, bf16[32,1280]{1,0:T(8,128)(2,1)S(1)}, u32[]{:S(2)}, u32[]{:S(2)}) collective-permute-start(bf16[32,1280]{1,0:T(8,128)(2,1)S(1)} %slice.31), channel_id=1, source_target_pairs={{0,4},{1,5},{2,6},{3,7},{8,12},{9,13},{10,14},{11,15},{16,20},{17,... | collective-permute-start | bytes 245768 | tf_op jit(solution)/shard_map/ppermute | solution.py:397
  145.6 2.5 shard_map.54
  148.2 2.2 shard_map.55.att_own
  156.9 1.8 shard_map.59
  158.6 2.7 %collective-permute-start.14 = (bf16[96,1280]{1,0:T(8,128)(2,1)S(1)}, bf16[96,1280]{1,0:T(8,128)(2,1)S(1)}, u32[]{:S(2)}, u32[]{:S(2)}) collective-permute-start(bf16[96,1280]{1,0:T(8,128)(2,1)S(1)} %get-tuple-element.47), channel_id=1, source_target_pairs={{0,2},{1,3},{2,4},{3,5},{4,6},{5,7},{8,10},{9,11},{10,12},{11,13},... | collective-permute-start | bytes 737288 | tf_op jit(solution)/shard_map/ppermute | solution.py:397
  161.3 5.0 %collective-permute-start.15 = (bf16[32,1280]{1,0:T(8,128)(2,1)S(1)}, bf16[32,1280]{1,0:T(8,128)(2,1)S(1)}, u32[]{:S(2)}, u32[]{:S(2)}) collective-permute-start(bf16[32,1280]{1,0:T(8,128)(2,1)S(1)} %slice.32), channel_id=1, source_target_pairs={{0,4},{1,5},{2,6},{3,7},{8,12},{9,13},{10,14},{11,15},{16,20},{17,... | collective-permute-start | bytes 245768 | tf_op jit(solution)/shard_map/ppermute | solution.py:397
  167.6 2.5 shard_map.60
  170.2 2.2 shard_map.61.att_own
  177.2 49.3 %collective-permute-done.18.own.x_own = bf16[256,1280]{1,0:T(8,128)(2,1)S(1)} collective-permute-done((bf16[256,1280]{1,0:T(8,128)(2,1)S(1)}, bf16[256,1280]{1,0:T(8,128)(2,1)S(1)}, u32[]{:S(2)}, u32[]{:S(2)}) %collective-permute-start.18) | collective-permute-done | bytes 655392 | tf_op jit(solution)/shard_map/ppermute | solution.py:463
  229.1 1.8 shard_map.65
  230.9 2.5 collective-permute-start.20
  233.4 5.3 %collective-permute-start.21 = (bf16[32,1280]{1,0:T(8,128)(2,1)S(1)}, bf16[32,1280]{1,0:T(8,128)(2,1)S(1)}, u32[]{:S(2)}, u32[]{:S(2)}) collective-permute-start(bf16[32,1280]{1,0:T(8,128)(2,1)S(1)} %slice.33), channel_id=1, source_target_pairs={{0,4},{1,5},{2,6},{3,7},{8,12},{9,13},{10,14},{11,15},{16,20},{17,... | collective-permute-start | bytes 245768 | tf_op jit(solution)/shard_map/ppermute | solution.py:397
  240.0 2.5 shard_map.66
  242.6 3.0 %shard_map.67.att_own = bf16[256,640]{1,0:T(8,128)(2,1)} custom-call(s32[42]{0:T(128)S(1)} %pad_add_fusion.scalars, bf16[256,640]{1,0:T(8,128)(2,1)S(1)} %get-tuple-element.49.query, f32[256,1280]{1,0:T(8,128)S(1)} %get-tuple-element.50.acc, f32[256,128]{1,0:T(8,128)S(1)} %get-tuple-element.51.stat, bf16[96,1280]{1,0:T(8,128)(2,1)S(1)} %collective-permute-done.20.near, ...), custom_call_target="tpu_custom_call" | custom-call | flops 104857600 | bytes 1 | tf_op jit(solution)/shard_map/pallas_call | solution.py:265
  249.3 1.8 shard_map.69
  (98 shorter events, 44.0 us)
Async XLA Ops:
  6.5 101.2 %all-gather.2.cloned.1.call-start = ((), (), s32[]{:S(2)}) async-start(), calls=%async_computation | async-start | bytes 13926400 | tf_op jit(solution)/shard_map/weights/all_gather | solution.py:411
  8.7 2.3 collective-permute-start.1
  13.1 2.2 collective-permute-start
  114.1 14.8 %collective-permute-start.2 = (bf16[96,1280]{1,0:T(8,128)(2,1)S(1)}, bf16[96,1280]{1,0:T(8,128)(2,1)S(1)}, u32[]{:S(2)}, u32[]{:S(2)}) collective-permute-start(bf16[96,1280]{1,0:T(8,128)(2,1)S(1)} %get-tuple-element.36), channel_id=1, source_target_pairs={{0,2},{1,3},{2,4},{3,5},{4,6},{5,7},{8,10},{9,11},{10,12},{11,13},... | collective-permute-start | bytes 737288 | tf_op jit(solution)/shard_map/ppermute | solution.py:397
  117.1 11.8 %collective-permute-start.3 = (bf16[32,1280]{1,0:T(8,128)(2,1)S(1)}, bf16[32,1280]{1,0:T(8,128)(2,1)S(1)}, u32[]{:S(2)}, u32[]{:S(2)}) collective-permute-start(bf16[32,1280]{1,0:T(8,128)(2,1)S(1)} %slice.30), channel_id=1, source_target_pairs={{0,4},{1,5},{2,6},{3,7},{8,12},{9,13},{10,14},{11,15},{16,20},{17,... | collective-permute-start | bytes 245768 | tf_op jit(solution)/shard_map/ppermute | solution.py:397
  121.7 7.2 %collective-permute-start.4 = (bf16[32,1280]{1,0:T(8,128)(2,1)S(1)}, bf16[32,1280]{1,0:T(8,128)(2,1)S(1)}, u32[]{:S(2)}, u32[]{:S(2)}) collective-permute-start(bf16[32,1280]{1,0:T(8,128)(2,1)S(1)} %slice.30), channel_id=1, source_target_pairs={{0,6},{1,7},{8,14},{9,15},{16,22},{17,23},{24,30},{25,31},{32,38},... | collective-permute-start | bytes 245768 | tf_op jit(solution)/shard_map/ppermute | solution.py:397
  131.2 2.6 collective-permute-start.5
  135.7 2.2 collective-permute-start.7
  139.7 8.5 %collective-permute-start.8 = (bf16[96,1280]{1,0:T(8,128)(2,1)S(1)}, bf16[96,1280]{1,0:T(8,128)(2,1)S(1)}, u32[]{:S(2)}, u32[]{:S(2)}) collective-permute-start(bf16[96,1280]{1,0:T(8,128)(2,1)S(1)} %get-tuple-element.42), channel_id=1, source_target_pairs={{0,2},{1,3},{2,4},{3,5},{4,6},{5,7},{8,10},{9,11},{10,12},{11,13},... | collective-permute-start | bytes 737288 | tf_op jit(solution)/shard_map/ppermute | solution.py:397
  141.0 7.1 %collective-permute-start.9 = (bf16[32,1280]{1,0:T(8,128)(2,1)S(1)}, bf16[32,1280]{1,0:T(8,128)(2,1)S(1)}, u32[]{:S(2)}, u32[]{:S(2)}) collective-permute-start(bf16[32,1280]{1,0:T(8,128)(2,1)S(1)} %slice.31), channel_id=1, source_target_pairs={{0,4},{1,5},{2,6},{3,7},{8,12},{9,13},{10,14},{11,15},{16,20},{17,... | collective-permute-start | bytes 245768 | tf_op jit(solution)/shard_map/ppermute | solution.py:397
  144.1 4.0 %collective-permute-start.10 = (bf16[32,1280]{1,0:T(8,128)(2,1)S(1)}, bf16[32,1280]{1,0:T(8,128)(2,1)S(1)}, u32[]{:S(2)}, u32[]{:S(2)}) collective-permute-start(bf16[32,1280]{1,0:T(8,128)(2,1)S(1)} %slice.31), channel_id=1, source_target_pairs={{0,6},{1,7},{8,14},{9,15},{16,22},{17,23},{24,30},{25,31},{32,38},... | collective-permute-start | bytes 245768 | tf_op jit(solution)/shard_map/ppermute | solution.py:397
  150.4 2.3 collective-permute-start.11
  154.7 2.2 collective-permute-start.13
  158.6 11.5 %collective-permute-start.14 = (bf16[96,1280]{1,0:T(8,128)(2,1)S(1)}, bf16[96,1280]{1,0:T(8,128)(2,1)S(1)}, u32[]{:S(2)}, u32[]{:S(2)}) collective-permute-start(bf16[96,1280]{1,0:T(8,128)(2,1)S(1)} %get-tuple-element.47), channel_id=1, source_target_pairs={{0,2},{1,3},{2,4},{3,5},{4,6},{5,7},{8,10},{9,11},{10,12},{11,13},... | collective-permute-start | bytes 737288 | tf_op jit(solution)/shard_map/ppermute | solution.py:397
  161.3 8.8 %collective-permute-start.15 = (bf16[32,1280]{1,0:T(8,128)(2,1)S(1)}, bf16[32,1280]{1,0:T(8,128)(2,1)S(1)}, u32[]{:S(2)}, u32[]{:S(2)}) collective-permute-start(bf16[32,1280]{1,0:T(8,128)(2,1)S(1)} %slice.32), channel_id=1, source_target_pairs={{0,4},{1,5},{2,6},{3,7},{8,12},{9,13},{10,14},{11,15},{16,20},{17,... | collective-permute-start | bytes 245768 | tf_op jit(solution)/shard_map/ppermute | solution.py:397
  166.3 3.8 %collective-permute-start.16 = (bf16[32,1280]{1,0:T(8,128)(2,1)S(1)}, bf16[32,1280]{1,0:T(8,128)(2,1)S(1)}, u32[]{:S(2)}, u32[]{:S(2)}) collective-permute-start(bf16[32,1280]{1,0:T(8,128)(2,1)S(1)} %slice.32), channel_id=1, source_target_pairs={{0,6},{1,7},{8,14},{9,15},{16,22},{17,23},{24,30},{25,31},{32,38},... | collective-permute-start | bytes 245768 | tf_op jit(solution)/shard_map/ppermute | solution.py:397
  172.4 2.3 collective-permute-start.17
  175.9 50.6 %collective-permute-start.18 = (bf16[256,1280]{1,0:T(8,128)(2,1)S(1)}, bf16[256,1280]{1,0:T(8,128)(2,1)S(1)}, u32[]{:S(2)}, u32[]{:S(2)}) collective-permute-start(bf16[256,1280]{1,0:T(8,128)(2,1)S(1)} %shard_map.63), channel_id=1, source_target_pairs={{64,96},{65,97},{66,98},{67,99},{68,100},{69,101},{70,102},{71,103... | collective-permute-start | bytes 1966088 | tf_op jit(solution)/shard_map/ppermute | solution.py:463
  226.5 2.6 collective-permute-start.19
  230.9 11.7 %collective-permute-start.20 = (bf16[96,1280]{1,0:T(8,128)(2,1)S(1)}, bf16[96,1280]{1,0:T(8,128)(2,1)S(1)}, u32[]{:S(2)}, u32[]{:S(2)}) collective-permute-start(bf16[96,1280]{1,0:T(8,128)(2,1)S(1)} %get-tuple-element.52), channel_id=1, source_target_pairs={{0,2},{1,3},{2,4},{3,5},{4,6},{5,7},{8,10},{9,11},{10,12},{11,13},... | collective-permute-start | bytes 737288 | tf_op jit(solution)/shard_map/ppermute | solution.py:397
  233.4 9.1 %collective-permute-start.21 = (bf16[32,1280]{1,0:T(8,128)(2,1)S(1)}, bf16[32,1280]{1,0:T(8,128)(2,1)S(1)}, u32[]{:S(2)}, u32[]{:S(2)}) collective-permute-start(bf16[32,1280]{1,0:T(8,128)(2,1)S(1)} %slice.33), channel_id=1, source_target_pairs={{0,4},{1,5},{2,6},{3,7},{8,12},{9,13},{10,14},{11,15},{16,20},{17,... | collective-permute-start | bytes 245768 | tf_op jit(solution)/shard_map/ppermute | solution.py:397
  238.7 3.8 %collective-permute-start.22 = (bf16[32,1280]{1,0:T(8,128)(2,1)S(1)}, bf16[32,1280]{1,0:T(8,128)(2,1)S(1)}, u32[]{:S(2)}, u32[]{:S(2)}) collective-permute-start(bf16[32,1280]{1,0:T(8,128)(2,1)S(1)} %slice.33), channel_id=1, source_target_pairs={{0,6},{1,7},{8,14},{9,15},{16,22},{17,23},{24,30},{25,31},{32,38},... | collective-permute-start | bytes 245768 | tf_op jit(solution)/shard_map/ppermute | solution.py:397
  245.5 3.7 %collective-permute-start.23 = (bf16[256,640]{1,0:T(8,128)(2,1)}, bf16[256,640]{1,0:T(8,128)(2,1)}, u32[]{:S(2)}, u32[]{:S(2)}) collective-permute-start(bf16[256,640]{1,0:T(8,128)(2,1)} %shard_map.67.att_own), channel_id=1, source_target_pairs={{0,1},{1,0},{2,3},{3,2},{4,5},{5,4},{6,7},{7,6},{8,9},{9,8},{10,11... | collective-permute-start | bytes 983048 | tf_op jit(solution)/shard_map/ppermute | solution.py:388
  251.3 1.7 collective-permute-start.24
  (17 other events, 303.0 us)
Sparse Core Ops, SparseCore 0:
  13.2 94.5 all-gather.1

commit v4 on v3

--- a/solution.py
+++ b/solution.py
@@ -1,3 +1,4 @@
+import functools
 import math
 
 import jax
@@ -39,7 +40,7 @@
     acc[...] = dot(own[...], rows_of(scalars[0], w))
 
 
-def kv_kernel(scalars, acc, other, w, kv_out, send_out):
+def kv_kernel(scalars, acc, other, w, kv_out, pair_out, send_out):
     width = kv_out.shape[1]
     heads = width // (2 * HD)
     kv_out[...] = (acc[...] + dot(other[...], rows_of(1 - scalars[0], w))).astype(BF16)
@@ -51,7 +52,9 @@
         source = jnp.where(row < 64, 4 * row + off2, 8 * (row - 64) + off3)
         pick = jnp.where(col == source, 1.0, 0.0).astype(BF16)
         cols = slice(2 * i * HD, 2 * (i + 1) * HD)
-        send_out[:, cols] = dot(pick, kv_out[:, cols]).astype(BF16)
+        picked = dot(pick, kv_out[:, cols]).astype(BF16)
+        pair_out[:, cols] = picked[:64]
+        send_out[:, cols] = picked[64:]
 
 
 def with_ones(values):
@@ -116,7 +119,7 @@
     stat_out[128:] = stats[1]
 
 
-def remote_kernel(scalars, query, acc, stat, near, mid, far, out):
+def remote_kernel(scalars, query, acc, stat, pair, near, mid, far, out):
     heads = out.shape[1] // HD
     scaling = 1.0 / math.sqrt(HD)
     chip = scalars[1]
@@ -133,7 +136,9 @@
         off2 = offset_of(scalars, 2, i, heads)
         off3 = offset_of(scalars, 3, i, heads)
         allowed = (row2 == off2) | (row3 == off3)
-        key_rows = jnp.concatenate([near[:, keys], mid[:, keys], far[:, keys]], axis=0)
+        key_rows = jnp.concatenate(
+            [pair[:, keys], near[:, keys], mid[:, keys], far[:, keys]], axis=0
+        )
         raw = dot_t(query[:, i * HD : (i + 1) * HD], key_rows) * scaling
         scores.append(jnp.where(allowed, raw, NEG_FILL))
     for i in range(heads):
@@ -142,7 +147,9 @@
         expos.append(jnp.exp(scores[i] - peaks[i]))
     for i in range(heads):
         vals = slice((2 * i + 1) * HD, (2 * i + 2) * HD)
-        value_rows = jnp.concatenate([near[:, vals], mid[:, vals], far[:, vals]], axis=0)
+        value_rows = jnp.concatenate(
+            [pair[:, vals], near[:, vals], mid[:, vals], far[:, vals]], axis=0
+        )
         mixed.append(dot(expos[i].astype(BF16), with_ones(value_rows)))
     for i in range(heads):
         shrink = jnp.exp(stat[:, i : i + 1] - peaks[i])
@@ -154,8 +161,17 @@
     acc[...] = x_own[...].astype(F32) + dot(att_own[...], rows_of(scalars[0], w))
 
 
-def back_kernel(scalars, acc, att_other, w, out):
+def back_kernel(tick, scalars, acc, att_other, w, earlier, out, result):
     out[...] = (acc[...] + dot(att_other[...], rows_of(1 - scalars[0], w))).astype(BF16)
+    mine = scalars[scalars.shape[0] - 1] == tick
+
+    @pl.when(mine)
+    def _():
+        result[...] = out[...]
+
+    @pl.when(jnp.logical_not(mine))
+    def _():
+        result[...] = earlier[...]
 
 
 def pack_kernel(core_ref, w_qkv_hbm, w_out_hbm, own, other, w_qkv, w_out, sems):
@@ -312,7 +328,8 @@
         kv_kernel,
         [
             jax.ShapeDtypeStruct((rows, width), BF16),
-            jax.ShapeDtypeStruct((96, width), BF16),
+            jax.ShapeDtypeStruct((64, width), BF16),
+            jax.ShapeDtypeStruct((32, width), BF16),
         ],
         2 * rows * other.shape[1] * width,
         scalars,
@@ -341,7 +358,7 @@
     )
 
 
-def attend_remote(scalars, query, acc, stats, near, mid, far):
+def attend_remote(scalars, query, acc, stats, *sent):
     rows, width = query.shape
     return call(
         remote_kernel,
@@ -351,9 +368,7 @@
         query,
         acc,
         stats,
-        near,
-        mid,
-        far,
+        *sent,
     )
 
 
@@ -370,16 +385,17 @@
     )
 
 
-def project_back(scalars, acc, att_other, w):
+def project_back(scalars, tick, acc, att_other, w, earlier):
     rows, size = acc.shape
     return call(
-        back_kernel,
-        jax.ShapeDtypeStruct((rows, size), BF16),
+        functools.partial(back_kernel, tick),
+        [jax.ShapeDtypeStruct((rows, size), BF16)] * 2,
         2 * rows * size * att_other.shape[1],
         scalars,
         acc,
         att_other,
         w,
+        earlier,
     )
 
 
@@ -394,6 +410,12 @@
     for source in range(count):
         if (source // 2) % GROUP_CHIPS + steps < GROUP_CHIPS:
             pairs.append((source, source + 2 * steps))
+    return lax.ppermute(value, "seq", pairs)
+
+
+def to_partner_chip(value):
+    count = lax.axis_size("seq")
+    pairs = [(source, source + 2) for source in range(count) if (source // 2) % 2 == 0]
     return lax.ppermute(value, "seq", pairs)
 
 
@@ -420,6 +442,7 @@
         [
             jnp.stack([core, (seq // 2) % GROUP_CHIPS]).astype(jnp.int32),
             offsets.reshape(-1).astype(jnp.int32),
+            jnp.full((1,), section, jnp.int32),
         ]
     )
     with jax.named_scope("weights"):
@@ -428,7 +451,9 @@
         cut = w_out.shape[2] // 2
         core_array = jnp.full((1,), core, jnp.int32)
         own, other = pack_weights(core_array, w_qkv, w_out)
-        w_all = gather_chips(join_weights(core_array, own, swap(other)))
+        block = join_weights(core_array, own, swap(other))
+        block, tokens = lax.optimization_barrier((block, tokens))
+        w_all = gather_chips(block)
         depth = w_all.shape[0]
         w_kv = unpack(
             unpack_kv_kernel, w_all, jax.ShapeDtypeStruct((depth, 2 * width), BF16), [8]
@@ -447,18 +472,18 @@
         left, right = both[:, :cut], both[:, cut:]
         x_own = jnp.where(core == 0, left, right)
         x_other = jnp.where(core == 0, right, left)
-    result = jnp.zeros_like(x_own)
+    result = x_own
     for tick in range(section_count):
         acc = project_early(scalars, x_own, w_kv)
-        kv, send = project_kv(scalars, acc, x_other, w_kv)
+        kv, send_pair, send = project_kv(scalars, acc, x_other, w_kv)
         near = to_later_chip(send, 1)
-        mid = to_later_chip(send[64:], 2)
-        far = to_later_chip(send[64:], 3)
+        mid = to_later_chip(send, 2)
+        far = to_later_chip(send, 3)
+        pair = to_partner_chip(send_pair)
         query, acc, stats = attend_local(scalars, x_own, x_other, w_q, kv)
-        att = attend_remote(scalars, query, acc, stats, near, mid, far)
+        att = attend_remote(scalars, query, acc, stats, pair, near, mid, far)
         acc = project_back_early(scalars, x_own, att, w_back)
-        produced = project_back(scalars, acc, swap(att), w_back)
-        result = jnp.where(section == tick, produced, result)
+        produced, result = project_back(scalars, tick, acc, swap(att), w_back, result)
         if tick + 1 < section_count:
             x_own = lax.ppermute(produced, "section", [(tick, tick + 1)])
             x_other = swap(x_own)

time: 261 us -> 259 us (level)
    ppermute x12, starting transfers between devices: 32.7 us -> 18.5 us  [to_later_chip(): return lax.ppermute(value, 'seq', pairs)]
    ppermute x0 -> x4, starting transfers between devices: none -> 12.8 us  [to_partner_chip(): return lax.ppermute(value, 'seq', pairs)]
  transfers between devices with their start and end apart: 26 -> 30, of which waited for: 8 -> 11; matrix products, arithmetic and copies ran while one was open for 0% -> 0% of each run, Pallas kernels for 9% -> 9%
where the time goes in v4:
time: 259 us; the launch traced here: 258 us
  waiting for transfers between devices  147 us (57%)
  Pallas kernels  52.8 us (20%)
  starting transfers between devices  42.4 us (16%)
  between operations  13.9 us (5%)
    all_gather x1, waiting for transfers between devices, gather_chips(): lax.all_gather(block, 'seq', axis=0, tiled=True, axis_index_groups=groups)  92.1 us
    ppermute x3, waiting for transfers between devices, local(): x_own = lax.ppermute(produced, 'section', [(tick, tick + 1)])  49.2 us
    pallas_call x25, Pallas kernels, call(): pl.pallas_call(body, in_specs=in_specs, out_specs=out_specs, out_shape=ou...  44.3 us
    ppermute x12, starting transfers between devices, to_later_chip(): return lax.ppermute(value, 'seq', pairs)  18.5 us
    ppermute x4, starting transfers between devices, to_partner_chip(): return lax.ppermute(value, 'seq', pairs)  12.8 us
    ppermute x10, starting transfers between devices, swap(): return lax.ppermute(value, 'seq', [(i, i ^ 1) for i in range(count)])  8.47 us
    pallas_call x2, Pallas kernels, unpack(): pl.pallas_call(body, in_specs=[pl.BlockSpec(memory_space=pl.ANY)], out_sp...  6.33 us
  transfers between devices with their start and end apart: 30, of which 11 were waited for; matrix products, arithmetic and copies ran while one was open for 0% of the time, Pallas kernels for 9%

profile of v4, /device:TPU:25, one launch (start us, length us, event | category | flops | bytes accessed | tf_op | source)
XLA Modules:
  0.0 258.4 jit_solution(8656615669694316622)
XLA Ops:
  6.5 2.1 weights.4
  15.6 92.1 %all-gather.2.cloned.1.call-done.w = bf16[2560,2560]{1,0:T(8,128)(2,1)} async-done(((bf16[160,2560]{1,0:T(8,128)(2,1)}), bf16[2560,2560]{1,0:T(8,128)(2,1)}) %all-gather.2.cloned.1.call-update) | async-done | bytes 13107216 | tf_op jit(solution)/shard_map/weights/all_gather | solution.py:433
  107.7 2.9 %weights.7.w = bf16[2560,1280]{1,0:T(8,128)(2,1)S(1)} custom-call(bf16[2560,2560]{1,0:T(8,128)(2,1)} %all-gather.2.cloned.1.call-done.w), custom_call_target="tpu_custom_call" | custom-call | tf_op jit(solution)/shard_map/weights/pallas_call | solution.py:267
  112.2 1.8 shard_map.47
  114.0 2.9 %collective-permute-start.2 = (bf16[64,1280]{1,0:T(8,128)(2,1)S(1)}, bf16[64,1280]{1,0:T(8,128)(2,1)S(1)}, u32[]{:S(2)}, u32[]{:S(2)}) collective-permute-start(bf16[64,1280]{1,0:T(8,128)(2,1)S(1)} %get-tuple-element.51), channel_id=1, source_target_pairs={{0,2},{1,3},{4,6},{5,7},{8,10},{9,11},{12,14},{13,15},{16,18},{17,... | collective-permute-start | bytes 491528 | tf_op jit(solution)/shard_map/ppermute | solution.py:419
  117.0 2.7 %collective-permute-start.5 = (bf16[32,1280]{1,0:T(8,128)(2,1)S(1)}, bf16[32,1280]{1,0:T(8,128)(2,1)S(1)}, u32[]{:S(2)}, u32[]{:S(2)}) collective-permute-start(bf16[32,1280]{1,0:T(8,128)(2,1)S(1)} %get-tuple-element.52), channel_id=1, source_target_pairs={{0,6},{1,7},{8,14},{9,15},{16,22},{17,23},{24,30},{25,31},{32,38},... | collective-permute-start | bytes 245768 | tf_op jit(solution)/shard_map/ppermute | solution.py:413
  119.6 2.5 collective-permute-start.4
  123.4 3.4 %weights.6 = (bf16[2560,640]{1,0:T(8,128)(2,1)S(1)}, bf16[1280,1280]{1,0:T(8,128)(2,1)S(1)}) custom-call(bf16[2560,2560]{1,0:T(8,128)(2,1)} %all-gather.2.cloned.1.call-done.w), custom_call_target="tpu_custom_call" | custom-call | tf_op jit(solution)/shard_map/weights/pallas_call | solution.py:267
  126.8 2.5 shard_map.48
  129.4 2.2 shard_map.49.att_own
  138.4 1.8 shard_map.53
  140.2 1.6 collective-permute-start.9
  145.9 2.5 shard_map.54
  148.5 2.2 shard_map.55.att_own
  157.5 1.8 shard_map.59
  159.3 4.1 %collective-permute-start.16 = (bf16[64,1280]{1,0:T(8,128)(2,1)S(1)}, bf16[64,1280]{1,0:T(8,128)(2,1)S(1)}, u32[]{:S(2)}, u32[]{:S(2)}) collective-permute-start(bf16[64,1280]{1,0:T(8,128)(2,1)S(1)} %get-tuple-element.67), channel_id=1, source_target_pairs={{0,2},{1,3},{4,6},{5,7},{8,10},{9,11},{12,14},{13,15},{16,18},{17,... | collective-permute-start | bytes 491528 | tf_op jit(solution)/shard_map/ppermute | solution.py:419
  167.3 2.5 shard_map.60
  170.1 2.2 shard_map.61.att_own
  177.5 49.2 %collective-permute-done.21.own.x_own = bf16[256,1280]{1,0:T(8,128)(2,1)S(1)} collective-permute-done((bf16[256,1280]{1,0:T(8,128)(2,1)S(1)}, bf16[256,1280]{1,0:T(8,128)(2,1)S(1)}, u32[]{:S(2)}, u32[]{:S(2)}) %collective-permute-start.21) | collective-permute-done | bytes 655392 | tf_op jit(solution)/shard_map/ppermute | solution.py:488
  229.3 1.8 shard_map.65
  231.1 4.1 %collective-permute-start.23 = (bf16[64,1280]{1,0:T(8,128)(2,1)S(1)}, bf16[64,1280]{1,0:T(8,128)(2,1)S(1)}, u32[]{:S(2)}, u32[]{:S(2)}) collective-permute-start(bf16[64,1280]{1,0:T(8,128)(2,1)S(1)} %get-tuple-element.75), channel_id=1, source_target_pairs={{0,2},{1,3},{4,6},{5,7},{8,10},{9,11},{12,14},{13,15},{16,18},{17,... | collective-permute-start | bytes 491528 | tf_op jit(solution)/shard_map/ppermute | solution.py:419
  239.4 2.5 shard_map.66
  242.1 2.2 shard_map.67.att_own
  246.7 2.1 shard_map.69
  (77 shorter events, 48.5 us)
Async XLA Ops:
  6.5 101.2 %all-gather.2.cloned.1.call-start = ((), (), s32[]{:S(2)}) async-start(), calls=%async_computation | async-start | bytes 13926400 | tf_op jit(solution)/shard_map/weights/all_gather | solution.py:433
  8.7 2.3 collective-permute-start
  114.0 15.3 %collective-permute-start.2 = (bf16[64,1280]{1,0:T(8,128)(2,1)S(1)}, bf16[64,1280]{1,0:T(8,128)(2,1)S(1)}, u32[]{:S(2)}, u32[]{:S(2)}) collective-permute-start(bf16[64,1280]{1,0:T(8,128)(2,1)S(1)} %get-tuple-element.51), channel_id=1, source_target_pairs={{0,2},{1,3},{4,6},{5,7},{8,10},{9,11},{12,14},{13,15},{16,18},{17,... | collective-permute-start | bytes 491528 | tf_op jit(solution)/shard_map/ppermute | solution.py:419
  117.0 12.4 %collective-permute-start.5 = (bf16[32,1280]{1,0:T(8,128)(2,1)S(1)}, bf16[32,1280]{1,0:T(8,128)(2,1)S(1)}, u32[]{:S(2)}, u32[]{:S(2)}) collective-permute-start(bf16[32,1280]{1,0:T(8,128)(2,1)S(1)} %get-tuple-element.52), channel_id=1, source_target_pairs={{0,6},{1,7},{8,14},{9,15},{16,22},{17,23},{24,30},{25,31},{32,38},... | collective-permute-start | bytes 245768 | tf_op jit(solution)/shard_map/ppermute | solution.py:413
  119.6 9.7 %collective-permute-start.4 = (bf16[32,1280]{1,0:T(8,128)(2,1)S(1)}, bf16[32,1280]{1,0:T(8,128)(2,1)S(1)}, u32[]{:S(2)}, u32[]{:S(2)}) collective-permute-start(bf16[32,1280]{1,0:T(8,128)(2,1)S(1)} %get-tuple-element.52), channel_id=1, source_target_pairs={{0,4},{1,5},{2,6},{3,7},{8,12},{9,13},{10,14},{11,15},{16,20},{17,... | collective-permute-start | bytes 245768 | tf_op jit(solution)/shard_map/ppermute | solution.py:413
  122.1 7.2 %collective-permute-start.3 = (bf16[32,1280]{1,0:T(8,128)(2,1)S(1)}, bf16[32,1280]{1,0:T(8,128)(2,1)S(1)}, u32[]{:S(2)}, u32[]{:S(2)}) collective-permute-start(bf16[32,1280]{1,0:T(8,128)(2,1)S(1)} %get-tuple-element.52), channel_id=1, source_target_pairs={{0,2},{1,3},{2,4},{3,5},{4,6},{5,7},{8,10},{9,11},{10,12},{11,13},... | collective-permute-start | bytes 245768 | tf_op jit(solution)/shard_map/ppermute | solution.py:413
  131.6 2.6 collective-permute-start.6
  140.2 8.3 %collective-permute-start.9 = (bf16[64,1280]{1,0:T(8,128)(2,1)S(1)}, bf16[64,1280]{1,0:T(8,128)(2,1)S(1)}, u32[]{:S(2)}, u32[]{:S(2)}) collective-permute-start(bf16[64,1280]{1,0:T(8,128)(2,1)S(1)} %get-tuple-element.59), channel_id=1, source_target_pairs={{0,2},{1,3},{4,6},{5,7},{8,10},{9,11},{12,14},{13,15},{16,18},{17,... | collective-permute-start | bytes 491528 | tf_op jit(solution)/shard_map/ppermute | solution.py:419
  141.8 6.6 %collective-permute-start.12 = (bf16[32,1280]{1,0:T(8,128)(2,1)S(1)}, bf16[32,1280]{1,0:T(8,128)(2,1)S(1)}, u32[]{:S(2)}, u32[]{:S(2)}) collective-permute-start(bf16[32,1280]{1,0:T(8,128)(2,1)S(1)} %get-tuple-element.60), channel_id=1, source_target_pairs={{0,6},{1,7},{8,14},{9,15},{16,22},{17,23},{24,30},{25,31},{32,38},... | collective-permute-start | bytes 245768 | tf_op jit(solution)/shard_map/ppermute | solution.py:413
  143.1 5.3 %collective-permute-start.11 = (bf16[32,1280]{1,0:T(8,128)(2,1)S(1)}, bf16[32,1280]{1,0:T(8,128)(2,1)S(1)}, u32[]{:S(2)}, u32[]{:S(2)}) collective-permute-start(bf16[32,1280]{1,0:T(8,128)(2,1)S(1)} %get-tuple-element.60), channel_id=1, source_target_pairs={{0,4},{1,5},{2,6},{3,7},{8,12},{9,13},{10,14},{11,15},{16,20},{17,... | collective-permute-start | bytes 245768 | tf_op jit(solution)/shard_map/ppermute | solution.py:413
  144.4 4.1 %collective-permute-start.10 = (bf16[32,1280]{1,0:T(8,128)(2,1)S(1)}, bf16[32,1280]{1,0:T(8,128)(2,1)S(1)}, u32[]{:S(2)}, u32[]{:S(2)}) collective-permute-start(bf16[32,1280]{1,0:T(8,128)(2,1)S(1)} %get-tuple-element.60), channel_id=1, source_target_pairs={{0,2},{1,3},{2,4},{3,5},{4,6},{5,7},{8,10},{9,11},{10,12},{11,13},... | collective-permute-start | bytes 245768 | tf_op jit(solution)/shard_map/ppermute | solution.py:413
  150.8 2.5 collective-permute-start.13
  159.3 10.8 %collective-permute-start.16 = (bf16[64,1280]{1,0:T(8,128)(2,1)S(1)}, bf16[64,1280]{1,0:T(8,128)(2,1)S(1)}, u32[]{:S(2)}, u32[]{:S(2)}) collective-permute-start(bf16[64,1280]{1,0:T(8,128)(2,1)S(1)} %get-tuple-element.67), channel_id=1, source_target_pairs={{0,2},{1,3},{4,6},{5,7},{8,10},{9,11},{12,14},{13,15},{16,18},{17,... | collective-permute-start | bytes 491528 | tf_op jit(solution)/shard_map/ppermute | solution.py:419
  163.4 6.4 %collective-permute-start.19 = (bf16[32,1280]{1,0:T(8,128)(2,1)S(1)}, bf16[32,1280]{1,0:T(8,128)(2,1)S(1)}, u32[]{:S(2)}, u32[]{:S(2)}) collective-permute-start(bf16[32,1280]{1,0:T(8,128)(2,1)S(1)} %get-tuple-element.68), channel_id=1, source_target_pairs={{0,6},{1,7},{8,14},{9,15},{16,22},{17,23},{24,30},{25,31},{32,38},... | collective-permute-start | bytes 245768 | tf_op jit(solution)/shard_map/ppermute | solution.py:413
  164.7 5.1 %collective-permute-start.18 = (bf16[32,1280]{1,0:T(8,128)(2,1)S(1)}, bf16[32,1280]{1,0:T(8,128)(2,1)S(1)}, u32[]{:S(2)}, u32[]{:S(2)}) collective-permute-start(bf16[32,1280]{1,0:T(8,128)(2,1)S(1)} %get-tuple-element.68), channel_id=1, source_target_pairs={{0,4},{1,5},{2,6},{3,7},{8,12},{9,13},{10,14},{11,15},{16,20},{17,... | collective-permute-start | bytes 245768 | tf_op jit(solution)/shard_map/ppermute | solution.py:413
  166.0 4.1 %collective-permute-start.17 = (bf16[32,1280]{1,0:T(8,128)(2,1)S(1)}, bf16[32,1280]{1,0:T(8,128)(2,1)S(1)}, u32[]{:S(2)}, u32[]{:S(2)}) collective-permute-start(bf16[32,1280]{1,0:T(8,128)(2,1)S(1)} %get-tuple-element.68), channel_id=1, source_target_pairs={{0,2},{1,3},{2,4},{3,5},{4,6},{5,7},{8,10},{9,11},{10,12},{11,13},... | collective-permute-start | bytes 245768 | tf_op jit(solution)/shard_map/ppermute | solution.py:413
  172.4 2.5 collective-permute-start.20
  176.2 50.5 %collective-permute-start.21 = (bf16[256,1280]{1,0:T(8,128)(2,1)S(1)}, bf16[256,1280]{1,0:T(8,128)(2,1)S(1)}, u32[]{:S(2)}, u32[]{:S(2)}) collective-permute-start(bf16[256,1280]{1,0:T(8,128)(2,1)S(1)} %get-tuple-element.70), channel_id=1, source_target_pairs={{64,96},{65,97},{66,98},{67,99},{68,100},{69,101},{70,102},{71,103... | collective-permute-start | bytes 1966088 | tf_op jit(solution)/shard_map/ppermute | solution.py:488
  226.7 2.6 %collective-permute-start.22 = (bf16[256,1280]{1,0:T(8,128)(2,1)S(1)}, bf16[256,1280]{1,0:T(8,128)(2,1)S(1)}, u32[]{:S(2)}, u32[]{:S(2)}) collective-permute-start(bf16[256,1280]{1,0:T(8,128)(2,1)S(1)} %collective-permute-done.21.own.x_own), channel_id=1, source_target_pairs={{0,1},{1,0},{2,3},{3,2},{4,5},{5,4},{6,7},{7,6},{8,9},{9,8},{10,11... | collective-permute-start | bytes 1966088 | tf_op jit(solution)/shard_map/ppermute | solution.py:404
  231.1 11.0 %collective-permute-start.23 = (bf16[64,1280]{1,0:T(8,128)(2,1)S(1)}, bf16[64,1280]{1,0:T(8,128)(2,1)S(1)}, u32[]{:S(2)}, u32[]{:S(2)}) collective-permute-start(bf16[64,1280]{1,0:T(8,128)(2,1)S(1)} %get-tuple-element.75), channel_id=1, source_target_pairs={{0,2},{1,3},{4,6},{5,7},{8,10},{9,11},{12,14},{13,15},{16,18},{17,... | collective-permute-start | bytes 491528 | tf_op jit(solution)/shard_map/ppermute | solution.py:419
  235.2 6.6 %collective-permute-start.26 = (bf16[32,1280]{1,0:T(8,128)(2,1)S(1)}, bf16[32,1280]{1,0:T(8,128)(2,1)S(1)}, u32[]{:S(2)}, u32[]{:S(2)}) collective-permute-start(bf16[32,1280]{1,0:T(8,128)(2,1)S(1)} %get-tuple-element.76), channel_id=1, source_target_pairs={{0,6},{1,7},{8,14},{9,15},{16,22},{17,23},{24,30},{25,31},{32,38},... | collective-permute-start | bytes 245768 | tf_op jit(solution)/shard_map/ppermute | solution.py:413
  236.6 5.3 %collective-permute-start.25 = (bf16[32,1280]{1,0:T(8,128)(2,1)S(1)}, bf16[32,1280]{1,0:T(8,128)(2,1)S(1)}, u32[]{:S(2)}, u32[]{:S(2)}) collective-permute-start(bf16[32,1280]{1,0:T(8,128)(2,1)S(1)} %get-tuple-element.76), channel_id=1, source_target_pairs={{0,4},{1,5},{2,6},{3,7},{8,12},{9,13},{10,14},{11,15},{16,20},{17,... | collective-permute-start | bytes 245768 | tf_op jit(solution)/shard_map/ppermute | solution.py:413
  238.0 4.1 %collective-permute-start.24 = (bf16[32,1280]{1,0:T(8,128)(2,1)S(1)}, bf16[32,1280]{1,0:T(8,128)(2,1)S(1)}, u32[]{:S(2)}, u32[]{:S(2)}) collective-permute-start(bf16[32,1280]{1,0:T(8,128)(2,1)S(1)} %get-tuple-element.76), channel_id=1, source_target_pairs={{0,2},{1,3},{2,4},{3,5},{4,6},{5,7},{8,10},{9,11},{10,12},{11,13},... | collective-permute-start | bytes 245768 | tf_op jit(solution)/shard_map/ppermute | solution.py:413
  244.3 2.4 collective-permute-start.27
  (9 other events, 22.0 us)
Sparse Core Ops, SparseCore 0:
  13.2 94.5 all-gather.1

commit v5 on v4

--- a/solution.py
+++ b/solution.py
@@ -16,7 +16,7 @@
 F32 = jnp.float32
 VMEM_LIMIT = 20 * 1024 * 1024
 UNPACK_LIMIT = 46 * 1024 * 1024
-PACK_LIMIT = 60 * 1024 * 1024
+PACK_LIMIT = 16 * 1024 * 1024
 
 
 def dot(a, b):
@@ -372,6 +372,37 @@
     )
 
 
+def last_kernel(tick, scalars, acc, att_other, w, earlier, mine, theirs, result):
+    core = scalars[0]
+    rows = mine.shape[0]
+    is_mine = scalars[scalars.shape[0] - 1] == tick
+
+    @pl.when(is_mine)
+    def _():
+        part = acc[...] + dot(att_other[...], rows_of(1 - core, w))
+        result[...] = part.astype(BF16)
+
+    @pl.when(jnp.logical_not(is_mine))
+    def _():
+        result[...] = earlier[...]
+
+    mine[...] = result[pl.ds(pl.multiple_of(core * rows, 16), rows), :]
+    theirs[...] = result[pl.ds(pl.multiple_of((1 - core) * rows, 16), rows), :]
+
+
+def project_last(scalars, tick, acc, att_other, w, earlier):
+    rows, size = acc.shape
+    return pl.pallas_call(
+        functools.partial(last_kernel, tick),
+        in_specs=[pl.BlockSpec(memory_space=pltpu.SMEM)]
+        + [pl.BlockSpec(memory_space=pltpu.VMEM)] * 4,
+        out_specs=[pl.BlockSpec(memory_space=pltpu.VMEM)] * 2,
+        out_shape=[jax.ShapeDtypeStruct((rows // 2, size), BF16)] * 2,
+        scratch_shapes=[pltpu.VMEM((rows, size), BF16)],
+        compiler_params=pltpu.CompilerParams(vmem_limit_bytes=VMEM_LIMIT),
+    )(scalars, acc, att_other, w, earlier)
+
+
 def project_back_early(scalars, x_own, att_own, w):
     rows, size = x_own.shape
     return call(
@@ -483,14 +514,15 @@
         query, acc, stats = attend_local(scalars, x_own, x_other, w_q, kv)
         att = attend_remote(scalars, query, acc, stats, pair, near, mid, far)
         acc = project_back_early(scalars, x_own, att, w_back)
-        produced, result = project_back(scalars, tick, acc, swap(att), w_back, result)
+        if tick + 1 < section_count:
+            produced, result = project_back(scalars, tick, acc, swap(att), w_back, result)
+        else:
+            mine, theirs = project_last(scalars, tick, acc, swap(att), w_back, result)
         if tick + 1 < section_count:
             x_own = lax.ppermute(produced, "section", [(tick, tick + 1)])
             x_other = swap(x_own)
     with jax.named_scope("result"):
-        top, bottom = result[:128], result[128:]
-        mine = jnp.where(core == 0, top, bottom)
-        theirs = swap(jnp.where(core == 0, bottom, top))
+        theirs = swap(theirs)
         return in_order(core, mine, theirs, 1)[None, None]
 
 

time: 259 us -> 258 us (level)
    pallas_call x25 -> x24, Pallas kernels: 44.3 us -> 42.2 us  [call(): pl.pallas_call(body, in_specs=in_specs, out_specs=out_specs, out_shape=ou...]
where the time goes in v5:
time: 258 us; the launch traced here: 257 us
  waiting for transfers between devices  147 us (57%)
  Pallas kernels  50.3 us (19%)
  starting transfers between devices  42.4 us (16%)
  between operations  13.9 us (5%)
    all_gather x1, waiting for transfers between devices, gather_chips(): lax.all_gather(block, 'seq', axis=0, tiled=True, axis_index_groups=groups)  92.1 us
    ppermute x3, waiting for transfers between devices, local(): x_own = lax.ppermute(produced, 'section', [(tick, tick + 1)])  49.2 us
    pallas_call x24, Pallas kernels, call(): pl.pallas_call(body, in_specs=in_specs, out_specs=out_specs, out_shape=ou...  42.2 us
    ppermute x12, starting transfers between devices, to_later_chip(): return lax.ppermute(value, 'seq', pairs)  18.5 us
    ppermute x4, starting transfers between devices, to_partner_chip(): return lax.ppermute(value, 'seq', pairs)  12.8 us
    ppermute x10, starting transfers between devices, swap(): return lax.ppermute(value, 'seq', [(i, i ^ 1) for i in range(count)])  8.45 us
    pallas_call x2, Pallas kernels, unpack(): pl.pallas_call(body, in_specs=[pl.BlockSpec(memory_space=pl.ANY)], out_sp...  6.33 us
  transfers between devices with their start and end apart: 30, of which 11 were waited for; matrix products, arithmetic and copies ran while one was open for 0% of the time, Pallas kernels for 9%

profile of v5, /device:TPU:25, one launch (start us, length us, event | category | flops | bytes accessed | tf_op | source)
XLA Modules:
  0.0 256.8 jit_solution(11835019666483457661)
XLA Ops:
  14.8 92.1 %all-gather.2.cloned.1.call-done.w = bf16[2560,2560]{1,0:T(8,128)(2,1)} async-done(((bf16[160,2560]{1,0:T(8,128)(2,1)}), bf16[2560,2560]{1,0:T(8,128)(2,1)}) %all-gather.2.cloned.1.call-update) | async-done | bytes 13107216 | tf_op jit(solution)/shard_map/weights/all_gather | solution.py:464
  106.9 2.9 %weights.7.w = bf16[2560,1280]{1,0:T(8,128)(2,1)S(1)} custom-call(bf16[2560,2560]{1,0:T(8,128)(2,1)} %all-gather.2.cloned.1.call-done.w), custom_call_target="tpu_custom_call" | custom-call | tf_op jit(solution)/shard_map/weights/pallas_call | solution.py:267
  111.4 1.8 shard_map.47
  113.2 2.9 %collective-permute-start.2 = (bf16[64,1280]{1,0:T(8,128)(2,1)S(1)}, bf16[64,1280]{1,0:T(8,128)(2,1)S(1)}, u32[]{:S(2)}, u32[]{:S(2)}) collective-permute-start(bf16[64,1280]{1,0:T(8,128)(2,1)S(1)} %get-tuple-element.52), channel_id=1, source_target_pairs={{0,2},{1,3},{4,6},{5,7},{8,10},{9,11},{12,14},{13,15},{16,18},{17,... | collective-permute-start | bytes 491528 | tf_op jit(solution)/shard_map/ppermute | solution.py:450
  116.2 2.7 %collective-permute-start.5 = (bf16[32,1280]{1,0:T(8,128)(2,1)S(1)}, bf16[32,1280]{1,0:T(8,128)(2,1)S(1)}, u32[]{:S(2)}, u32[]{:S(2)}) collective-permute-start(bf16[32,1280]{1,0:T(8,128)(2,1)S(1)} %get-tuple-element.53), channel_id=1, source_target_pairs={{0,6},{1,7},{8,14},{9,15},{16,22},{17,23},{24,30},{25,31},{32,38},... | collective-permute-start | bytes 245768 | tf_op jit(solution)/shard_map/ppermute | solution.py:444
  118.8 2.5 collective-permute-start.4
  122.6 3.4 %weights.6 = (bf16[2560,640]{1,0:T(8,128)(2,1)S(1)}, bf16[1280,1280]{1,0:T(8,128)(2,1)S(1)}) custom-call(bf16[2560,2560]{1,0:T(8,128)(2,1)} %all-gather.2.cloned.1.call-done.w), custom_call_target="tpu_custom_call" | custom-call | tf_op jit(solution)/shard_map/weights/pallas_call | solution.py:267
  126.0 2.5 shard_map.48
  128.6 2.2 shard_map.49.att_own
  135.9 1.6 shard_map.52.acc
  137.6 1.8 shard_map.53
  139.4 1.6 collective-permute-start.9
  145.1 2.5 shard_map.54
  147.7 2.2 shard_map.55.att_own
  155.0 1.6 shard_map.58.acc
  156.7 1.8 shard_map.59
  158.5 4.1 %collective-permute-start.16 = (bf16[64,1280]{1,0:T(8,128)(2,1)S(1)}, bf16[64,1280]{1,0:T(8,128)(2,1)S(1)}, u32[]{:S(2)}, u32[]{:S(2)}) collective-permute-start(bf16[64,1280]{1,0:T(8,128)(2,1)S(1)} %get-tuple-element.68), channel_id=1, source_target_pairs={{0,2},{1,3},{4,6},{5,7},{8,10},{9,11},{12,14},{13,15},{16,18},{17,... | collective-permute-start | bytes 491528 | tf_op jit(solution)/shard_map/ppermute | solution.py:450
  166.5 2.5 shard_map.60
  169.3 2.2 shard_map.61.att_own
  176.7 49.2 %collective-permute-done.21.own.x_own = bf16[256,1280]{1,0:T(8,128)(2,1)S(1)} collective-permute-done((bf16[256,1280]{1,0:T(8,128)(2,1)S(1)}, bf16[256,1280]{1,0:T(8,128)(2,1)S(1)}, u32[]{:S(2)}, u32[]{:S(2)}) %collective-permute-start.21) | collective-permute-done | bytes 655392 | tf_op jit(solution)/shard_map/ppermute | solution.py:522
  228.5 1.8 shard_map.65
  230.3 4.1 %collective-permute-start.23 = (bf16[64,1280]{1,0:T(8,128)(2,1)S(1)}, bf16[64,1280]{1,0:T(8,128)(2,1)S(1)}, u32[]{:S(2)}, u32[]{:S(2)}) collective-permute-start(bf16[64,1280]{1,0:T(8,128)(2,1)S(1)} %get-tuple-element.76), channel_id=1, source_target_pairs={{0,2},{1,3},{4,6},{5,7},{8,10},{9,11},{12,14},{13,15},{16,18},{17,... | collective-permute-start | bytes 491528 | tf_op jit(solution)/shard_map/ppermute | solution.py:450
  238.6 2.5 shard_map.66
  241.3 2.2 shard_map.67.att_own
  (78 shorter events, 48.0 us)
Async XLA Ops:
  6.5 100.4 %all-gather.2.cloned.1.call-start = ((), (), s32[]{:S(2)}) async-start(), calls=%async_computation | async-start | bytes 13926400 | tf_op jit(solution)/shard_map/weights/all_gather | solution.py:464
  113.2 15.4 %collective-permute-start.2 = (bf16[64,1280]{1,0:T(8,128)(2,1)S(1)}, bf16[64,1280]{1,0:T(8,128)(2,1)S(1)}, u32[]{:S(2)}, u32[]{:S(2)}) collective-permute-start(bf16[64,1280]{1,0:T(8,128)(2,1)S(1)} %get-tuple-element.52), channel_id=1, source_target_pairs={{0,2},{1,3},{4,6},{5,7},{8,10},{9,11},{12,14},{13,15},{16,18},{17,... | collective-permute-start | bytes 491528 | tf_op jit(solution)/shard_map/ppermute | solution.py:450
  116.2 12.4 %collective-permute-start.5 = (bf16[32,1280]{1,0:T(8,128)(2,1)S(1)}, bf16[32,1280]{1,0:T(8,128)(2,1)S(1)}, u32[]{:S(2)}, u32[]{:S(2)}) collective-permute-start(bf16[32,1280]{1,0:T(8,128)(2,1)S(1)} %get-tuple-element.53), channel_id=1, source_target_pairs={{0,6},{1,7},{8,14},{9,15},{16,22},{17,23},{24,30},{25,31},{32,38},... | collective-permute-start | bytes 245768 | tf_op jit(solution)/shard_map/ppermute | solution.py:444
  118.8 9.7 %collective-permute-start.4 = (bf16[32,1280]{1,0:T(8,128)(2,1)S(1)}, bf16[32,1280]{1,0:T(8,128)(2,1)S(1)}, u32[]{:S(2)}, u32[]{:S(2)}) collective-permute-start(bf16[32,1280]{1,0:T(8,128)(2,1)S(1)} %get-tuple-element.53), channel_id=1, source_target_pairs={{0,4},{1,5},{2,6},{3,7},{8,12},{9,13},{10,14},{11,15},{16,20},{17,... | collective-permute-start | bytes 245768 | tf_op jit(solution)/shard_map/ppermute | solution.py:444
  121.3 7.2 %collective-permute-start.3 = (bf16[32,1280]{1,0:T(8,128)(2,1)S(1)}, bf16[32,1280]{1,0:T(8,128)(2,1)S(1)}, u32[]{:S(2)}, u32[]{:S(2)}) collective-permute-start(bf16[32,1280]{1,0:T(8,128)(2,1)S(1)} %get-tuple-element.53), channel_id=1, source_target_pairs={{0,2},{1,3},{2,4},{3,5},{4,6},{5,7},{8,10},{9,11},{10,12},{11,13},... | collective-permute-start | bytes 245768 | tf_op jit(solution)/shard_map/ppermute | solution.py:444
  130.8 2.6 collective-permute-start.6
  135.4 2.2 collective-permute-start.8
  139.4 8.3 %collective-permute-start.9 = (bf16[64,1280]{1,0:T(8,128)(2,1)S(1)}, bf16[64,1280]{1,0:T(8,128)(2,1)S(1)}, u32[]{:S(2)}, u32[]{:S(2)}) collective-permute-start(bf16[64,1280]{1,0:T(8,128)(2,1)S(1)} %get-tuple-element.60), channel_id=1, source_target_pairs={{0,2},{1,3},{4,6},{5,7},{8,10},{9,11},{12,14},{13,15},{16,18},{17,... | collective-permute-start | bytes 491528 | tf_op jit(solution)/shard_map/ppermute | solution.py:450
  141.0 6.6 %collective-permute-start.12 = (bf16[32,1280]{1,0:T(8,128)(2,1)S(1)}, bf16[32,1280]{1,0:T(8,128)(2,1)S(1)}, u32[]{:S(2)}, u32[]{:S(2)}) collective-permute-start(bf16[32,1280]{1,0:T(8,128)(2,1)S(1)} %get-tuple-element.61), channel_id=1, source_target_pairs={{0,6},{1,7},{8,14},{9,15},{16,22},{17,23},{24,30},{25,31},{32,38},... | collective-permute-start | bytes 245768 | tf_op jit(solution)/shard_map/ppermute | solution.py:444
  142.3 5.3 %collective-permute-start.11 = (bf16[32,1280]{1,0:T(8,128)(2,1)S(1)}, bf16[32,1280]{1,0:T(8,128)(2,1)S(1)}, u32[]{:S(2)}, u32[]{:S(2)}) collective-permute-start(bf16[32,1280]{1,0:T(8,128)(2,1)S(1)} %get-tuple-element.61), channel_id=1, source_target_pairs={{0,4},{1,5},{2,6},{3,7},{8,12},{9,13},{10,14},{11,15},{16,20},{17,... | collective-permute-start | bytes 245768 | tf_op jit(solution)/shard_map/ppermute | solution.py:444
  143.6 4.1 %collective-permute-start.10 = (bf16[32,1280]{1,0:T(8,128)(2,1)S(1)}, bf16[32,1280]{1,0:T(8,128)(2,1)S(1)}, u32[]{:S(2)}, u32[]{:S(2)}) collective-permute-start(bf16[32,1280]{1,0:T(8,128)(2,1)S(1)} %get-tuple-element.61), channel_id=1, source_target_pairs={{0,2},{1,3},{2,4},{3,5},{4,6},{5,7},{8,10},{9,11},{10,12},{11,13},... | collective-permute-start | bytes 245768 | tf_op jit(solution)/shard_map/ppermute | solution.py:444
  150.0 2.5 collective-permute-start.13
  158.5 10.8 %collective-permute-start.16 = (bf16[64,1280]{1,0:T(8,128)(2,1)S(1)}, bf16[64,1280]{1,0:T(8,128)(2,1)S(1)}, u32[]{:S(2)}, u32[]{:S(2)}) collective-permute-start(bf16[64,1280]{1,0:T(8,128)(2,1)S(1)} %get-tuple-element.68), channel_id=1, source_target_pairs={{0,2},{1,3},{4,6},{5,7},{8,10},{9,11},{12,14},{13,15},{16,18},{17,... | collective-permute-start | bytes 491528 | tf_op jit(solution)/shard_map/ppermute | solution.py:450
  162.6 6.4 %collective-permute-start.19 = (bf16[32,1280]{1,0:T(8,128)(2,1)S(1)}, bf16[32,1280]{1,0:T(8,128)(2,1)S(1)}, u32[]{:S(2)}, u32[]{:S(2)}) collective-permute-start(bf16[32,1280]{1,0:T(8,128)(2,1)S(1)} %get-tuple-element.69), channel_id=1, source_target_pairs={{0,6},{1,7},{8,14},{9,15},{16,22},{17,23},{24,30},{25,31},{32,38},... | collective-permute-start | bytes 245768 | tf_op jit(solution)/shard_map/ppermute | solution.py:444
  163.9 5.1 %collective-permute-start.18 = (bf16[32,1280]{1,0:T(8,128)(2,1)S(1)}, bf16[32,1280]{1,0:T(8,128)(2,1)S(1)}, u32[]{:S(2)}, u32[]{:S(2)}) collective-permute-start(bf16[32,1280]{1,0:T(8,128)(2,1)S(1)} %get-tuple-element.69), channel_id=1, source_target_pairs={{0,4},{1,5},{2,6},{3,7},{8,12},{9,13},{10,14},{11,15},{16,20},{17,... | collective-permute-start | bytes 245768 | tf_op jit(solution)/shard_map/ppermute | solution.py:444
  165.2 4.1 %collective-permute-start.17 = (bf16[32,1280]{1,0:T(8,128)(2,1)S(1)}, bf16[32,1280]{1,0:T(8,128)(2,1)S(1)}, u32[]{:S(2)}, u32[]{:S(2)}) collective-permute-start(bf16[32,1280]{1,0:T(8,128)(2,1)S(1)} %get-tuple-element.69), channel_id=1, source_target_pairs={{0,2},{1,3},{2,4},{3,5},{4,6},{5,7},{8,10},{9,11},{10,12},{11,13},... | collective-permute-start | bytes 245768 | tf_op jit(solution)/shard_map/ppermute | solution.py:444
  171.6 2.5 collective-permute-start.20
  175.4 50.5 %collective-permute-start.21 = (bf16[256,1280]{1,0:T(8,128)(2,1)S(1)}, bf16[256,1280]{1,0:T(8,128)(2,1)S(1)}, u32[]{:S(2)}, u32[]{:S(2)}) collective-permute-start(bf16[256,1280]{1,0:T(8,128)(2,1)S(1)} %get-tuple-element.71), channel_id=1, source_target_pairs={{64,96},{65,97},{66,98},{67,99},{68,100},{69,101},{70,102},{71,103... | collective-permute-start | bytes 1966088 | tf_op jit(solution)/shard_map/ppermute | solution.py:522
  225.9 2.6 %collective-permute-start.22 = (bf16[256,1280]{1,0:T(8,128)(2,1)S(1)}, bf16[256,1280]{1,0:T(8,128)(2,1)S(1)}, u32[]{:S(2)}, u32[]{:S(2)}) collective-permute-start(bf16[256,1280]{1,0:T(8,128)(2,1)S(1)} %collective-permute-done.21.own.x_own), channel_id=1, source_target_pairs={{0,1},{1,0},{2,3},{3,2},{4,5},{5,4},{6,7},{7,6},{8,9},{9,8},{10,11... | collective-permute-start | bytes 1966088 | tf_op jit(solution)/shard_map/ppermute | solution.py:435
  230.3 11.0 %collective-permute-start.23 = (bf16[64,1280]{1,0:T(8,128)(2,1)S(1)}, bf16[64,1280]{1,0:T(8,128)(2,1)S(1)}, u32[]{:S(2)}, u32[]{:S(2)}) collective-permute-start(bf16[64,1280]{1,0:T(8,128)(2,1)S(1)} %get-tuple-element.76), channel_id=1, source_target_pairs={{0,2},{1,3},{4,6},{5,7},{8,10},{9,11},{12,14},{13,15},{16,18},{17,... | collective-permute-start | bytes 491528 | tf_op jit(solution)/shard_map/ppermute | solution.py:450
  234.5 6.6 %collective-permute-start.26 = (bf16[32,1280]{1,0:T(8,128)(2,1)S(1)}, bf16[32,1280]{1,0:T(8,128)(2,1)S(1)}, u32[]{:S(2)}, u32[]{:S(2)}) collective-permute-start(bf16[32,1280]{1,0:T(8,128)(2,1)S(1)} %get-tuple-element.77), channel_id=1, source_target_pairs={{0,6},{1,7},{8,14},{9,15},{16,22},{17,23},{24,30},{25,31},{32,38},... | collective-permute-start | bytes 245768 | tf_op jit(solution)/shard_map/ppermute | solution.py:444
  235.8 5.3 %collective-permute-start.25 = (bf16[32,1280]{1,0:T(8,128)(2,1)S(1)}, bf16[32,1280]{1,0:T(8,128)(2,1)S(1)}, u32[]{:S(2)}, u32[]{:S(2)}) collective-permute-start(bf16[32,1280]{1,0:T(8,128)(2,1)S(1)} %get-tuple-element.77), channel_id=1, source_target_pairs={{0,4},{1,5},{2,6},{3,7},{8,12},{9,13},{10,14},{11,15},{16,20},{17,... | collective-permute-start | bytes 245768 | tf_op jit(solution)/shard_map/ppermute | solution.py:444
  237.3 4.1 %collective-permute-start.24 = (bf16[32,1280]{1,0:T(8,128)(2,1)S(1)}, bf16[32,1280]{1,0:T(8,128)(2,1)S(1)}, u32[]{:S(2)}, u32[]{:S(2)}) collective-permute-start(bf16[32,1280]{1,0:T(8,128)(2,1)S(1)} %get-tuple-element.77), channel_id=1, source_target_pairs={{0,2},{1,3},{2,4},{3,5},{4,6},{5,7},{8,10},{9,11},{10,12},{11,13},... | collective-permute-start | bytes 245768 | tf_op jit(solution)/shard_map/ppermute | solution.py:444
  243.6 2.4 collective-permute-start.27
  (10 other events, 18.4 us)
Sparse Core Ops, SparseCore 0:
  12.4 94.5 all-gather.1

commit v6 on v5

--- a/solution.py
+++ b/solution.py
@@ -53,7 +53,7 @@
         pick = jnp.where(col == source, 1.0, 0.0).astype(BF16)
         cols = slice(2 * i * HD, 2 * (i + 1) * HD)
         picked = dot(pick, kv_out[:, cols]).astype(BF16)
-        pair_out[:, cols] = picked[:64]
+        pair_out[:, cols] = picked
         send_out[:, cols] = picked[64:]
 
 
@@ -119,15 +119,16 @@
     stat_out[128:] = stats[1]
 
 
-def remote_kernel(scalars, query, acc, stat, pair, near, mid, far, out):
+def remote_kernel(scalars, query, acc, stat, pair, mid, cross, out):
     heads = out.shape[1] // HD
     scaling = 1.0 / math.sqrt(HD)
     chip = scalars[1]
     shape = (CHIP_ROWS, 160)
     row = lax.broadcasted_iota(jnp.int32, shape, 0)
     col = lax.broadcasted_iota(jnp.int32, shape, 1)
-    second = (col < 64) & ((chip & 1) == 1)
-    third = (col >= 64) & (chip >= 1 + (col - 64) // 32)
+    odd = (chip & 1) == 1
+    second = (col < 64) & odd
+    third = ((col >= 64) & (col < 96) & odd) | ((col >= 96) & (chip >= 2))
     row2 = jnp.where(second, row & 3, -1)
     row3 = jnp.where(third, row & 7, -1)
     scores, peaks, expos, mixed = [], [], [], []
@@ -137,7 +138,7 @@
         off3 = offset_of(scalars, 3, i, heads)
         allowed = (row2 == off2) | (row3 == off3)
         key_rows = jnp.concatenate(
-            [pair[:, keys], near[:, keys], mid[:, keys], far[:, keys]], axis=0
+            [pair[:, keys], mid[:, keys], cross[:, keys]], axis=0
         )
         raw = dot_t(query[:, i * HD : (i + 1) * HD], key_rows) * scaling
         scores.append(jnp.where(allowed, raw, NEG_FILL))
@@ -148,7 +149,7 @@
     for i in range(heads):
         vals = slice((2 * i + 1) * HD, (2 * i + 2) * HD)
         value_rows = jnp.concatenate(
-            [pair[:, vals], near[:, vals], mid[:, vals], far[:, vals]], axis=0
+            [pair[:, vals], mid[:, vals], cross[:, vals]], axis=0
         )
         mixed.append(dot(expos[i].astype(BF16), with_ones(value_rows)))
     for i in range(heads):
@@ -328,7 +329,7 @@
         kv_kernel,
         [
             jax.ShapeDtypeStruct((rows, width), BF16),
-            jax.ShapeDtypeStruct((64, width), BF16),
+            jax.ShapeDtypeStruct((96, width), BF16),
             jax.ShapeDtypeStruct((32, width), BF16),
         ],
         2 * rows * other.shape[1] * width,
@@ -435,18 +436,15 @@
     return lax.ppermute(value, "seq", [(i, i ^ 1) for i in range(count)])
 
 
-def to_later_chip(value, steps):
+def to_chips(value, moves):
     count = lax.axis_size("seq")
-    pairs = []
-    for source in range(count):
-        if (source // 2) % GROUP_CHIPS + steps < GROUP_CHIPS:
-            pairs.append((source, source + 2 * steps))
-    return lax.ppermute(value, "seq", pairs)
-
-
-def to_partner_chip(value):
-    count = lax.axis_size("seq")
-    pairs = [(source, source + 2) for source in range(count) if (source // 2) % 2 == 0]
+    step = 2 * GROUP_CHIPS
+    pairs = [
+        (first + 2 * source + core, first + 2 * target + core)
+        for first in range(0, count, step)
+        for source, target in moves
+        for core in range(2)
+    ]
     return lax.ppermute(value, "seq", pairs)
 
 
@@ -507,12 +505,11 @@
     for tick in range(section_count):
         acc = project_early(scalars, x_own, w_kv)
         kv, send_pair, send = project_kv(scalars, acc, x_other, w_kv)
-        near = to_later_chip(send, 1)
-        mid = to_later_chip(send, 2)
-        far = to_later_chip(send, 3)
-        pair = to_partner_chip(send_pair)
+        cross = to_chips(send, ((0, 3), (1, 2)))
+        mid = to_chips(send, ((0, 2), (1, 3)))
+        pair = to_chips(send_pair, ((0, 1), (2, 3)))
         query, acc, stats = attend_local(scalars, x_own, x_other, w_q, kv)
-        att = attend_remote(scalars, query, acc, stats, pair, near, mid, far)
+        att = attend_remote(scalars, query, acc, stats, pair, mid, cross)
         acc = project_back_early(scalars, x_own, att, w_back)
         if tick + 1 < section_count:
             produced, result = project_back(scalars, tick, acc, swap(att), w_back, result)

time: 258 us -> 256 us (level)
    ppermute x16 -> x12, starting transfers between devices: 31.3 us -> 30.7 us  [to_chips(): return lax.ppermute(value, 'seq', pairs)]
  transfers between devices with their start and end apart: 30 -> 26, of which waited for: 11 -> 9; matrix products, arithmetic and copies ran while one was open for 0% -> 0% of each run, Pallas kernels for 9% -> 9%
where the time goes in v6:
time: 256 us
  waiting for transfers between devices  147 us (57%)
  Pallas kernels  50.4 us (20%)
  starting transfers between devices  41.2 us (16%)
  between operations  13.8 us (5%)
    all_gather x1, waiting for transfers between devices, gather_chips(): lax.all_gather(block, 'seq', axis=0, tiled=True, axis_index_groups=groups)  92.1 us
    ppermute x3, waiting for transfers between devices, local(): x_own = lax.ppermute(produced, 'section', [(tick, tick + 1)])  49.2 us
    pallas_call x24, Pallas kernels, call(): pl.pallas_call(body, in_specs=in_specs, out_specs=out_specs, out_shape=ou...  42.2 us
    ppermute x12, starting transfers between devices, to_chips(): return lax.ppermute(value, 'seq', pairs)  30.7 us
    ppermute x10, starting transfers between devices, swap(): return lax.ppermute(value, 'seq', [(i, i ^ 1) for i in range(count)])  7.78 us
    pallas_call x2, Pallas kernels, unpack(): pl.pallas_call(body, in_specs=[pl.BlockSpec(memory_space=pl.ANY)], out_sp...  6.33 us
  transfers between devices with their start and end apart: 26, of which 9 were waited for; matrix products, arithmetic and copies ran while one was open for 0% of the time, Pallas kernels for 9%

profile of v6, /device:TPU:25, one launch (start us, length us, event | category | flops | bytes accessed | tf_op | source)
XLA Modules:
  0.0 255.5 jit_solution(17735235423092907877)
XLA Ops:
  14.8 92.1 %all-gather.2.cloned.1.call-done.w = bf16[2560,2560]{1,0:T(8,128)(2,1)} async-done(((bf16[160,2560]{1,0:T(8,128)(2,1)}), bf16[2560,2560]{1,0:T(8,128)(2,1)}) %all-gather.2.cloned.1.call-update) | async-done | bytes 13107216 | tf_op jit(solution)/shard_map/weights/all_gather | solution.py:462
  106.9 2.9 %weights.7.w = bf16[2560,1280]{1,0:T(8,128)(2,1)S(1)} custom-call(bf16[2560,2560]{1,0:T(8,128)(2,1)} %all-gather.2.cloned.1.call-done.w), custom_call_target="tpu_custom_call" | custom-call | tf_op jit(solution)/shard_map/weights/pallas_call | solution.py:268
  113.2 2.9 %collective-permute-start.2 = (bf16[96,1280]{1,0:T(8,128)(2,1)S(1)}, bf16[96,1280]{1,0:T(8,128)(2,1)S(1)}, u32[]{:S(2)}, u32[]{:S(2)}) collective-permute-start(bf16[96,1280]{1,0:T(8,128)(2,1)S(1)} %get-tuple-element.52), channel_id=1, source_target_pairs={{0,2},{1,3},{4,6},{5,7},{8,10},{9,11},{12,14},{13,15},{16,18},{17,... | collective-permute-start | bytes 737288 | tf_op jit(solution)/shard_map/ppermute | solution.py:448
  116.2 2.7 %collective-permute-start.4 = (bf16[32,1280]{1,0:T(8,128)(2,1)S(1)}, bf16[32,1280]{1,0:T(8,128)(2,1)S(1)}, u32[]{:S(2)}, u32[]{:S(2)}) collective-permute-start(bf16[32,1280]{1,0:T(8,128)(2,1)S(1)} %get-tuple-element.53), channel_id=1, source_target_pairs={{0,6},{1,7},{2,4},{3,5},{8,14},{9,15},{10,12},{11,13},{16,22},{17,... | collective-permute-start | bytes 245768 | tf_op jit(solution)/shard_map/ppermute | solution.py:448
  118.8 3.1 %collective-permute-start.3 = (bf16[32,1280]{1,0:T(8,128)(2,1)S(1)}, bf16[32,1280]{1,0:T(8,128)(2,1)S(1)}, u32[]{:S(2)}, u32[]{:S(2)}) collective-permute-start(bf16[32,1280]{1,0:T(8,128)(2,1)S(1)} %get-tuple-element.53), channel_id=1, source_target_pairs={{0,4},{1,5},{2,6},{3,7},{8,12},{9,13},{10,14},{11,15},{16,20},{17,... | collective-permute-start | bytes 245768 | tf_op jit(solution)/shard_map/ppermute | solution.py:448
  122.0 3.4 %weights.6 = (bf16[2560,640]{1,0:T(8,128)(2,1)S(1)}, bf16[1280,1280]{1,0:T(8,128)(2,1)S(1)}) custom-call(bf16[2560,2560]{1,0:T(8,128)(2,1)} %all-gather.2.cloned.1.call-done.w), custom_call_target="tpu_custom_call" | custom-call | tf_op jit(solution)/shard_map/weights/pallas_call | solution.py:268
  125.4 2.5 shard_map.48
  127.9 2.2 shard_map.49.att_own
  136.9 1.8 shard_map.53
  141.6 2.4 collective-permute-start.9
  144.0 2.5 shard_map.54
  147.0 2.2 shard_map.55.att_own
  156.0 1.8 shard_map.59
  157.8 3.2 %collective-permute-start.14 = (bf16[96,1280]{1,0:T(8,128)(2,1)S(1)}, bf16[96,1280]{1,0:T(8,128)(2,1)S(1)}, u32[]{:S(2)}, u32[]{:S(2)}) collective-permute-start(bf16[96,1280]{1,0:T(8,128)(2,1)S(1)} %get-tuple-element.68), channel_id=1, source_target_pairs={{0,2},{1,3},{4,6},{5,7},{8,10},{9,11},{12,14},{13,15},{16,18},{17,... | collective-permute-start | bytes 737288 | tf_op jit(solution)/shard_map/ppermute | solution.py:448
  162.3 3.7 %collective-permute-start.15 = (bf16[32,1280]{1,0:T(8,128)(2,1)S(1)}, bf16[32,1280]{1,0:T(8,128)(2,1)S(1)}, u32[]{:S(2)}, u32[]{:S(2)}) collective-permute-start(bf16[32,1280]{1,0:T(8,128)(2,1)S(1)} %get-tuple-element.69), channel_id=1, source_target_pairs={{0,4},{1,5},{2,6},{3,7},{8,12},{9,13},{10,14},{11,15},{16,20},{17,... | collective-permute-start | bytes 245768 | tf_op jit(solution)/shard_map/ppermute | solution.py:448
  166.0 2.5 shard_map.60
  168.6 2.2 shard_map.61.att_own
  175.4 49.2 %collective-permute-done.18.own.x_own = bf16[256,1280]{1,0:T(8,128)(2,1)S(1)} collective-permute-done((bf16[256,1280]{1,0:T(8,128)(2,1)S(1)}, bf16[256,1280]{1,0:T(8,128)(2,1)S(1)}, u32[]{:S(2)}, u32[]{:S(2)}) %collective-permute-start.18) | collective-permute-done | bytes 655392 | tf_op jit(solution)/shard_map/ppermute | solution.py:519
  227.3 1.8 shard_map.65
  229.1 2.1 collective-permute-start.20
  231.2 3.3 %collective-permute-start.22 = (bf16[32,1280]{1,0:T(8,128)(2,1)S(1)}, bf16[32,1280]{1,0:T(8,128)(2,1)S(1)}, u32[]{:S(2)}, u32[]{:S(2)}) collective-permute-start(bf16[32,1280]{1,0:T(8,128)(2,1)S(1)} %get-tuple-element.77), channel_id=1, source_target_pairs={{0,6},{1,7},{2,4},{3,5},{8,14},{9,15},{10,12},{11,13},{16,22},{17,... | collective-permute-start | bytes 245768 | tf_op jit(solution)/shard_map/ppermute | solution.py:448
  234.5 3.1 %collective-permute-start.21 = (bf16[32,1280]{1,0:T(8,128)(2,1)S(1)}, bf16[32,1280]{1,0:T(8,128)(2,1)S(1)}, u32[]{:S(2)}, u32[]{:S(2)}) collective-permute-start(bf16[32,1280]{1,0:T(8,128)(2,1)S(1)} %get-tuple-element.77), channel_id=1, source_target_pairs={{0,4},{1,5},{2,6},{3,7},{8,12},{9,13},{10,14},{11,15},{16,20},{17,... | collective-permute-start | bytes 245768 | tf_op jit(solution)/shard_map/ppermute | solution.py:448
  237.6 2.5 shard_map.66
  240.2 2.2 shard_map.67.att_own
  (70 shorter events, 43.1 us)
Async XLA Ops:
  6.5 100.4 %all-gather.2.cloned.1.call-start = ((), (), s32[]{:S(2)}) async-start(), calls=%async_computation | async-start | bytes 13926400 | tf_op jit(solution)/shard_map/weights/all_gather | solution.py:462
  9.1 2.1 collective-permute-start
  12.3 2.2 collective-permute-start.1
  113.2 14.6 %collective-permute-start.2 = (bf16[96,1280]{1,0:T(8,128)(2,1)S(1)}, bf16[96,1280]{1,0:T(8,128)(2,1)S(1)}, u32[]{:S(2)}, u32[]{:S(2)}) collective-permute-start(bf16[96,1280]{1,0:T(8,128)(2,1)S(1)} %get-tuple-element.52), channel_id=1, source_target_pairs={{0,2},{1,3},{4,6},{5,7},{8,10},{9,11},{12,14},{13,15},{16,18},{17,... | collective-permute-start | bytes 737288 | tf_op jit(solution)/shard_map/ppermute | solution.py:448
  116.2 11.7 %collective-permute-start.4 = (bf16[32,1280]{1,0:T(8,128)(2,1)S(1)}, bf16[32,1280]{1,0:T(8,128)(2,1)S(1)}, u32[]{:S(2)}, u32[]{:S(2)}) collective-permute-start(bf16[32,1280]{1,0:T(8,128)(2,1)S(1)} %get-tuple-element.53), channel_id=1, source_target_pairs={{0,6},{1,7},{2,4},{3,5},{8,14},{9,15},{10,12},{11,13},{16,22},{17,... | collective-permute-start | bytes 245768 | tf_op jit(solution)/shard_map/ppermute | solution.py:448
  118.8 9.0 %collective-permute-start.3 = (bf16[32,1280]{1,0:T(8,128)(2,1)S(1)}, bf16[32,1280]{1,0:T(8,128)(2,1)S(1)}, u32[]{:S(2)}, u32[]{:S(2)}) collective-permute-start(bf16[32,1280]{1,0:T(8,128)(2,1)S(1)} %get-tuple-element.53), channel_id=1, source_target_pairs={{0,4},{1,5},{2,6},{3,7},{8,12},{9,13},{10,14},{11,15},{16,20},{17,... | collective-permute-start | bytes 245768 | tf_op jit(solution)/shard_map/ppermute | solution.py:448
  130.1 2.6 %collective-permute-start.5 = (bf16[256,640]{1,0:T(8,128)(2,1)S(1)}, bf16[256,640]{1,0:T(8,128)(2,1)S(1)}, u32[]{:S(2)}, u32[]{:S(2)}) collective-permute-start(bf16[256,640]{1,0:T(8,128)(2,1)S(1)} %shard_map.49.att_own), channel_id=1, source_target_pairs={{0,1},{1,0},{2,3},{3,2},{4,5},{5,4},{6,7},{7,6},{8,9},{9,8},{10,11... | collective-permute-start | bytes 983048 | tf_op jit(solution)/shard_map/ppermute | solution.py:436
  134.7 2.2 collective-permute-start.7
  138.7 8.3 %collective-permute-start.8 = (bf16[96,1280]{1,0:T(8,128)(2,1)S(1)}, bf16[96,1280]{1,0:T(8,128)(2,1)S(1)}, u32[]{:S(2)}, u32[]{:S(2)}) collective-permute-start(bf16[96,1280]{1,0:T(8,128)(2,1)S(1)} %get-tuple-element.60), channel_id=1, source_target_pairs={{0,2},{1,3},{4,6},{5,7},{8,10},{9,11},{12,14},{13,15},{16,18},{17,... | collective-permute-start | bytes 737288 | tf_op jit(solution)/shard_map/ppermute | solution.py:448
  140.3 6.2 %collective-permute-start.10 = (bf16[32,1280]{1,0:T(8,128)(2,1)S(1)}, bf16[32,1280]{1,0:T(8,128)(2,1)S(1)}, u32[]{:S(2)}, u32[]{:S(2)}) collective-permute-start(bf16[32,1280]{1,0:T(8,128)(2,1)S(1)} %get-tuple-element.61), channel_id=1, source_target_pairs={{0,6},{1,7},{2,4},{3,5},{8,14},{9,15},{10,12},{11,13},{16,22},{17,... | collective-permute-start | bytes 245768 | tf_op jit(solution)/shard_map/ppermute | solution.py:448
  141.6 5.4 %collective-permute-start.9 = (bf16[32,1280]{1,0:T(8,128)(2,1)S(1)}, bf16[32,1280]{1,0:T(8,128)(2,1)S(1)}, u32[]{:S(2)}, u32[]{:S(2)}) collective-permute-start(bf16[32,1280]{1,0:T(8,128)(2,1)S(1)} %get-tuple-element.61), channel_id=1, source_target_pairs={{0,4},{1,5},{2,6},{3,7},{8,12},{9,13},{10,14},{11,15},{16,20},{17,... | collective-permute-start | bytes 245768 | tf_op jit(solution)/shard_map/ppermute | solution.py:448
  149.3 2.5 collective-permute-start.11
  153.8 2.2 collective-permute-start.13
  157.8 10.8 %collective-permute-start.14 = (bf16[96,1280]{1,0:T(8,128)(2,1)S(1)}, bf16[96,1280]{1,0:T(8,128)(2,1)S(1)}, u32[]{:S(2)}, u32[]{:S(2)}) collective-permute-start(bf16[96,1280]{1,0:T(8,128)(2,1)S(1)} %get-tuple-element.68), channel_id=1, source_target_pairs={{0,2},{1,3},{4,6},{5,7},{8,10},{9,11},{12,14},{13,15},{16,18},{17,... | collective-permute-start | bytes 737288 | tf_op jit(solution)/shard_map/ppermute | solution.py:448
  161.0 7.6 %collective-permute-start.16 = (bf16[32,1280]{1,0:T(8,128)(2,1)S(1)}, bf16[32,1280]{1,0:T(8,128)(2,1)S(1)}, u32[]{:S(2)}, u32[]{:S(2)}) collective-permute-start(bf16[32,1280]{1,0:T(8,128)(2,1)S(1)} %get-tuple-element.69), channel_id=1, source_target_pairs={{0,6},{1,7},{2,4},{3,5},{8,14},{9,15},{10,12},{11,13},{16,22},{17,... | collective-permute-start | bytes 245768 | tf_op jit(solution)/shard_map/ppermute | solution.py:448
  162.3 6.2 %collective-permute-start.15 = (bf16[32,1280]{1,0:T(8,128)(2,1)S(1)}, bf16[32,1280]{1,0:T(8,128)(2,1)S(1)}, u32[]{:S(2)}, u32[]{:S(2)}) collective-permute-start(bf16[32,1280]{1,0:T(8,128)(2,1)S(1)} %get-tuple-element.69), channel_id=1, source_target_pairs={{0,4},{1,5},{2,6},{3,7},{8,12},{9,13},{10,14},{11,15},{16,20},{17,... | collective-permute-start | bytes 245768 | tf_op jit(solution)/shard_map/ppermute | solution.py:448
  170.8 2.0 collective-permute-start.17
  174.1 50.5 %collective-permute-start.18 = (bf16[256,1280]{1,0:T(8,128)(2,1)S(1)}, bf16[256,1280]{1,0:T(8,128)(2,1)S(1)}, u32[]{:S(2)}, u32[]{:S(2)}) collective-permute-start(bf16[256,1280]{1,0:T(8,128)(2,1)S(1)} %get-tuple-element.71), channel_id=1, source_target_pairs={{64,96},{65,97},{66,98},{67,99},{68,100},{69,101},{70,102},{71,103... | collective-permute-start | bytes 1966088 | tf_op jit(solution)/shard_map/ppermute | solution.py:519
  224.6 2.6 %collective-permute-start.19 = (bf16[256,1280]{1,0:T(8,128)(2,1)S(1)}, bf16[256,1280]{1,0:T(8,128)(2,1)S(1)}, u32[]{:S(2)}, u32[]{:S(2)}) collective-permute-start(bf16[256,1280]{1,0:T(8,128)(2,1)S(1)} %collective-permute-done.18.own.x_own), channel_id=1, source_target_pairs={{0,1},{1,0},{2,3},{3,2},{4,5},{5,4},{6,7},{7,6},{8,9},{9,8},{10,11... | collective-permute-start | bytes 1966088 | tf_op jit(solution)/shard_map/ppermute | solution.py:436
  229.1 11.1 %collective-permute-start.20 = (bf16[96,1280]{1,0:T(8,128)(2,1)S(1)}, bf16[96,1280]{1,0:T(8,128)(2,1)S(1)}, u32[]{:S(2)}, u32[]{:S(2)}) collective-permute-start(bf16[96,1280]{1,0:T(8,128)(2,1)S(1)} %get-tuple-element.76), channel_id=1, source_target_pairs={{0,2},{1,3},{4,6},{5,7},{8,10},{9,11},{12,14},{13,15},{16,18},{17,... | collective-permute-start | bytes 737288 | tf_op jit(solution)/shard_map/ppermute | solution.py:448
  231.2 9.0 %collective-permute-start.22 = (bf16[32,1280]{1,0:T(8,128)(2,1)S(1)}, bf16[32,1280]{1,0:T(8,128)(2,1)S(1)}, u32[]{:S(2)}, u32[]{:S(2)}) collective-permute-start(bf16[32,1280]{1,0:T(8,128)(2,1)S(1)} %get-tuple-element.77), channel_id=1, source_target_pairs={{0,6},{1,7},{2,4},{3,5},{8,14},{9,15},{10,12},{11,13},{16,22},{17,... | collective-permute-start | bytes 245768 | tf_op jit(solution)/shard_map/ppermute | solution.py:448
  234.5 5.6 %collective-permute-start.21 = (bf16[32,1280]{1,0:T(8,128)(2,1)S(1)}, bf16[32,1280]{1,0:T(8,128)(2,1)S(1)}, u32[]{:S(2)}, u32[]{:S(2)}) collective-permute-start(bf16[32,1280]{1,0:T(8,128)(2,1)S(1)} %get-tuple-element.77), channel_id=1, source_target_pairs={{0,4},{1,5},{2,6},{3,7},{8,12},{9,13},{10,14},{11,15},{16,20},{17,... | collective-permute-start | bytes 245768 | tf_op jit(solution)/shard_map/ppermute | solution.py:448
  242.4 2.3 collective-permute-start.23
  246.0 1.7 collective-permute-start.24
  (6 other events, 10.2 us)
Sparse Core Ops, SparseCore 0:
  12.4 94.5 all-gather.1

commit v7 on v6

--- a/solution.py
+++ b/solution.py
@@ -123,39 +123,48 @@
     heads = out.shape[1] // HD
     scaling = 1.0 / math.sqrt(HD)
     chip = scalars[1]
-    shape = (CHIP_ROWS, 160)
-    row = lax.broadcasted_iota(jnp.int32, shape, 0)
-    col = lax.broadcasted_iota(jnp.int32, shape, 1)
-    odd = (chip & 1) == 1
-    second = (col < 64) & odd
-    third = ((col >= 64) & (col < 96) & odd) | ((col >= 96) & (chip >= 2))
-    row2 = jnp.where(second, row & 3, -1)
-    row3 = jnp.where(third, row & 7, -1)
-    scores, peaks, expos, mixed = [], [], [], []
-    for i in range(heads):
-        keys = slice(2 * i * HD, (2 * i + 1) * HD)
-        off2 = offset_of(scalars, 2, i, heads)
-        off3 = offset_of(scalars, 3, i, heads)
-        allowed = (row2 == off2) | (row3 == off3)
-        key_rows = jnp.concatenate(
-            [pair[:, keys], mid[:, keys], cross[:, keys]], axis=0
-        )
-        raw = dot_t(query[:, i * HD : (i + 1) * HD], key_rows) * scaling
-        scores.append(jnp.where(allowed, raw, NEG_FILL))
-    for i in range(heads):
-        peaks.append(jnp.maximum(stat[:, i : i + 1], jnp.max(scores[i], axis=1, keepdims=True)))
-    for i in range(heads):
-        expos.append(jnp.exp(scores[i] - peaks[i]))
-    for i in range(heads):
-        vals = slice((2 * i + 1) * HD, (2 * i + 2) * HD)
-        value_rows = jnp.concatenate(
-            [pair[:, vals], mid[:, vals], cross[:, vals]], axis=0
-        )
-        mixed.append(dot(expos[i].astype(BF16), with_ones(value_rows)))
-    for i in range(heads):
-        shrink = jnp.exp(stat[:, i : i + 1] - peaks[i])
-        both = acc[:, 2 * i * HD : 2 * (i + 1) * HD] * shrink + mixed[i]
-        out[:, i * HD : (i + 1) * HD] = (both[:, :HD] / both[:, HD:]).astype(BF16)
+
+    @pl.when(chip == 0)
+    def _():
+        for i in range(heads):
+            both = acc[:, 2 * i * HD : 2 * (i + 1) * HD]
+            out[:, i * HD : (i + 1) * HD] = (both[:, :HD] / both[:, HD:]).astype(BF16)
+
+    @pl.when(chip > 0)
+    def _():
+        shape = (CHIP_ROWS, 160)
+        row = lax.broadcasted_iota(jnp.int32, shape, 0)
+        col = lax.broadcasted_iota(jnp.int32, shape, 1)
+        odd = (chip & 1) == 1
+        second = (col < 64) & odd
+        third = ((col >= 64) & (col < 96) & odd) | ((col >= 96) & (chip >= 2))
+        row2 = jnp.where(second, row & 3, -1)
+        row3 = jnp.where(third, row & 7, -1)
+        scores, peaks, expos, mixed = [], [], [], []
+        for i in range(heads):
+            keys = slice(2 * i * HD, (2 * i + 1) * HD)
+            off2 = offset_of(scalars, 2, i, heads)
+            off3 = offset_of(scalars, 3, i, heads)
+            allowed = (row2 == off2) | (row3 == off3)
+            key_rows = jnp.concatenate(
+                [pair[:, keys], mid[:, keys], cross[:, keys]], axis=0
+            )
+            raw = dot_t(query[:, i * HD : (i + 1) * HD], key_rows) * scaling
+            scores.append(jnp.where(allowed, raw, NEG_FILL))
+        for i in range(heads):
+            peaks.append(jnp.maximum(stat[:, i : i + 1], jnp.max(scores[i], axis=1, keepdims=True)))
+        for i in range(heads):
+            expos.append(jnp.exp(scores[i] - peaks[i]))
+        for i in range(heads):
+            vals = slice((2 * i + 1) * HD, (2 * i + 2) * HD)
+            value_rows = jnp.concatenate(
+                [pair[:, vals], mid[:, vals], cross[:, vals]], axis=0
+            )
+            mixed.append(dot(expos[i].astype(BF16), with_ones(value_rows)))
+        for i in range(heads):
+            shrink = jnp.exp(stat[:, i : i + 1] - peaks[i])
+            both = acc[:, 2 * i * HD : 2 * (i + 1) * HD] * shrink + mixed[i]
+            out[:, i * HD : (i + 1) * HD] = (both[:, :HD] / both[:, HD:]).astype(BF16)
 
 
 def back_early_kernel(scalars, x_own, att_own, w, acc):

time: 256 us -> 256 us (level)
  Pallas kernels: 50.4 us -> 44.2 us
  starting transfers between devices: 41.2 us -> 46.1 us
    pallas_call x24, Pallas kernels: 42.2 us -> 36 us  [call(): pl.pallas_call(body, in_specs=in_specs, out_specs=out_specs, out_shape=ou...]
    ppermute x12, starting transfers between devices: 30.7 us -> 35.6 us  [to_chips(): return lax.ppermute(value, 'seq', pairs)]
where the time goes in v7:
time: 256 us; the launch traced here: 254 us
  waiting for transfers between devices  147 us (57%)
  starting transfers between devices  46.1 us (18%)
  Pallas kernels  44.2 us (17%)
  between operations  13.8 us (5%)
    all_gather x1, waiting for transfers between devices, gather_chips(): lax.all_gather(block, 'seq', axis=0, tiled=True, axis_index_groups=groups)  92.1 us
    ppermute x3, waiting for transfers between devices, local(): x_own = lax.ppermute(produced, 'section', [(tick, tick + 1)])  49.2 us
    pallas_call x24, Pallas kernels, call(): pl.pallas_call(body, in_specs=in_specs, out_specs=out_specs, out_shape=ou...  36 us
    ppermute x12, starting transfers between devices, to_chips(): return lax.ppermute(value, 'seq', pairs)  35.6 us
    ppermute x10, starting transfers between devices, swap(): return lax.ppermute(value, 'seq', [(i, i ^ 1) for i in range(count)])  7.8 us
    pallas_call x2, Pallas kernels, unpack(): pl.pallas_call(body, in_specs=[pl.BlockSpec(memory_space=pl.ANY)], out_sp...  6.33 us
  transfers between devices with their start and end apart: 26, of which 9 were waited for; matrix products, arithmetic and copies ran while one was open for 0% of the time, Pallas kernels for 9%

profile of v7, /device:TPU:25, one launch (start us, length us, event | category | flops | bytes accessed | tf_op | source)
XLA Modules:
  0.0 254.4 jit_solution(5739277208387304283)
XLA Ops:
  14.8 92.1 %all-gather.2.cloned.1.call-done.w = bf16[2560,2560]{1,0:T(8,128)(2,1)} async-done(((bf16[160,2560]{1,0:T(8,128)(2,1)}), bf16[2560,2560]{1,0:T(8,128)(2,1)}) %all-gather.2.cloned.1.call-update) | async-done | bytes 13107216 | tf_op jit(solution)/shard_map/weights/all_gather | solution.py:471
  106.9 2.9 %weights.7.w = bf16[2560,1280]{1,0:T(8,128)(2,1)S(1)} custom-call(bf16[2560,2560]{1,0:T(8,128)(2,1)} %all-gather.2.cloned.1.call-done.w), custom_call_target="tpu_custom_call" | custom-call | tf_op jit(solution)/shard_map/weights/pallas_call | solution.py:277
  109.9 1.6 shard_map.46.acc
  111.4 1.8 shard_map.47
  113.2 2.9 %collective-permute-start.2 = (bf16[96,1280]{1,0:T(8,128)(2,1)S(1)}, bf16[96,1280]{1,0:T(8,128)(2,1)S(1)}, u32[]{:S(2)}, u32[]{:S(2)}) collective-permute-start(bf16[96,1280]{1,0:T(8,128)(2,1)S(1)} %get-tuple-element.52), channel_id=1, source_target_pairs={{0,2},{1,3},{4,6},{5,7},{8,10},{9,11},{12,14},{13,15},{16,18},{17,... | collective-permute-start | bytes 737288 | tf_op jit(solution)/shard_map/ppermute | solution.py:457
  116.2 2.7 %collective-permute-start.4 = (bf16[32,1280]{1,0:T(8,128)(2,1)S(1)}, bf16[32,1280]{1,0:T(8,128)(2,1)S(1)}, u32[]{:S(2)}, u32[]{:S(2)}) collective-permute-start(bf16[32,1280]{1,0:T(8,128)(2,1)S(1)} %get-tuple-element.53), channel_id=1, source_target_pairs={{0,6},{1,7},{2,4},{3,5},{8,14},{9,15},{10,12},{11,13},{16,22},{17,... | collective-permute-start | bytes 245768 | tf_op jit(solution)/shard_map/ppermute | solution.py:457
  118.8 3.1 %collective-permute-start.3 = (bf16[32,1280]{1,0:T(8,128)(2,1)S(1)}, bf16[32,1280]{1,0:T(8,128)(2,1)S(1)}, u32[]{:S(2)}, u32[]{:S(2)}) collective-permute-start(bf16[32,1280]{1,0:T(8,128)(2,1)S(1)} %get-tuple-element.53), channel_id=1, source_target_pairs={{0,4},{1,5},{2,6},{3,7},{8,12},{9,13},{10,14},{11,15},{16,20},{17,... | collective-permute-start | bytes 245768 | tf_op jit(solution)/shard_map/ppermute | solution.py:457
  122.0 3.4 %weights.6 = (bf16[2560,640]{1,0:T(8,128)(2,1)S(1)}, bf16[1280,1280]{1,0:T(8,128)(2,1)S(1)}) custom-call(bf16[2560,2560]{1,0:T(8,128)(2,1)} %all-gather.2.cloned.1.call-done.w), custom_call_target="tpu_custom_call" | custom-call | tf_op jit(solution)/shard_map/weights/pallas_call | solution.py:277
  125.4 2.5 shard_map.48
  133.6 1.6 shard_map.52.acc
  135.3 1.8 shard_map.53
  137.1 3.2 %collective-permute-start.8 = (bf16[96,1280]{1,0:T(8,128)(2,1)S(1)}, bf16[96,1280]{1,0:T(8,128)(2,1)S(1)}, u32[]{:S(2)}, u32[]{:S(2)}) collective-permute-start(bf16[96,1280]{1,0:T(8,128)(2,1)S(1)} %get-tuple-element.60), channel_id=1, source_target_pairs={{0,2},{1,3},{4,6},{5,7},{8,10},{9,11},{12,14},{13,15},{16,18},{17,... | collective-permute-start | bytes 737288 | tf_op jit(solution)/shard_map/ppermute | solution.py:457
  141.6 2.2 collective-permute-start.9
  143.9 2.5 shard_map.54
  154.6 1.8 shard_map.59
  156.4 4.8 %collective-permute-start.14 = (bf16[96,1280]{1,0:T(8,128)(2,1)S(1)}, bf16[96,1280]{1,0:T(8,128)(2,1)S(1)}, u32[]{:S(2)}, u32[]{:S(2)}) collective-permute-start(bf16[96,1280]{1,0:T(8,128)(2,1)S(1)} %get-tuple-element.68), channel_id=1, source_target_pairs={{0,2},{1,3},{4,6},{5,7},{8,10},{9,11},{12,14},{13,15},{16,18},{17,... | collective-permute-start | bytes 737288 | tf_op jit(solution)/shard_map/ppermute | solution.py:457
  162.5 3.7 %collective-permute-start.15 = (bf16[32,1280]{1,0:T(8,128)(2,1)S(1)}, bf16[32,1280]{1,0:T(8,128)(2,1)S(1)}, u32[]{:S(2)}, u32[]{:S(2)}) collective-permute-start(bf16[32,1280]{1,0:T(8,128)(2,1)S(1)} %get-tuple-element.69), channel_id=1, source_target_pairs={{0,4},{1,5},{2,6},{3,7},{8,12},{9,13},{10,14},{11,15},{16,20},{17,... | collective-permute-start | bytes 245768 | tf_op jit(solution)/shard_map/ppermute | solution.py:457
  166.2 2.5 shard_map.60
  174.0 49.2 %collective-permute-done.18.own.x_own = bf16[256,1280]{1,0:T(8,128)(2,1)S(1)} collective-permute-done((bf16[256,1280]{1,0:T(8,128)(2,1)S(1)}, bf16[256,1280]{1,0:T(8,128)(2,1)S(1)}, u32[]{:S(2)}, u32[]{:S(2)}) %collective-permute-start.18) | collective-permute-done | bytes 655392 | tf_op jit(solution)/shard_map/ppermute | solution.py:528
  225.9 1.8 shard_map.65
  227.7 3.7 %collective-permute-start.20 = (bf16[96,1280]{1,0:T(8,128)(2,1)S(1)}, bf16[96,1280]{1,0:T(8,128)(2,1)S(1)}, u32[]{:S(2)}, u32[]{:S(2)}) collective-permute-start(bf16[96,1280]{1,0:T(8,128)(2,1)S(1)} %get-tuple-element.76), channel_id=1, source_target_pairs={{0,2},{1,3},{4,6},{5,7},{8,10},{9,11},{12,14},{13,15},{16,18},{17,... | collective-permute-start | bytes 737288 | tf_op jit(solution)/shard_map/ppermute | solution.py:457
  231.4 3.3 %collective-permute-start.22 = (bf16[32,1280]{1,0:T(8,128)(2,1)S(1)}, bf16[32,1280]{1,0:T(8,128)(2,1)S(1)}, u32[]{:S(2)}, u32[]{:S(2)}) collective-permute-start(bf16[32,1280]{1,0:T(8,128)(2,1)S(1)} %get-tuple-element.77), channel_id=1, source_target_pairs={{0,6},{1,7},{2,4},{3,5},{8,14},{9,15},{10,12},{11,13},{16,22},{17,... | collective-permute-start | bytes 245768 | tf_op jit(solution)/shard_map/ppermute | solution.py:457
  234.7 3.3 %collective-permute-start.21 = (bf16[32,1280]{1,0:T(8,128)(2,1)S(1)}, bf16[32,1280]{1,0:T(8,128)(2,1)S(1)}, u32[]{:S(2)}, u32[]{:S(2)}) collective-permute-start(bf16[32,1280]{1,0:T(8,128)(2,1)S(1)} %get-tuple-element.77), channel_id=1, source_target_pairs={{0,4},{1,5},{2,6},{3,7},{8,12},{9,13},{10,14},{11,15},{16,20},{17,... | collective-permute-start | bytes 245768 | tf_op jit(solution)/shard_map/ppermute | solution.py:457
  238.0 2.5 shard_map.66
  (70 shorter events, 39.6 us)
Async XLA Ops:
  6.5 100.4 %all-gather.2.cloned.1.call-start = ((), (), s32[]{:S(2)}) async-start(), calls=%async_computation | async-start | bytes 13926400 | tf_op jit(solution)/shard_map/weights/all_gather | solution.py:471
  9.1 2.1 collective-permute-start
  12.3 2.2 collective-permute-start.1
  113.2 14.6 %collective-permute-start.2 = (bf16[96,1280]{1,0:T(8,128)(2,1)S(1)}, bf16[96,1280]{1,0:T(8,128)(2,1)S(1)}, u32[]{:S(2)}, u32[]{:S(2)}) collective-permute-start(bf16[96,1280]{1,0:T(8,128)(2,1)S(1)} %get-tuple-element.52), channel_id=1, source_target_pairs={{0,2},{1,3},{4,6},{5,7},{8,10},{9,11},{12,14},{13,15},{16,18},{17,... | collective-permute-start | bytes 737288 | tf_op jit(solution)/shard_map/ppermute | solution.py:457
  116.2 11.7 %collective-permute-start.4 = (bf16[32,1280]{1,0:T(8,128)(2,1)S(1)}, bf16[32,1280]{1,0:T(8,128)(2,1)S(1)}, u32[]{:S(2)}, u32[]{:S(2)}) collective-permute-start(bf16[32,1280]{1,0:T(8,128)(2,1)S(1)} %get-tuple-element.53), channel_id=1, source_target_pairs={{0,6},{1,7},{2,4},{3,5},{8,14},{9,15},{10,12},{11,13},{16,22},{17,... | collective-permute-start | bytes 245768 | tf_op jit(solution)/shard_map/ppermute | solution.py:457
  118.8 9.0 %collective-permute-start.3 = (bf16[32,1280]{1,0:T(8,128)(2,1)S(1)}, bf16[32,1280]{1,0:T(8,128)(2,1)S(1)}, u32[]{:S(2)}, u32[]{:S(2)}) collective-permute-start(bf16[32,1280]{1,0:T(8,128)(2,1)S(1)} %get-tuple-element.53), channel_id=1, source_target_pairs={{0,4},{1,5},{2,6},{3,7},{8,12},{9,13},{10,14},{11,15},{16,20},{17,... | collective-permute-start | bytes 245768 | tf_op jit(solution)/shard_map/ppermute | solution.py:457
  128.5 2.6 %collective-permute-start.5 = (bf16[256,640]{1,0:T(8,128)(2,1)S(1)}, bf16[256,640]{1,0:T(8,128)(2,1)S(1)}, u32[]{:S(2)}, u32[]{:S(2)}) collective-permute-start(bf16[256,640]{1,0:T(8,128)(2,1)S(1)} %shard_map.49.att_own), channel_id=1, source_target_pairs={{0,1},{1,0},{2,3},{3,2},{4,5},{5,4},{6,7},{7,6},{8,9},{9,8},{10,11... | collective-permute-start | bytes 983048 | tf_op jit(solution)/shard_map/ppermute | solution.py:445
  133.1 2.2 collective-permute-start.7
  137.1 9.9 %collective-permute-start.8 = (bf16[96,1280]{1,0:T(8,128)(2,1)S(1)}, bf16[96,1280]{1,0:T(8,128)(2,1)S(1)}, u32[]{:S(2)}, u32[]{:S(2)}) collective-permute-start(bf16[96,1280]{1,0:T(8,128)(2,1)S(1)} %get-tuple-element.60), channel_id=1, source_target_pairs={{0,2},{1,3},{4,6},{5,7},{8,10},{9,11},{12,14},{13,15},{16,18},{17,... | collective-permute-start | bytes 737288 | tf_op jit(solution)/shard_map/ppermute | solution.py:457
  140.3 6.1 %collective-permute-start.10 = (bf16[32,1280]{1,0:T(8,128)(2,1)S(1)}, bf16[32,1280]{1,0:T(8,128)(2,1)S(1)}, u32[]{:S(2)}, u32[]{:S(2)}) collective-permute-start(bf16[32,1280]{1,0:T(8,128)(2,1)S(1)} %get-tuple-element.61), channel_id=1, source_target_pairs={{0,6},{1,7},{2,4},{3,5},{8,14},{9,15},{10,12},{11,13},{16,22},{17,... | collective-permute-start | bytes 245768 | tf_op jit(solution)/shard_map/ppermute | solution.py:457
  141.6 5.4 %collective-permute-start.9 = (bf16[32,1280]{1,0:T(8,128)(2,1)S(1)}, bf16[32,1280]{1,0:T(8,128)(2,1)S(1)}, u32[]{:S(2)}, u32[]{:S(2)}) collective-permute-start(bf16[32,1280]{1,0:T(8,128)(2,1)S(1)} %get-tuple-element.61), channel_id=1, source_target_pairs={{0,4},{1,5},{2,6},{3,7},{8,12},{9,13},{10,14},{11,15},{16,20},{17,... | collective-permute-start | bytes 245768 | tf_op jit(solution)/shard_map/ppermute | solution.py:457
  147.9 2.5 collective-permute-start.11
  152.4 2.2 collective-permute-start.13
  156.4 12.4 %collective-permute-start.14 = (bf16[96,1280]{1,0:T(8,128)(2,1)S(1)}, bf16[96,1280]{1,0:T(8,128)(2,1)S(1)}, u32[]{:S(2)}, u32[]{:S(2)}) collective-permute-start(bf16[96,1280]{1,0:T(8,128)(2,1)S(1)} %get-tuple-element.68), channel_id=1, source_target_pairs={{0,2},{1,3},{4,6},{5,7},{8,10},{9,11},{12,14},{13,15},{16,18},{17,... | collective-permute-start | bytes 737288 | tf_op jit(solution)/shard_map/ppermute | solution.py:457
  161.2 7.6 %collective-permute-start.16 = (bf16[32,1280]{1,0:T(8,128)(2,1)S(1)}, bf16[32,1280]{1,0:T(8,128)(2,1)S(1)}, u32[]{:S(2)}, u32[]{:S(2)}) collective-permute-start(bf16[32,1280]{1,0:T(8,128)(2,1)S(1)} %get-tuple-element.69), channel_id=1, source_target_pairs={{0,6},{1,7},{2,4},{3,5},{8,14},{9,15},{10,12},{11,13},{16,22},{17,... | collective-permute-start | bytes 245768 | tf_op jit(solution)/shard_map/ppermute | solution.py:457
  162.5 6.2 %collective-permute-start.15 = (bf16[32,1280]{1,0:T(8,128)(2,1)S(1)}, bf16[32,1280]{1,0:T(8,128)(2,1)S(1)}, u32[]{:S(2)}, u32[]{:S(2)}) collective-permute-start(bf16[32,1280]{1,0:T(8,128)(2,1)S(1)} %get-tuple-element.69), channel_id=1, source_target_pairs={{0,4},{1,5},{2,6},{3,7},{8,12},{9,13},{10,14},{11,15},{16,20},{17,... | collective-permute-start | bytes 245768 | tf_op jit(solution)/shard_map/ppermute | solution.py:457
  169.4 2.0 collective-permute-start.17
  172.7 50.5 %collective-permute-start.18 = (bf16[256,1280]{1,0:T(8,128)(2,1)S(1)}, bf16[256,1280]{1,0:T(8,128)(2,1)S(1)}, u32[]{:S(2)}, u32[]{:S(2)}) collective-permute-start(bf16[256,1280]{1,0:T(8,128)(2,1)S(1)} %get-tuple-element.71), channel_id=1, source_target_pairs={{64,96},{65,97},{66,98},{67,99},{68,100},{69,101},{70,102},{71,103... | collective-permute-start | bytes 1966088 | tf_op jit(solution)/shard_map/ppermute | solution.py:528
  223.2 2.6 %collective-permute-start.19 = (bf16[256,1280]{1,0:T(8,128)(2,1)S(1)}, bf16[256,1280]{1,0:T(8,128)(2,1)S(1)}, u32[]{:S(2)}, u32[]{:S(2)}) collective-permute-start(bf16[256,1280]{1,0:T(8,128)(2,1)S(1)} %collective-permute-done.18.own.x_own), channel_id=1, source_target_pairs={{0,1},{1,0},{2,3},{3,2},{4,5},{5,4},{6,7},{7,6},{8,9},{9,8},{10,11... | collective-permute-start | bytes 1966088 | tf_op jit(solution)/shard_map/ppermute | solution.py:445
  227.7 12.9 %collective-permute-start.20 = (bf16[96,1280]{1,0:T(8,128)(2,1)S(1)}, bf16[96,1280]{1,0:T(8,128)(2,1)S(1)}, u32[]{:S(2)}, u32[]{:S(2)}) collective-permute-start(bf16[96,1280]{1,0:T(8,128)(2,1)S(1)} %get-tuple-element.76), channel_id=1, source_target_pairs={{0,2},{1,3},{4,6},{5,7},{8,10},{9,11},{12,14},{13,15},{16,18},{17,... | collective-permute-start | bytes 737288 | tf_op jit(solution)/shard_map/ppermute | solution.py:457
  231.4 9.2 %collective-permute-start.22 = (bf16[32,1280]{1,0:T(8,128)(2,1)S(1)}, bf16[32,1280]{1,0:T(8,128)(2,1)S(1)}, u32[]{:S(2)}, u32[]{:S(2)}) collective-permute-start(bf16[32,1280]{1,0:T(8,128)(2,1)S(1)} %get-tuple-element.77), channel_id=1, source_target_pairs={{0,6},{1,7},{2,4},{3,5},{8,14},{9,15},{10,12},{11,13},{16,22},{17,... | collective-permute-start | bytes 245768 | tf_op jit(solution)/shard_map/ppermute | solution.py:457
  234.7 5.9 %collective-permute-start.21 = (bf16[32,1280]{1,0:T(8,128)(2,1)S(1)}, bf16[32,1280]{1,0:T(8,128)(2,1)S(1)}, u32[]{:S(2)}, u32[]{:S(2)}) collective-permute-start(bf16[32,1280]{1,0:T(8,128)(2,1)S(1)} %get-tuple-element.77), channel_id=1, source_target_pairs={{0,4},{1,5},{2,6},{3,7},{8,12},{9,13},{10,14},{11,15},{16,20},{17,... | collective-permute-start | bytes 245768 | tf_op jit(solution)/shard_map/ppermute | solution.py:457
  241.3 2.3 collective-permute-start.23
  244.8 1.7 collective-permute-start.24
  (6 other events, 10.2 us)
Sparse Core Ops, SparseCore 0:
  12.4 94.5 all-gather.1
